TPU v7x, 128 devices: a whole 4x4x4 slice. The times are simulated.
128 devices in a mesh: seq: 16 (over z, x), batch: 8 (over y, core).
Axes of the slice: x: 4, y: 4, z: 4, core: 2. Of those that a mesh axis runs over, the one named last changes fastest.
Arguments:
- tokens: bfloat16 [16, 2048, 576], P('batch', 'seq'), may hold values from -6 to 6
- doc_lengths: int32 [16, 16], P('batch'), may hold values from 0 to 2048, as said below
- second_query: bfloat16 [16, 2048, 576], P('batch', 'seq'), may hold values from -6 to 6
- second_grad: bfloat16 [16, 2048, 576], P('batch', 'seq'), may hold values from -6 to 6
- out_grad: bfloat16 [16, 2048, 576], P('batch', 'seq'), may hold values from -6 to 6
- first_gain: bfloat16 [576], replicated, may hold values from 0.5 to 1.5
- query_weight: bfloat16 [576, 576], replicated, may hold values from -0.25 to 0.25
- key_weight: bfloat16 [576, 192], replicated, may hold values from -0.25 to 0.25
- value_weight: bfloat16 [576, 192], replicated, may hold values from -0.25 to 0.25
- output_weight: bfloat16 [576, 576], replicated, may hold values from -1 to 1
- second_gain: bfloat16 [576], replicated, may hold values from 0.5 to 1.5
- gate_weight: bfloat16 [576, 1536], replicated, may hold values from -0.25 to 0.25
- up_weight: bfloat16 [576, 1536], replicated, may hold values from -0.25 to 0.25
- down_weight: bfloat16 [1536, 576], replicated, may hold values from -0.15625 to 0.15625
Outputs:
- result: bfloat16 [16, 2048, 576], P('batch', 'seq')
- input_grad: bfloat16 [16, 2048, 576], P('batch', 'seq')
- second_query_grad: bfloat16 [16, 2048, 576], P('batch', 'seq')
- first_gain_grad: float32 [576], replicated
- query_weight_grad: float32 [576, 576], replicated
- key_weight_grad: float32 [576, 192], replicated
- value_weight_grad: float32 [576, 192], replicated
- output_weight_grad: float32 [576, 576], replicated
- second_gain_grad: float32 [576], replicated
- gate_weight_grad: float32 [576, 1536], replicated
- up_weight_grad: float32 [576, 1536], replicated
- down_weight_grad: float32 [1536, 576], replicated
Inputs may be any that keep to these rules, and one draw needn't show every extreme that they name: `doc_lengths`: each row sums to 2048. Of the 2 sequences that one index of batch holds, one, chosen by the seed, is a single document of 2048 tokens and the other entries of its row are 0.
All inputs are finite; a program needn't handle non-finite values.
Results may differ from a plain program's by a relative error of at most 0.015.
Values may be sent and summed in bfloat16 or wider, within the bound.
No kernel may reach another device: no remote copies, remote signals or barrier semaphores. Data moves between devices by JAX's collectives and lax.ppermute only.
A program may use at most 128 MiB of HBM per device.

v0:
```python
import functools
import math

import jax
import jax.numpy as jnp
from jax import lax
from jax.experimental import pallas as pl
from jax.experimental.pallas import tpu as pltpu
from jax.sharding import Mesh
from jax.sharding import PartitionSpec as P

HEADS = 9
KVH = 3
HD = 64
HALF = HD // 2
GROUP = HEADS // KVH
NEGATIVE = -1e30
EPSILON = 1e-05
ROPE_BASE = 100000.0
FACTOR = 1.0 / math.sqrt(HD)
LANES = 128
SIDE = 4
KEYS = 256
CHUNK = 384
SEQ = ("z", "x")
SIMPLE = {"kv_weights": 2.0, "input_back": 1.0, "prepare": 1.0, "query": 1.0}
f32 = jnp.float32
bf16 = jnp.bfloat16

VMEM = pl.BlockSpec(memory_space=pltpu.VMEM)
SMEM = pl.BlockSpec(memory_space=pltpu.SMEM)


def cost(microseconds):
    return pl.CostEstimate(flops=int(microseconds * 10**9), bytes_accessed=1000, transcendentals=0)


ANY = pl.BlockSpec(memory_space=pl.ANY)


def params(megabytes=56):
    return pltpu.CompilerParams(vmem_limit_bytes=megabytes * 1024 * 1024)


def shape_of(dims, dtype):
    return jax.ShapeDtypeStruct(dims, dtype)


def mul(left, right):
    return lax.dot_general(left, right, (((1,), (0,)), ((), ())), preferred_element_type=f32)


def mul_nt(left, right):
    return lax.dot_general(left, right, (((1,), (1,)), ((), ())), preferred_element_type=f32)


def flip(array):
    rows, cols = array.shape
    spare = -cols % LANES
    if spare:
        array = jnp.concatenate([array, jnp.zeros((rows, spare), array.dtype)], axis=1)
    extra = -rows % LANES
    if extra:
        array = jnp.concatenate([array, jnp.zeros((extra, cols + spare), array.dtype)], axis=0)
    return jnp.transpose(array)[:cols, :rows]


def side_by_side(ref):
    return jnp.concatenate([ref[m] for m in range(ref.shape[0])], axis=1)


def own_block():
    return lax.axis_index("z") * SIDE + lax.axis_index("x")


def far_block():
    return SIDE * SIDE - 1 - own_block()


def turn(flat, cosine, sine, heads):
    parts = []
    for head in range(heads):
        front = flat[head * HD : head * HD + HALF]
        back = flat[head * HD + HALF : (head + 1) * HD]
        parts += [front * cosine - back * sine, back * cosine + front * sine]
    return parts


def simple(kernel, in_specs, outs, args, name):
    return pl.pallas_call(
        kernel,
        in_specs=in_specs,
        out_specs=[VMEM] * len(outs),
        out_shape=outs,
        compiler_params=params(),
        cost_estimate=cost(SIMPLE[name]),
        name=name,
    )(*args)


def prepare_kernel(lengths, tokens, gain, wk, wv, normed_out, kv_out, cos_out, sin_out, starts, far_starts):
    micro, _, rows = tokens.shape
    lane = lax.broadcasted_iota(jnp.int32, (1, rows), 1)
    places = own_block() * rows + lane
    far_places = far_block() * rows + lane
    positions = []
    for m in range(micro):
        start = jnp.zeros((1, rows), jnp.int32)
        far = jnp.zeros((1, rows), jnp.int32)
        end = jnp.int32(0)
        for j in range(lengths.shape[1]):
            length = lengths[m, j]
            end = end + length
            start = start + jnp.where(places >= end, length, 0)
            far = far + jnp.where(far_places >= end, length, 0)
        starts[m] = start
        far_starts[m] = far
        positions.append(places - start)
    order = lax.broadcasted_iota(jnp.int32, (HALF, micro * rows), 0).astype(f32)
    frequency = jnp.exp(order * (-2.0 * math.log(ROPE_BASE) / HD))
    angles = jnp.concatenate(positions, axis=1).astype(f32) * frequency
    cosine, sine = jnp.cos(angles), jnp.sin(angles)
    cos_out[...] = cosine
    sin_out[...] = sine
    inputs = side_by_side(tokens).astype(f32)
    scale = lax.rsqrt(jnp.mean(inputs * inputs, axis=0, keepdims=True) + EPSILON)
    normed = (inputs * scale * gain[...].astype(f32)).astype(bf16)
    width = tokens.shape[1]
    for m in range(micro):
        span = slice(m * rows, (m + 1) * rows)
        normed_out[m, :width] = normed[:, span]
        base = width
        for table in (cosine, sine):
            high = table[:, span].astype(bf16)
            normed_out[m, base : base + HALF] = high
            normed_out[m, base + HALF : base + 2 * HALF] = (table[:, span] - high.astype(f32)).astype(bf16)
            base += 2 * HALF
    parts = turn(mul(wk[...], normed), cosine, sine, KVH)
    flat = jnp.concatenate(parts + [mul(wv[...], normed)], axis=0).astype(bf16)
    for m in range(micro):
        kv_out[m] = flip(flat[:, m * rows : (m + 1) * rows])


def query_kernel(normed, weight, cos_ref, sin_ref, q1_out):
    width = weight.shape[0]
    flat = mul(flip(weight[...]), jnp.concatenate([normed[m, :width] for m in range(normed.shape[0])], axis=1))
    parts = turn(flat, cos_ref[...], sin_ref[...], HEADS)
    turned = (jnp.concatenate(parts, axis=0).astype(bf16) * FACTOR).astype(bf16)
    rows = q1_out.shape[2]
    for m in range(q1_out.shape[0]):
        q1_out[m] = turned[:, m * rows : (m + 1) * rows]


def lane_heads(ref, group):
    return jnp.concatenate(
        [ref[(group * GROUP + h) * HD : (group * GROUP + h + 1) * HD, :] for h in range(GROUP)], axis=1
    )


def padded(block, place):
    zero = jnp.zeros_like(block)
    return jnp.concatenate([block, zero] if place % 2 == 0 else [zero, block], axis=0)


def visible_bias(start, block, first_key, rows):
    keys = first_key + lax.broadcasted_iota(jnp.int32, (KEYS, rows), 0)
    queries = block * rows + lax.broadcasted_iota(jnp.int32, (KEYS, rows), 1)
    seen = (keys >= start) & (keys <= queries)
    bias = jnp.where(seen, 0.0, NEGATIVE)
    return jnp.concatenate([bias] * GROUP, axis=1)


def key_steps(start, block, rows):
    per = KEYS // rows
    return jnp.min(start) // KEYS, block // per + 1


def forward_kernel(far, held, query_ref, starts, low_out, flat_out, lse_out, acc, peak, mass, query):
    block_place = far_block() if far else own_block()
    scale = FACTOR if far else 1.0
    query[...] = (query_ref[0] * scale).astype(bf16)
    rows = query.shape[1]
    per = KEYS // rows
    acc[...] = jnp.zeros_like(acc)
    peak[...] = jnp.full_like(peak, NEGATIVE)
    mass[...] = jnp.zeros_like(mass)
    start = starts[0]
    first_step, last_step = key_steps(start, block_place, rows)

    @pl.loop(first_step, last_step)
    def _(step):
        block = held[pl.ds(step * per, per), 0].reshape(KEYS, held.shape[3])
        bias = visible_bias(start, block_place, step * KEYS, rows)
        tiles = [block[:, i * LANES : (i + 1) * LANES] for i in range(3)]
        turned = [None, jnp.transpose(tiles[1]), jnp.transpose(tiles[2])]
        for g in range(KVH):
            scores = mul(tiles[g // 2], padded(lane_heads(query, g), g)) + bias
            old = peak[g]
            top = jnp.maximum(old, jnp.max(scores, axis=0, keepdims=True))
            weights = jnp.exp(scores - top)
            decay = jnp.exp(old - top)
            place = KVH + g
            values = turned[place // 2][(place % 2) * HD : (place % 2 + 1) * HD]
            mass[g] = mass[g] * decay + jnp.sum(weights, axis=0, keepdims=True)
            acc[g] = acc[g] * decay + mul(values, weights.astype(bf16))
            peak[g] = top

    for g in range(KVH):
        lse_out[0, g] = peak[g] + jnp.log(mass[g])
        result = acc[g] * (1.0 / mass[g])
        for h in range(GROUP):
            head = g * GROUP + h
            flat_out[0, head * HD : (head + 1) * HD, :] = result[:, h * rows : (h + 1) * rows]
    low_out[...] = flat_out[...].astype(bf16)


def one_of(dims, axis=0):
    block = tuple(1 if i == axis else n for i, n in enumerate(dims))
    return pl.BlockSpec(block, lambda m: tuple(m if i == axis else 0 for i in range(len(dims))))


def attend_forward(far, kv, query, starts):
    micro, width, rows = query.shape
    lanes = GROUP * rows
    low = shape_of(query.shape, bf16)
    flat = shape_of(query.shape, f32)
    lse = shape_of((micro, KVH, 1, lanes), f32)
    return pl.pallas_call(
        functools.partial(forward_kernel, far),
        grid=(micro,),
        in_specs=[one_of(kv.shape, 1), one_of(query.shape), one_of(starts.shape)],
        out_specs=[one_of(v.shape) for v in (low, flat, lse)],
        out_shape=[low, flat, lse],
        scratch_shapes=[
            pltpu.VMEM((KVH, HD, lanes), f32),
            pltpu.VMEM((KVH, 1, lanes), f32),
            pltpu.VMEM((KVH, 1, lanes), f32),
            pltpu.VMEM((width, rows), bf16),
        ],
        compiler_params=params(),
        cost_estimate=cost(2.5),
        name="attention_forward",
    )(kv, query, starts)


def backward_kernel(
    held, q1_ref, q2_ref, d1_ref, d2_ref, o1, o2, lse1, lse2, starts, far_starts, cos_ref, sin_ref,
    kv_out, first_grad, second_grad, sums, delta, dq, query2,
):
    rows = q1_ref.shape[2]
    per = KEYS // rows
    query2[...] = (q2_ref[0] * FACTOR).astype(bf16)
    sums[...] = jnp.zeros_like(sums)
    dq[...] = jnp.zeros_like(dq)

    def attention(a, q_ref, d_ref, o_ref, lse_ref, start, block_place):
        for g in range(KVH):
            product = lane_heads(d_ref, g).astype(f32) * lane_heads(o_ref, g)
            delta[a, g] = jnp.sum(product, axis=0, keepdims=True)
        first_step, last_step = key_steps(start, block_place, rows)

        @pl.loop(first_step, last_step)
        def _(step):
            block = held[pl.ds(step * per, per), 0].reshape(KEYS, held.shape[3])
            bias = visible_bias(start, block_place, step * KEYS, rows)
            tiles = [block[:, i * LANES : (i + 1) * LANES] for i in range(3)]
            turned = [jnp.transpose(tiles[0]), jnp.transpose(tiles[1])]
            total = [None] * 3

            def add(place, value):
                total[place] = value if total[place] is None else total[place] + value

            for g in range(KVH):
                place = KVH + g
                keys = turned[g // 2][(g % 2) * HD : (g % 2 + 1) * HD]
                query = padded(lane_heads(q_ref, g), g)
                grad = padded(lane_heads(d_ref, g), place)
                scores = mul(tiles[g // 2], query) + bias
                weights = jnp.exp(scores - lse_ref[0, g])
                weight_grad = mul(tiles[place // 2], grad)
                score_grad = (weights * (weight_grad - delta[a, g])).astype(bf16)
                dq[a, g] += mul(keys, score_grad)
                add(g // 2, mul_nt(score_grad, query))
                add(place // 2, mul_nt(weights.astype(bf16), grad))
            joined = jnp.concatenate(total, axis=1)
            sums[pl.ds(step * per, per)] += joined.reshape(per, rows, joined.shape[1])

    attention(0, q1_ref.at[0], d1_ref.at[0], o1.at[0], lse1, starts[0], own_block())
    attention(1, query2, d2_ref.at[0], o2.at[0], lse2, far_starts[0], far_block())
    kv_out[:, 0] = sums[...].astype(bf16)
    cosine, sine = cos_ref[...], -sin_ref[...]
    for g in range(KVH):
        for h in range(GROUP):
            head = g * GROUP + h
            lanes = slice(h * rows, (h + 1) * rows)
            target = slice(head * HD, (head + 1) * HD)
            parts = turn(dq[0, g][:, lanes] * FACTOR, cosine, sine, 1)
            first_grad[0, target, :] = jnp.concatenate(parts, axis=0).astype(bf16)
            second_grad[0, target, :] = (dq[1, g][:, lanes] * FACTOR).astype(bf16)


def attend_backward(kv, *arrays):
    micro, width, rows = arrays[0].shape
    lanes = GROUP * rows
    blocks, _, _, kv_width = kv.shape
    part = shape_of((micro, width, rows), bf16)
    table = pl.BlockSpec((HALF, rows), lambda m: (0, m))
    return pl.pallas_call(
        backward_kernel,
        grid=(micro,),
        in_specs=[one_of(kv.shape, 1)] + [one_of(v.shape) for v in arrays[:-2]] + [table] * 2,
        out_specs=[one_of(kv.shape, 1)] + [one_of(part.shape)] * 2,
        out_shape=[shape_of(kv.shape, bf16), part, part],
        scratch_shapes=[
            pltpu.VMEM((blocks, rows, kv_width), f32),
            pltpu.VMEM((2, KVH, 1, lanes), f32),
            pltpu.VMEM((2, KVH, HD, lanes), f32),
            pltpu.VMEM((width, rows), bf16),
        ],
        compiler_params=params(),
        cost_estimate=cost(7),
        name="attention_backward",
    )(kv, *arrays)


def kv_weights_kernel(sums, normed, starts, far_starts, k_out, v_out):
    micro, _, rows = starts.shape
    width = v_out.shape[0]
    cut = KVH * HD
    per = KEYS // rows
    k_out[...] = jnp.zeros_like(k_out)
    v_out[...] = jnp.zeros_like(v_out)
    for m in range(micro):

        def add(step):
            block = sums[pl.ds(step * per, per), m].reshape(KEYS, sums.shape[3])
            inner = [normed[step * per + i, m] for i in range(per)]
            values = jnp.concatenate([v[:width] for v in inner], axis=1)
            tables = jnp.concatenate([v[width:] for v in inner], axis=1).astype(f32)
            cosine = tables[:HALF] + tables[HALF : 2 * HALF]
            sine = tables[2 * HALF : 3 * HALF] + tables[3 * HALF :]
            flat = jnp.concatenate(
                [jnp.transpose(block[:, :LANES]), jnp.transpose(block[:, LANES : 2 * LANES])[: cut - LANES]], axis=0
            )
            keys = jnp.concatenate(turn(flat.astype(f32), cosine, -sine, KVH), axis=0).astype(bf16)
            k_out[...] += mul_nt(keys, values)
            v_out[...] += mul(values, block[:, LANES:])

        near = key_steps(starts[m], own_block(), rows)
        far = key_steps(far_starts[m], far_block(), rows)
        pl.loop(*near)(add)

        @pl.loop(*far)
        def _(step):
            pl.when((step < near[0]) | (step >= near[1]))(lambda: add(step))


def norm_back(vector, scale, gain, gradient):
    weighted = gradient * gain
    gain_grad = jnp.sum(gradient * vector * scale, axis=1, keepdims=True)
    inner = jnp.mean(weighted * vector, axis=0, keepdims=True)
    return scale * weighted - vector * (scale * scale * scale * inner), gain_grad


def ffn_kernel(
    last, core, first, tokens, out_weight, gain, out_grad, wg, wu, wd, *refs,
):
    step = pl.program_id(0)
    micro, width, rows = tokens.shape
    if last:
        before, result_before, grad_before, received = refs[:4]
        result, main0, main1, middle_grad, d1, gain_grad, wo_grad = refs[4:11]
        normed, normed_t, grad, grad_t, result_sum, normed_grad = refs[11:]
        middle = before
    else:
        main, middle, result_sum, normed_grad = refs[:4]
        normed, normed_t, grad, grad_t = refs[4:]

    @pl.when(step == 0)
    def _():
        if last:
            value = before[...]
            result_sum[...] = result_before[...]
            normed_grad[...] = grad_before[...]
        else:
            value = side_by_side(tokens).astype(f32) + mul(flip(out_weight[...]), side_by_side(first))
            middle[...] = value
            result_sum[...] = jnp.zeros_like(result_sum)
            normed_grad[...] = jnp.zeros_like(normed_grad)
        scale = lax.rsqrt(jnp.mean(value * value, axis=0, keepdims=True) + EPSILON)
        low = (value * scale * gain[...].astype(f32)).astype(bf16)
        normed_t[...] = low
        normed[...] = flip(low)
        flat = side_by_side(out_grad)
        grad_t[...] = flat
        grad[...] = flip(flat)

    low = normed[...]
    gate = mul(low, wg[...])
    up = mul(low, wu[...])
    sigmoid = 1.0 / (1.0 + jnp.exp(-gate))
    active = gate * sigmoid
    hidden = (active * up).astype(bf16)
    result_sum[...] += mul_nt(hidden, wd[...])
    hidden_grad = mul(grad[...], wd[...])
    gate_grad = (hidden_grad * up * sigmoid * (1.0 + gate * (1.0 - sigmoid))).astype(bf16)
    up_grad = (hidden_grad * active).astype(bf16)
    parts = (mul(normed_t[...], gate_grad), mul(normed_t[...], up_grad), mul(grad_t[...], hidden))
    for i in range(CHUNK // LANES):
        span = slice(i * LANES, (i + 1) * LANES)
        for k, part in enumerate(parts):
            rows_at = slice((i * 3 + k) * width, (i * 3 + k + 1) * width)
            value = part[:, span].astype(bf16)
            if last:
                value = (value.astype(f32) + received[rows_at].astype(f32)).astype(bf16)
                for index, target in enumerate((main0, main1)):
                    pl.when(step == index)(functools.partial(target.__setitem__, rows_at, value))
            else:
                main[rows_at] = value
    normed_grad[...] += mul_nt(gate_grad, wg[...]) + mul_nt(up_grad, wu[...])
    if not last:
        return

    @pl.when(step == pl.num_programs(0) - 1)
    def _():
        value = middle[...]
        final = (value + flip(result_sum[...])).astype(bf16)
        scale = lax.rsqrt(jnp.mean(value * value, axis=0, keepdims=True) + EPSILON)
        part, gains = norm_back(value, scale, gain[...].astype(f32), flip(normed_grad[...]))
        gain_grad[...] = gains
        total = grad_t[...].astype(f32) + part
        middle_grad[...] = total
        branch = total.astype(bf16)
        wo_grad[...] = mul_nt(side_by_side(first), branch).astype(bf16)
        back = mul(out_weight[...], branch).astype(bf16)
        for m in range(micro):
            span = slice(m * rows, (m + 1) * rows)
            d1[m] = back[:, span]
            result[m] = final[:, span]


def pack_rows(target, base, array):
    rows, cols = array.shape
    for i in range(-(-cols // LANES)):
        span = array[:, i * LANES : (i + 1) * LANES]
        if span.shape[1] < LANES:
            span = jnp.concatenate([span, jnp.zeros((rows, LANES - span.shape[1]), span.dtype)], axis=1)
        target[base : base + rows] = span
        base += rows
    return base


def main_rows(width):
    used = CHUNK // LANES * 3 * width
    unit = SIDE * SIDE * SIDE * 8
    return -(-used // unit) * unit


def feed_forward(core, first, tokens, out_weight, gain, out_grad, wg, wu, wd, before):
    micro, width, rows = tokens.shape
    total = micro * rows
    hidden = wg.shape[1]
    steps = hidden // 2 // CHUNK
    block = pl.BlockSpec((CHUNK // LANES * 3 * width, LANES), lambda i, c: (i, 0))
    first_block = pl.BlockSpec((CHUNK // LANES * 3 * width, LANES), lambda i, c: (0, 0))
    last = len(before) > 0

    def whole(*dims):
        return pl.BlockSpec(dims, lambda i, c: (0,) * len(dims))

    def column(i, c):
        side = c[0] if last else 1 - c[0]
        return (0, side * steps + i)

    weight = pl.BlockSpec((width, CHUNK), column)
    flat, natural = shape_of((width, total), f32), shape_of((total, width), f32)
    spec, tall = whole(width, total), whole(total, width)
    token_spec, token_shape = whole(micro, width, rows), shape_of((micro, width, rows), bf16)
    if last:
        outs = [
            (token_shape, token_spec),
            (shape_of((main_rows(width), LANES), bf16), first_block),
            (shape_of((main_rows(width), LANES), bf16), first_block),
            (flat, spec),
            (token_shape, token_spec),
            (shape_of((width, 1), f32), whole(width, 1)),
            (shape_of((width, width), bf16), whole(width, width)),
        ]
        more = [spec, tall, tall, block]
        scratch = [pltpu.VMEM((total, width), f32)] * 2
    else:
        outs = [
            (shape_of((hidden // 2 // LANES * 3 * width, LANES), bf16), block),
            (flat, spec),
            (natural, tall),
            (natural, tall),
        ]
        more, scratch = [], []
    low = [pltpu.VMEM((total, width), bf16), pltpu.VMEM((width, total), bf16)]
    return pl.pallas_call(
        functools.partial(ffn_kernel, last),
        grid_spec=pltpu.PrefetchScalarGridSpec(
            num_scalar_prefetch=1,
            grid=(steps,),
            in_specs=[
                token_spec,
                token_spec,
                whole(width, width),
                whole(width, 1),
                token_spec,
                weight,
                weight,
                weight,
            ]
            + more,
            out_specs=[v[1] for v in outs],
            scratch_shapes=low * 2 + scratch,
        ),
        out_shape=[v[0] for v in outs],
        compiler_params=params(),
        cost_estimate=cost(3),
        name="feed_forward",
    )(core, first, tokens, out_weight, gain, out_grad, wg, wu, wd, *before)


def query_back_kernel(
    normed, grad_ref, weight, wk_grad, wv_grad, wo_grad, gain_two_grad, normed_grad, kept, away, packed
):
    grad = side_by_side(grad_ref)
    width = weight.shape[0]
    values = jnp.concatenate([normed[m, :width] for m in range(normed.shape[0])], axis=1)
    normed_grad[...] = mul(weight[...], grad)
    lane = lax.broadcasted_iota(jnp.int32, (width, LANES), 1)
    gains = flip(jnp.where(lane == 0, gain_two_grad[...], 0.0))[:16]
    base = 0
    for array in (mul_nt(values, grad), wk_grad[...], wv_grad[...], wo_grad[...], gains):
        base = pack_rows(packed, base, array.astype(bf16))
    packed[base:] = jnp.zeros((packed.shape[0] - base, LANES), bf16)
    unit = kept.shape[1]
    for dy in range(SIDE):
        for target, dc in ((kept, 0), (away, 1)):
            target[dy] = packed[pl.ds(pl.multiple_of(place_of(dc, dy, 1) * unit, 16), unit)]


def tail_rows(width):
    tiles = -(-width // LANES)
    used = tiles * (2 * width + KVH * HD + 16) + (2 * KVH * HD // LANES - 1) * width
    unit = 2 * SIDE * SIDE * SIDE * 8
    return -(-used // unit) * (unit // 2)


def place_of(dc, dy, sign):
    cc = lax.rem(lax.axis_index("core") + dc, 2)
    yy = lax.rem(lax.axis_index("y") + sign * dy + SIDE, SIDE)
    return cc * SIDE + yy


def input_back_kernel(
    kv_grad, wk, wv, cos_ref, sin_ref, partial, tokens, gain, middle_grad, second, input_grad, second_grad
):
    second_grad[...] = second[...]
    micro, width, rows = tokens.shape
    flat = jnp.concatenate(
        [flip(kv_grad[m * rows : (m + 1) * rows].astype(f32)) for m in range(micro)], axis=1
    )
    cut = KVH * HD
    parts = turn(flat[:cut], cos_ref[...], -sin_ref[...], KVH)
    low = jnp.concatenate(parts + [flat[cut:]], axis=0).astype(bf16)
    weights = flip(jnp.concatenate([wk[...], wv[...]], axis=0))
    normed_grad = partial[...] + mul(weights, low)
    inputs = side_by_side(tokens).astype(f32)
    scale = lax.rsqrt(jnp.mean(inputs * inputs, axis=0, keepdims=True) + EPSILON)
    part, _ = norm_back(inputs, scale, gain[...].astype(f32), normed_grad)
    final = (middle_grad[...] + part).astype(bf16)
    for m in range(micro):
        input_grad[m] = final[:, m * rows : (m + 1) * rows]


def unpack_tail_kernel(kept, away, wq, wk, wv, gain, q_out, k_out, v_out, o_out, gain_one, gain_two, held):
    unit = kept.shape[1]
    for dy in range(SIDE):
        for source, dc in ((kept, 0), (away, 1)):
            held[pl.ds(pl.multiple_of(place_of(dc, dy, -1) * unit, 16), unit)] = source[dy]
    width = q_out.shape[0]
    cut = k_out.shape[0]
    base = 0

    def section(rows, cols):
        nonlocal base
        count = -(-cols // LANES)
        parts = [held[base + i * rows : base + (i + 1) * rows] for i in range(count)]
        base += count * rows
        return jnp.concatenate(parts, axis=1)[:, :cols].astype(f32)

    query = section(width, width)
    key = section(cut, width)
    value = flip(section(width, 2 * cut - LANES))[cut - LANES :]
    q_out[...] = query
    k_out[...] = key
    v_out[...] = value
    o_out[...] = section(width, width)
    gain_two[...] = section(16, width)[0]
    total = jnp.sum(query * wq[...].astype(f32), axis=1, keepdims=True) / gain[...].astype(f32)
    total = flip(jnp.broadcast_to(total, (width, LANES)))[0:1]
    rest = jnp.sum(key * wk[...].astype(f32), axis=0, keepdims=True)
    rest = rest + jnp.sum(value * wv[...].astype(f32), axis=0, keepdims=True)
    line = flip(jnp.broadcast_to(gain[...].astype(f32), (width, LANES)))[0:1]
    gain_one[...] = (total + rest / line)[0]


def unpack_main_kernel(other, *refs):
    pieces = refs[:SIDE]
    gate, up, down, held, wide, sems = refs[-6:]
    unit = pieces[0].shape[0]
    part = unit // 2
    for k in range(SIDE):
        place = lax.rem(lax.axis_index("y") - k + SIDE, SIDE)
        for index in range(2):
            span = pl.ds(pl.multiple_of(place * part, 16), part)
            held[index, span] = pieces[k][index * part : (index + 1) * part]
    core = lax.axis_index("core")
    core = 1 - core if other else core
    width, cols = wide.shape[1:]
    copies = []
    for k, target in enumerate((gate, up, down)):
        for t in range(cols // LANES):
            per = CHUNK // LANES
            base = (t % per * 3 + k) * width
            wide[k, :, t * LANES : (t + 1) * LANES] = held[t // per, base : base + width].astype(f32)
        span = pl.ds(pl.multiple_of(core * cols, LANES), cols)
        copies.append(pltpu.make_async_copy(wide.at[k], target.at[:, span], sems.at[k]))
        copies[-1].start()
    for copy in copies:
        copy.wait()


def unpack_main(pieces, width, hidden, filled):
    unit = pieces[0].shape[0]
    outs = [shape_of((width, hidden), f32)] * 3
    return pl.pallas_call(
        functools.partial(unpack_main_kernel, filled is not None),
        in_specs=[VMEM] * SIDE + ([ANY] * 3 if filled else []),
        out_specs=[ANY] * 3,
        out_shape=outs,
        scratch_shapes=[
            pltpu.VMEM((2, SIDE * unit // 2, LANES), bf16),
            pltpu.VMEM((3, width, hidden // 2), f32),
            pltpu.SemaphoreType.DMA((3,)),
        ],
        input_output_aliases={SIDE + i: i for i in range(3)} if filled else {},
        compiler_params=params(),
        cost_estimate=cost(1.5),
        name="unpack_main",
    )(*pieces, *(filled or ()))


def shift(value, axis, distance):
    size = lax.axis_size(axis)
    return lax.ppermute(value, axis, [(i, (i + distance) % size) for i in range(size)])


def mirror(value):
    size = SIDE * SIDE
    return lax.ppermute(value, SEQ, [(i, size - 1 - i) for i in range(size)])


def collect(value, axis):
    return [value] + [shift(value, axis, k) for k in range(1, SIDE)]


def exchange(parts, axis):
    total = parts[0].astype(f32)
    for k in range(1, SIDE):
        total = total + shift(parts[k], axis, k).astype(f32)
    return total


def scatter_parts(held, axis):
    rows, lanes = held.shape
    places = lax.axis_size(axis)
    return lax.all_to_all(held.reshape(places, rows // places, lanes), axis, 0, 0)


def sum_parts(parts):
    return jnp.sum(parts.astype(f32), axis=0).astype(bf16)


def scatter_sum(held, axis):
    return sum_parts(scatter_parts(held, axis))


def gather_all(held, axis):
    rows, lanes = held.shape
    places = lax.axis_size(axis)
    spread = jnp.broadcast_to(held[None], (places,) + held.shape)
    return lax.all_to_all(spread, axis, 0, 0).reshape(places * rows, lanes)


def after(value, *others):
    return lax.optimization_barrier((value, *others))[0]


def per_device(
    tokens,
    doc_lengths,
    second_query,
    second_grad,
    out_grad,
    first_gain,
    query_weight,
    key_weight,
    value_weight,
    output_weight,
    second_gain,
    gate_weight,
    up_weight,
    down_weight,
):
    micro, rows, width = tokens.shape
    kwidth = key_weight.shape[1]
    total = micro * rows
    tiles = -(-width // LANES)
    core = lax.axis_index("core").reshape(1)
    tokens, second_query, second_grad, out_grad = (
        jnp.swapaxes(v, 1, 2) for v in (tokens, second_query, second_grad, out_grad)
    )
    wk, wv, wd = key_weight.T, value_weight.T, down_weight.T
    gain_one, gain_two = first_gain.reshape(width, 1), second_gain.reshape(width, 1)

    table = shape_of((HALF, total), f32)
    start = shape_of((micro, 1, rows), jnp.int32)
    normed, kv, cosine, sine, starts, far_starts = simple(
        prepare_kernel,
        [SMEM] + [VMEM] * 4,
        [
            shape_of((micro, width + 4 * HALF, rows), bf16),
            shape_of((micro, rows, 2 * kwidth), bf16),
            table,
            table,
            start,
            start,
        ],
        (doc_lengths, tokens, gain_one, wk, wv),
        "prepare",
    )
    kv = lax.all_gather(kv, SEQ, axis=0)
    (q1,) = simple(
        query_kernel,
        [VMEM] * 4,
        [shape_of((micro, width, rows), bf16)],
        (normed, query_weight, cosine, sine),
        "query",
    )
    kv, q1, second_query, second_grad, gathered = lax.optimization_barrier(
        (kv, q1, second_query, second_grad, normed)
    )
    gathered = lax.all_gather(gathered, SEQ, axis=0)
    far_query, far_grad = mirror(second_query), mirror(second_grad)
    first_low, first_flat, first_lse = attend_forward(False, kv, q1, starts)
    first_low, far_query = lax.optimization_barrier((first_low, far_query))
    ffn_args = (first_low, tokens, output_weight, gain_two, out_grad, gate_weight, up_weight, wd)
    away, *before = feed_forward(core, *ffn_args, ())
    far_query = after(far_query, away)
    _, second_flat, second_lse = attend_forward(True, kv, far_query, far_starts)
    received, second_lse = lax.optimization_barrier((shift(away, "core", 1), second_lse))
    result, main0, main1, middle_grad, d1, gain_two_grad, wo_grad = feed_forward(core, *ffn_args, (*before, received))
    main0 = scatter_parts(main0, "y")
    kv_grad, query_grad, second_query_grad = attend_backward(
        kv,
        q1,
        far_query,
        d1,
        far_grad,
        first_flat,
        second_flat,
        first_lse,
        second_lse,
        starts,
        far_starts,
        cosine,
        sine,
    )
    kv_grad, gathered = lax.optimization_barrier((kv_grad, gathered))
    wk_grad, wv_grad = simple(
        kv_weights_kernel,
        [VMEM] * 4,
        [shape_of((kwidth, width), f32), shape_of((width, 2 * kwidth - LANES), f32)],
        (after(kv_grad, main0), gathered, starts, far_starts),
        "kv_weights",
    )
    main1 = scatter_parts(after(main1, main0), "y")
    kv_grad = lax.psum_scatter(kv_grad.reshape(-1, 2 * kwidth), SEQ, scatter_dimension=0, tiled=True)
    half = tail_rows(width)
    tail_half = shape_of((SIDE, half // SIDE, LANES), bf16)
    normed_part, tail, tail_away = pl.pallas_call(
        query_back_kernel,
        in_specs=[VMEM] * 7,
        out_specs=[VMEM] * 3,
        out_shape=[shape_of((width, total), f32), tail_half, tail_half],
        scratch_shapes=[pltpu.VMEM((2 * half, LANES), bf16)],
        compiler_params=params(),
        cost_estimate=cost(1),
        name="query_back",
    )(normed, query_grad, query_weight, wk_grad, wv_grad, wo_grad, gain_two_grad)
    second_query_grad = mirror(second_query_grad)
    main1 = after(main1, normed_part)
    main = jnp.concatenate([sum_parts(main0), sum_parts(main1)], axis=0)
    main = scatter_parts(main, SEQ)
    tail = (tail.astype(f32) + shift(tail_away, "core", 1).astype(f32)).astype(bf16)
    tail = exchange([tail[k] for k in range(SIDE)], "y").astype(bf16)
    tail, main = lax.optimization_barrier((tail, main))
    main = gather_all(sum_parts(main), SEQ)
    main = collect(main, "y")
    tail = gather_all(scatter_sum(tail, SEQ), SEQ)
    tail, main = lax.optimization_barrier((tail, main))
    hidden = gate_weight.shape[1]
    main_away = [shift(v, "core", 1) for v in main]
    filled = unpack_main(main, width, hidden, None)
    tail, filled = lax.optimization_barrier((collect(tail, "y"), filled))
    tail = jnp.stack(tail)
    tail_away = shift(tail, "core", 1)
    gate, up, down = unpack_main(main_away, width, hidden, filled)
    tokens_like = shape_of((micro, width, rows), bf16)
    input_grad, second_query_grad = simple(
        input_back_kernel,
        [VMEM] * 10,
        [tokens_like, tokens_like],
        (kv_grad, wk, wv, cosine, sine, normed_part, tokens, gain_one, middle_grad, second_query_grad),
        "input_back",
    )
    square = shape_of((width, width), f32)
    narrow = shape_of((kwidth, width), f32)
    line = shape_of((width,), f32)
    q_total, k_total, v_total, o_total, gain_one_total, gain_two_total = pl.pallas_call(
        unpack_tail_kernel,
        in_specs=[VMEM] * 6,
        out_specs=[VMEM] * 6,
        out_shape=[square, narrow, narrow, square, line, line],
        scratch_shapes=[pltpu.VMEM((2 * half, LANES), bf16)],
        compiler_params=params(),
        cost_estimate=cost(1),
        name="unpack_tail",
    )(tail, tail_away, query_weight, wk, wv, gain_one)
    return (
        jnp.swapaxes(result, 1, 2),
        jnp.swapaxes(input_grad, 1, 2),
        jnp.swapaxes(second_query_grad, 1, 2),
        gain_one_total,
        q_total,
        k_total.T,
        v_total.T,
        o_total,
        gain_two_total,
        gate,
        up,
        down.T,
    )


def exchange_all(value, axis):
    return [value.astype(f32)] + [shift(value, axis, k).astype(f32) for k in range(1, SIDE)]


def solution(mesh):
    grid = Mesh(mesh.devices.reshape(SIDE, SIDE, SIDE, 2), ("z", "x", "y", "core"))
    split = P(("y", "core"), SEQ, None)
    in_specs = (split, P(("y", "core"), None), split, split, split) + (P(),) * 9
    out_specs = (split, split, split) + (P(),) * 9
    return jax.shard_map(
        per_device, mesh=grid, in_specs=in_specs, out_specs=out_specs, check_vma=False
    )
```

profile of v0, /device:TPU:1, one launch (start us, length us, event | category | flops | bytes accessed | tf_op | source)
XLA Modules:
  0.0 283.3 jit_solution(18389726695729672793)
XLA Ops:
  8.7 2.6 prepare.1
  11.4 2.4 query.1.query_ref.q1_ref
  13.8 48.7 %all-gather.5.cloned.1.call-done = bf16[32,128,384]{2,1,0:T(8,128)(2,1)} async-done(((bf16[2,128,384]{2,1,0:T(8,128)(2,1)}), bf16[32,128,384]{2,1,0:T(8,128)(2,1)}) %all-gather.5.cloned.1.call-update) | async-done | bytes 3145744 | tf_op jit(solution)/shard_map/all_gather | solution.py:746
  62.5 2.5 collective-permute-start
  65.8 4.6 %attention_forward.2 = (bf16[2,576,128]{2,1,0:T(8,128)(2,1)}, f32[2,576,128]{2,1,0:T(8,128)}, f32[2,3,1,384]{3,2,1,0:T(1,128)}) custom-call(bf16[16,2,128,384]{3,2,1,0:T(8,128)(2,1)} %bitcast.64, bf16[2,576,128]{2,1,0:T(8,128)(2,1)} %query.1.query_ref.q1_ref, s32[2,1,128]{2,1,0:T(1,128)} %get-tuple-element.91.starts), custom_call_target="tpu_custom_call" | custom-call | flops 2500000000 | bytes 1000 | tf_op jit(solution)/shard_map/attention_forward/pallas_call | solution.py:228
  70.4 3.0 %collective-permute-done.query_ref.q2_ref = bf16[2,576,128]{2,1,0:T(8,128)(2,1)S(1)} collective-permute-done((bf16[2,576,128]{2,1,0:T(8,128)(2,1)S(1)}, bf16[2,576,128]{2,1,0:T(8,128)(2,1)S(1)}, u32[]{:S(2)}, u32[]{:S(2)}) %collective-permute-start) | collective-permute-done | bytes 294944 | tf_op jit(solution)/shard_map/ppermute | solution.py:664
  73.4 8.5 %feed_forward.2 = (bf16[10368,128]{1,0:T(8,128)(2,1)}, f32[576,256]{1,0:T(8,128)}, f32[256,576]{1,0:T(8,128)}, f32[256,576]{1,0:T(8,128)}) custom-call(s32[1]{0:T(128)} %bitcast.core, bf16[2,576,128]{2,1,0:T(8,128)(2,1)} %get-tuple-element.94.first, bf16[2,576,128]{2,1,0:T(8,128)(2,1)} %bitcast.58, bf16[576,576]{1,0:T(8,128)(2,1)} %out_weight.3, ...), custom_call_target="tpu_custom_call" | custom-call | flops 3000000000 | bytes 1000 | tf_op jit(solution)/shard_map/feed_forward/pallas_call | solution.py:500
  81.9 1.9 collective-permute-start.1
  83.8 5.5 %collective-permute-start.2 = (bf16[2,576,128]{2,1,0:T(8,128)(2,1)S(1)}, bf16[2,576,128]{2,1,0:T(8,128)(2,1)S(1)}, u32[]{:S(2)}, u32[]{:S(2)}) collective-permute-start(bf16[2,576,128]{2,1,0:T(8,128)(2,1)S(1)} %bitcast.68), channel_id=1, source_target_pairs={{0,120},{8,112},{16,104},{24,96},{32,88},{40,80},{48,72},{56,64},{... | collective-permute-start | bytes 884744 | tf_op jit(solution)/shard_map/ppermute | solution.py:664
  89.3 11.5 %attention_forward.3 = (bf16[2,576,128]{2,1,0:T(8,128)(2,1)}, f32[2,576,128]{2,1,0:T(8,128)}, f32[2,3,1,384]{3,2,1,0:T(1,128)}) custom-call(bf16[16,2,128,384]{3,2,1,0:T(8,128)(2,1)} %bitcast.65, bf16[2,576,128]{2,1,0:T(8,128)(2,1)} %copy-done.17, s32[2,1,128]{2,1,0:T(1,128)} %get-tuple-element.101.starts.far_starts), custom_call_target="tpu_custom_call" | custom-call | flops 2500000000 | bytes 1000 | tf_op jit(solution)/shard_map/attention_forward/pallas_call | solution.py:228
  102.3 12.2 %feed_forward.3 = (bf16[2,576,128]{2,1,0:T(8,128)(2,1)}, bf16[5632,128]{1,0:T(8,128)(2,1)}, bf16[5632,128]{1,0:T(8,128)(2,1)}, f32[576,256]{1,0:T(8,128)}, bf16[...) custom-call(s32[1]{0:T(128)} %bitcast.core, bf16[2,576,128]{2,1,0:T(8,128)(2,1)} %get-tuple-element.94.first, ...), custom_call_target="tpu_custom_call" | custom-call | flops 3000000000 | bytes 1000 | tf_op jit(solution)/shard_map/feed_forward/pallas_call | solution.py:500
  114.5 4.0 %all-to-all-start = ((bf16[4,1408,128]{2,1,0:T(8,128)(2,1)}), bf16[4,1408,128]{2,1,0:T(8,128)(2,1)S(1)}, u32[]{:S(2)}, u32[]{:S(2)}) async-start(bf16[4,1408,128]{2,1,0:T(8,128)(2,1)} %bitcast.44), calls=%async_computation.1 | async-start | bytes 2883584 | tf_op jit(solution)/shard_map/all_to_all | solution.py:681
  119.2 18.6 %attention_backward.1 = (bf16[16,2,128,384]{3,2,1,0:T(8,128)(2,1)}, bf16[2,576,128]{2,1,0:T(8,128)(2,1)}, bf16[2,576,128]{2,1,0:T(8,128)(2,1)}) custom-call(bf16[16,2,128,384]{3,2,1,0:T(8,128)(2,1)} %bitcast.66, bf16[2,576,128]{2,1,0:T(8,128)(2,1)} %query.1.query_ref.q1_ref, bf16[2,576,128]{2,1,0:T(8,128)(2,1)} %copy-done.17, ...), custom_call_target="tpu_custom_call" | custom-call | flops 7000000000 | bytes 1000 | tf_op jit(solution)/shard_map/attention_backward/pallas_call | solution.py:308
  137.9 4.2 %all-to-all-start.1 = ((bf16[4,1408,128]{2,1,0:T(8,128)(2,1)}), bf16[4,1408,128]{2,1,0:T(8,128)(2,1)S(1)}, u32[]{:S(2)}, u32[]{:S(2)}) async-start(bf16[4,1408,128]{2,1,0:T(8,128)(2,1)} %bitcast.43), calls=%async_computation.2 | async-start | bytes 2883584 | tf_op jit(solution)/shard_map/all_to_all | solution.py:681
  142.1 8.6 %kv_weights.1 = (f32[192,576]{1,0:T(8,128)}, f32[576,256]{1,0:T(8,128)}) custom-call(bf16[16,2,128,384]{3,2,1,0:T(8,128)(2,1)} %get-tuple-element.116.sums, bf16[16,2,704,128]{3,2,1,0:T(8,128)(2,1)} %bitcast.39, s32[2,1,128]{2,1,0:T(1,128)} %get-tuple-element.91.starts, s32[2,1,128]{2,1,0:T(1,128)} %get-tuple-element.101.starts.far_starts), custom_call_target="tpu_custom_call" | custom-call | flops 2000000000 | bytes 1000 | tf_op jit(solution)/shard_map/kv_weights/pallas_call | solution.py:90
  150.7 4.3 %query_back.1 = (f32[576,256]{1,0:T(8,128)}, bf16[4,1024,128]{2,1,0:T(8,128)(2,1)}, bf16[4,1024,128]{2,1,0:T(8,128)(2,1)}) custom-call(bf16[2,704,128]{2,1,0:T(8,128)(2,1)} %get-tuple-element.112.normed, bf16[2,576,128]{2,1,0:T(8,128)(2,1)} %get-tuple-element.114.grad_ref, bf16[576,576]{1,0:T(8,128)(2,1)} %wq.1, f32[192,576]{1,0:T(8,128)} %get-tuple-element.118.wk_grad, ...), custom_call_target="tpu_custom_call" | custom-call | flops 1000000000 | bytes 1000 | tf_op jit(solution)/shard_map/query_back/pallas_call | solution.py:795
  156.7 3.5 %all-to-all-done.1 = bf16[4,1408,128]{2,1,0:T(8,128)(2,1)S(1)} async-done(((bf16[4,1408,128]{2,1,0:T(8,128)(2,1)}), bf16[4,1408,128]{2,1,0:T(8,128)(2,1)S(1)}, u32[]{:S(2)}, u32[]{:S(2)}) %all-to-all-start.1) | async-done | bytes 1441824 | tf_op jit(solution)/shard_map/all_to_all | solution.py:681
  161.6 7.4 %all-to-all-start.2 = ((bf16[16,176,128]{2,1,0:T(8,128)(2,1)}), bf16[16,176,128]{2,1,0:T(8,128)(2,1)S(1)}, u32[]{:S(2)}, u32[]{:S(2)}) async-start(bf16[16,176,128]{2,1,0:T(8,128)(2,1)} %bitcast.20), calls=%async_computation.3 | async-start | bytes 1441792 | tf_op jit(solution)/shard_map/all_to_all | solution.py:681
  171.0 2.3 collective-permute-start.7
  173.3 6.0 %collective-permute-done.5 = bf16[1024,128]{1,0:T(8,128)(2,1)S(1)} collective-permute-done((bf16[1024,128]{1,0:T(8,128)(2,1)S(1)}, bf16[1024,128]{1,0:T(8,128)(2,1)S(1)}, u32[]{:S(2)}, u32[]{:S(2)}) %collective-permute-start.5) | collective-permute-done | bytes 262176 | tf_op jit(solution)/shard_map/ppermute | solution.py:659
  179.3 4.4 %collective-permute-done.6 = bf16[1024,128]{1,0:T(8,128)(2,1)S(1)} collective-permute-done((bf16[1024,128]{1,0:T(8,128)(2,1)S(1)}, bf16[1024,128]{1,0:T(8,128)(2,1)S(1)}, u32[]{:S(2)}, u32[]{:S(2)}) %collective-permute-start.6) | collective-permute-done | bytes 262176 | tf_op jit(solution)/shard_map/ppermute | solution.py:659
  184.1 17.7 %all_to_all.30 = bf16[16,176,128]{2,1,0:T(8,128)(2,1)S(1)} all-to-all(bf16[16,176,128]{2,1,0:T(8,128)(2,1)S(1)} %broadcast_in_dim.5), channel_id=1, replica_groups=mesh['z'=4,'x'=4,'y'=4,'core'=2] {'z','x'}, dimensions={0} | all-to-all | bytes 1441792 | tf_op jit(solution)/shard_map/all_to_all | solution.py:696
  203.2 2.2 collective-permute-start.9
  205.4 11.3 %all_to_all.31 = bf16[16,64,128]{2,1,0:T(8,128)(2,1)S(1)} all-to-all(bf16[16,64,128]{2,1,0:T(8,128)(2,1)S(1)} %bitcast.45), channel_id=1, replica_groups=mesh['z'=4,'x'=4,'y'=4,'core'=2] {'z','x'}, dimensions={0} | all-to-all | bytes 524288 | tf_op jit(solution)/shard_map/all_to_all | solution.py:681
  216.8 10.4 %all_to_all.32 = bf16[16,64,128]{2,1,0:T(8,128)(2,1)S(1)} all-to-all(bf16[16,64,128]{2,1,0:T(8,128)(2,1)S(1)} %broadcast_in_dim.4), channel_id=1, replica_groups=mesh['z'=4,'x'=4,'y'=4,'core'=2] {'z','x'}, dimensions={0} | all-to-all | bytes 524288 | tf_op jit(solution)/shard_map/all_to_all | solution.py:696
  227.2 11.1 %collective-permute-done.8.refs_1_ = bf16[2816,128]{1,0:T(8,128)(2,1)} collective-permute-done((bf16[2816,128]{1,0:T(8,128)(2,1)S(1)}, bf16[2816,128]{1,0:T(8,128)(2,1)}, u32[]{:S(2)}, u32[]{:S(2)}) %collective-permute-start.8) | collective-permute-done | bytes 720928 | tf_op jit(solution)/shard_map/ppermute | solution.py:659
  239.8 4.5 %unpack_main.2 = (f32[576,1536]{1,0:T(8,128)}, f32[576,1536]{1,0:T(8,128)}, f32[576,1536]{1,0:T(8,128)}) custom-call(bf16[2816,128]{1,0:T(8,128)(2,1)} %bitcast.53, bf16[2816,128]{1,0:T(8,128)(2,1)} %collective-permute-done.8.refs_1_, bf16[2816,128]{1,0:T(8,128)(2,1)} %copy-done.13, bf16[2816,128]{1,0:T(8,128)(2,1)} %copy-done.11), custom_call_target="tpu_custom_call" | custom-call | flops 1500000000 | bytes 1000 | tf_op jit(solution)/shard_map/unpack_main/pallas_call | solution.py:640
  246.6 7.1 %collective-permute-done.11 = bf16[1024,128]{1,0:T(8,128)(2,1)S(1)} collective-permute-done((bf16[1024,128]{1,0:T(8,128)(2,1)S(1)}, bf16[1024,128]{1,0:T(8,128)(2,1)S(1)}, u32[]{:S(2)}, u32[]{:S(2)}) %collective-permute-start.11) | collective-permute-done | bytes 262176 | tf_op jit(solution)/shard_map/ppermute | solution.py:659
  255.6 3.3 %collective-permute-done.15.refs_0_ = bf16[2816,128]{1,0:T(8,128)(2,1)S(1)} collective-permute-done((bf16[2816,128]{1,0:T(8,128)(2,1)S(1)}, bf16[2816,128]{1,0:T(8,128)(2,1)S(1)}, u32[]{:S(2)}, u32[]{:S(2)}) %collective-permute-start.15) | collective-permute-done | bytes 720928 | tf_op jit(solution)/shard_map/ppermute | solution.py:659
  263.0 4.5 %unpack_main.3 = (f32[576,1536]{1,0:T(8,128)}, f32[576,1536]{1,0:T(8,128)}, f32[576,1536]{1,0:T(8,128)}) custom-call(bf16[2816,128]{1,0:T(8,128)(2,1)} %copy-done.5, bf16[2816,128]{1,0:T(8,128)(2,1)} %copy-done.6, bf16[2816,128]{1,0:T(8,128)(2,1)} %copy-done.7, ...), custom_call_target="tpu_custom_call", output_to_operand_aliasing={{0}: (4, {}), {1}: (5, {}), {2}: (6, {})} | custom-call | flops 1500000000 | bytes 1000 | tf_op jit(solution)/shard_map/unpack_main/pallas_call | solution.py:640
  268.4 4.6 %unpack_tail.1 = (f32[576,576]{1,0:T(8,128)}, f32[192,576]{1,0:T(8,128)}, f32[192,576]{1,0:T(8,128)}, f32[576,576]{1,0:T(8,128)}, f32[576]{0:T(1024)}, /*index=5*/f32[576]{0:T(1024)}) custom-call(bf16[4,1024,128]{2,1,0:T(8,128)(2,1)} %copy-done.2, bf16[4,1024,128]{2,1,0:T(8,128)(2,1)} %copy-done.10, bf16[576,576]{1,0:T(8,128)(2,1)} %wq.1, ...), custom_call_target="tpu_custom_call" | custom-call | flops 1000000000 | bytes 1000 | tf_op jit(solution)/shard_map/unpack_tail/pallas_call | solution.py:834
  273.7 3.1 %input_back.1 = (bf16[2,576,128]{2,1,0:T(8,128)(2,1)}, bf16[2,576,128]{2,1,0:T(8,128)(2,1)}) custom-call(bf16[256,384]{1,0:T(8,128)(2,1)} %reduce-scatter.2.cloned.1.call-done.kv_grad, bf16[192,576]{1,0:T(8,128)(2,1)} %bitcast.72, bf16[192,576]{1,0:T(8,128)(2,1)} %bitcast.75, f32[32,256]{1,0:T(8,128)} %get-tuple-element.87.cos_ref, ...), custom_call_target="tpu_custom_call" | custom-call | flops 1000000000 | bytes 1000 | tf_op jit(solution)/shard_map/input_back/pallas_call | solution.py:90
  (90 shorter events, 22.9 us)
Async XLA Ops:
  7.2 55.3 %all-gather.5.cloned.1.call-start = ((), (), s32[]{:S(2)}) async-start(), calls=%async_computation.8 | async-start | bytes 3342336 | tf_op jit(solution)/shard_map/all_gather | solution.py:746
  11.3 51.2 %copy-start.14 = (bf16[2,128,576]{1,2,0:T(8,128)(2,1)S(1)}, bf16[2,128,576]{1,2,0:T(8,128)(2,1)}, u32[]{:S(2)}) copy-start(bf16[2,128,576]{1,2,0:T(8,128)(2,1)} %param.16) | copy-start | bytes 884740
  11.3 53.7 %copy-start.9 = (bf16[576]{0:T(1024)(128)(2,1)S(1)}, bf16[576]{0:T(1024)(128)(2,1)}, u32[]{:S(2)}) copy-start(bf16[576]{0:T(1024)(128)(2,1)} %param.24) | copy-start | bytes 3460
  11.3 126.5 %all-gather.7.cloned.1.call-start = ((), (), s32[]{:S(2)}) async-start(), calls=%async_computation.9 | async-start | bytes 6127616 | tf_op jit(solution)/shard_map/all_gather | solution.py:757
  62.5 10.9 %collective-permute-start = (bf16[2,576,128]{2,1,0:T(8,128)(2,1)S(1)}, bf16[2,576,128]{2,1,0:T(8,128)(2,1)S(1)}, u32[]{:S(2)}, u32[]{:S(2)}) collective-permute-start(bf16[2,576,128]{2,1,0:T(8,128)(2,1)S(1)} %bitcast.67), channel_id=1, source_target_pairs={{0,120},{8,112},{16,104},{24,96},{32,88},{40,80},{48,72},{56,64},{... | collective-permute-start | bytes 884744 | tf_op jit(solution)/shard_map/ppermute | solution.py:664
  81.9 18.9 %collective-permute-start.1 = (bf16[10368,128]{1,0:T(8,128)(2,1)}, bf16[10368,128]{1,0:T(8,128)(2,1)S(1)}, u32[]{:S(2)}, u32[]{:S(2)}) collective-permute-start(bf16[10368,128]{1,0:T(8,128)(2,1)} %get-tuple-element.98), channel_id=1, source_target_pairs={{0,1},{1,0},{2,3},{3,2},{4,5},{5,4},{6,7},{7,6},{8,9},{9,8},{10,11... | collective-permute-start | bytes 7962632 | tf_op jit(solution)/shard_map/ppermute | solution.py:659
  83.8 34.7 %collective-permute-start.2 = (bf16[2,576,128]{2,1,0:T(8,128)(2,1)S(1)}, bf16[2,576,128]{2,1,0:T(8,128)(2,1)S(1)}, u32[]{:S(2)}, u32[]{:S(2)}) collective-permute-start(bf16[2,576,128]{2,1,0:T(8,128)(2,1)S(1)} %bitcast.68), channel_id=1, source_target_pairs={{0,120},{8,112},{16,104},{24,96},{32,88},{40,80},{48,72},{56,64},{... | collective-permute-start | bytes 884744 | tf_op jit(solution)/shard_map/ppermute | solution.py:664
  114.5 23.3 %all-to-all-start = ((bf16[4,1408,128]{2,1,0:T(8,128)(2,1)}), bf16[4,1408,128]{2,1,0:T(8,128)(2,1)S(1)}, u32[]{:S(2)}, u32[]{:S(2)}) async-start(bf16[4,1408,128]{2,1,0:T(8,128)(2,1)} %bitcast.44), calls=%async_computation.1 | async-start | bytes 2883584 | tf_op jit(solution)/shard_map/all_to_all | solution.py:681
  118.5 154.5 %reduce-scatter.2.cloned.1.call-start = ((), (), s32[]{:S(2)}) async-start(), calls=%async_computation.7 | async-start | bytes 3342336 | tf_op jit(solution)/shard_map/reduce_scatter | solution.py:792
  137.9 22.3 %all-to-all-start.1 = ((bf16[4,1408,128]{2,1,0:T(8,128)(2,1)}), bf16[4,1408,128]{2,1,0:T(8,128)(2,1)S(1)}, u32[]{:S(2)}, u32[]{:S(2)}) async-start(bf16[4,1408,128]{2,1,0:T(8,128)(2,1)} %bitcast.43), calls=%async_computation.2 | async-start | bytes 2883584 | tf_op jit(solution)/shard_map/all_to_all | solution.py:681
  155.1 13.9 %collective-permute-start.4 = (bf16[4,1024,128]{2,1,0:T(8,128)(2,1)}, bf16[4,1024,128]{2,1,0:T(8,128)(2,1)}, u32[]{:S(2)}, u32[]{:S(2)}) collective-permute-start(bf16[4,1024,128]{2,1,0:T(8,128)(2,1)} %get-tuple-element.128), channel_id=1, source_target_pairs={{0,1},{1,0},{2,3},{3,2},{4,5},{5,4},{6,7},{7,6},{8,9},{9,8},{10,11... | collective-permute-start | bytes 3145736 | tf_op jit(solution)/shard_map/ppermute | solution.py:659
  161.6 22.3 %all-to-all-start.2 = ((bf16[16,176,128]{2,1,0:T(8,128)(2,1)}), bf16[16,176,128]{2,1,0:T(8,128)(2,1)S(1)}, u32[]{:S(2)}, u32[]{:S(2)}) async-start(bf16[16,176,128]{2,1,0:T(8,128)(2,1)} %bitcast.20), calls=%async_computation.3 | async-start | bytes 1441792 | tf_op jit(solution)/shard_map/all_to_all | solution.py:681
  170.5 8.8 %collective-permute-start.5 = (bf16[1024,128]{1,0:T(8,128)(2,1)S(1)}, bf16[1024,128]{1,0:T(8,128)(2,1)S(1)}, u32[]{:S(2)}, u32[]{:S(2)}) collective-permute-start(bf16[1024,128]{1,0:T(8,128)(2,1)S(1)} %get-tuple-element.158), channel_id=1, source_target_pairs={{0,2},{2,4},{4,6},{6,0},{1,3},{3,5},{5,7},{7,1},{8,10},{10,12},{12... | collective-permute-start | bytes 786440 | tf_op jit(solution)/shard_map/ppermute | solution.py:659
  171.0 8.3 %collective-permute-start.7 = (bf16[1024,128]{1,0:T(8,128)(2,1)S(1)}, bf16[1024,128]{1,0:T(8,128)(2,1)S(1)}, u32[]{:S(2)}, u32[]{:S(2)}) collective-permute-start(bf16[1024,128]{1,0:T(8,128)(2,1)S(1)} %get-tuple-element.159), channel_id=1, source_target_pairs={{0,6},{2,0},{4,2},{6,4},{1,7},{3,1},{5,3},{7,5},{8,14},{10,8},{12,... | collective-permute-start | bytes 786440 | tf_op jit(solution)/shard_map/ppermute | solution.py:659
  173.3 10.5 %collective-permute-start.6 = (bf16[1024,128]{1,0:T(8,128)(2,1)S(1)}, bf16[1024,128]{1,0:T(8,128)(2,1)S(1)}, u32[]{:S(2)}, u32[]{:S(2)}) collective-permute-start(bf16[1024,128]{1,0:T(8,128)(2,1)S(1)} %get-tuple-element.160), channel_id=1, source_target_pairs={{0,4},{2,6},{4,0},{6,2},{1,5},{3,7},{5,1},{7,3},{8,12},{10,14},{12... | collective-permute-start | bytes 786440 | tf_op jit(solution)/shard_map/ppermute | solution.py:659
  201.8 38.0 %copy-start.3 = (bf16[16,176,128]{2,1,0:T(8,128)(2,1)}, bf16[16,176,128]{2,1,0:T(8,128)(2,1)S(1)}, u32[]{:S(2)}) copy-start(bf16[16,176,128]{2,1,0:T(8,128)(2,1)S(1)} %all_to_all.30) | copy-start | bytes 2162692
  201.8 25.4 %collective-permute-start.10 = (bf16[2816,128]{1,0:T(8,128)(2,1)S(1)}, bf16[2816,128]{1,0:T(8,128)(2,1)S(1)}, u32[]{:S(2)}, u32[]{:S(2)}) collective-permute-start(bf16[2816,128]{1,0:T(8,128)(2,1)S(1)} %bitcast.50), channel_id=1, source_target_pairs={{0,6},{2,0},{4,2},{6,4},{1,7},{3,1},{5,3},{7,5},{8,14},{10,8},{12,... | collective-permute-start | bytes 2162696 | tf_op jit(solution)/shard_map/ppermute | solution.py:659
  203.2 24.0 %collective-permute-start.9 = (bf16[2816,128]{1,0:T(8,128)(2,1)S(1)}, bf16[2816,128]{1,0:T(8,128)(2,1)S(1)}, u32[]{:S(2)}, u32[]{:S(2)}) collective-permute-start(bf16[2816,128]{1,0:T(8,128)(2,1)S(1)} %bitcast.51), channel_id=1, source_target_pairs={{0,4},{2,6},{4,0},{6,2},{1,5},{3,7},{5,1},{7,3},{8,12},{10,14},{12... | collective-permute-start | bytes 2162696 | tf_op jit(solution)/shard_map/ppermute | solution.py:659
  205.4 32.9 %collective-permute-start.8 = (bf16[2816,128]{1,0:T(8,128)(2,1)S(1)}, bf16[2816,128]{1,0:T(8,128)(2,1)}, u32[]{:S(2)}, u32[]{:S(2)}) collective-permute-start(bf16[2816,128]{1,0:T(8,128)(2,1)S(1)} %bitcast.52), channel_id=1, source_target_pairs={{0,2},{2,4},{4,6},{6,0},{1,3},{3,5},{5,7},{7,1},{8,10},{10,12},{12... | collective-permute-start | bytes 2162696 | tf_op jit(solution)/shard_map/ppermute | solution.py:659
  227.2 12.6 %copy-start.11 = (bf16[2816,128]{1,0:T(8,128)(2,1)}, bf16[2816,128]{1,0:T(8,128)(2,1)S(1)}, u32[]{:S(2)}) copy-start(bf16[2816,128]{1,0:T(8,128)(2,1)S(1)} %collective-permute-done.10.refs_3_) | copy-start | bytes 2162692
  227.2 12.6 %copy-start.13 = (bf16[2816,128]{1,0:T(8,128)(2,1)}, bf16[2816,128]{1,0:T(8,128)(2,1)S(1)}, u32[]{:S(2)}) copy-start(bf16[2816,128]{1,0:T(8,128)(2,1)S(1)} %collective-permute-done.9.refs_2_) | copy-start | bytes 2162692
  238.3 7.4 %collective-permute-start.13 = (bf16[1024,128]{1,0:T(8,128)(2,1)S(1)}, bf16[1024,128]{1,0:T(8,128)(2,1)S(1)}, u32[]{:S(2)}, u32[]{:S(2)}) collective-permute-start(bf16[1024,128]{1,0:T(8,128)(2,1)S(1)} %bitcast.46), channel_id=1, source_target_pairs={{0,6},{2,0},{4,2},{6,4},{1,7},{3,1},{5,3},{7,5},{8,14},{10,8},{12,... | collective-permute-start | bytes 786440 | tf_op jit(solution)/shard_map/ppermute | solution.py:659
  238.3 8.3 %collective-permute-start.12 = (bf16[1024,128]{1,0:T(8,128)(2,1)S(1)}, bf16[1024,128]{1,0:T(8,128)(2,1)S(1)}, u32[]{:S(2)}, u32[]{:S(2)}) collective-permute-start(bf16[1024,128]{1,0:T(8,128)(2,1)S(1)} %bitcast.47), channel_id=1, source_target_pairs={{0,4},{2,6},{4,0},{6,2},{1,5},{3,7},{5,1},{7,3},{8,12},{10,14},{12... | collective-permute-start | bytes 786440 | tf_op jit(solution)/shard_map/ppermute | solution.py:659
  238.9 14.7 %collective-permute-start.11 = (bf16[1024,128]{1,0:T(8,128)(2,1)S(1)}, bf16[1024,128]{1,0:T(8,128)(2,1)S(1)}, u32[]{:S(2)}, u32[]{:S(2)}) collective-permute-start(bf16[1024,128]{1,0:T(8,128)(2,1)S(1)} %bitcast.48), channel_id=1, source_target_pairs={{0,2},{2,4},{4,6},{6,0},{1,3},{3,5},{5,7},{7,1},{8,10},{10,12},{12... | collective-permute-start | bytes 786440 | tf_op jit(solution)/shard_map/ppermute | solution.py:659
  244.3 14.7 %copy-start.16 = (bf16[2,576,128]{2,1,0:T(8,128)(2,1)S(1)}, bf16[2,576,128]{2,1,0:T(8,128)(2,1)}, u32[]{:S(2)}) copy-start(bf16[2,576,128]{2,1,0:T(8,128)(2,1)} %get-tuple-element.124) | copy-start | bytes 884740
  253.8 13.6 %copy-start.2 = (bf16[4,1024,128]{2,1,0:T(8,128)(2,1)}, bf16[4,1024,128]{2,1,0:T(8,128)(2,1)S(1)}, u32[]{:S(2)}) copy-start(bf16[4,1024,128]{2,1,0:T(8,128)(2,1)S(1)} %pad_maximum_fusion.kept) | copy-start | bytes 3145732
  253.8 13.6 %collective-permute-start.14 = (bf16[4,1024,128]{2,1,0:T(8,128)(2,1)S(1)}, bf16[4,1024,128]{2,1,0:T(8,128)(2,1)S(1)}, u32[]{:S(2)}, u32[]{:S(2)}) collective-permute-start(bf16[4,1024,128]{2,1,0:T(8,128)(2,1)S(1)} %pad_maximum_fusion.kept), channel_id=1, source_target_pairs={{0,1},{1,0},{2,3},{3,2},{4,5},{5,4},{6,7},{7,6},{8,9},{9,8},{10,11... | collective-permute-start | bytes 3145736 | tf_op jit(solution)/shard_map/ppermute | solution.py:659
  254.6 4.3 %collective-permute-start.15 = (bf16[2816,128]{1,0:T(8,128)(2,1)S(1)}, bf16[2816,128]{1,0:T(8,128)(2,1)S(1)}, u32[]{:S(2)}, u32[]{:S(2)}) collective-permute-start(bf16[2816,128]{1,0:T(8,128)(2,1)S(1)} %bitcast.54), channel_id=1, source_target_pairs={{0,1},{1,0},{2,3},{3,2},{4,5},{5,4},{6,7},{7,6},{8,9},{9,8},{10,11... | collective-permute-start | bytes 2162696 | tf_op jit(solution)/shard_map/ppermute | solution.py:659
  254.7 5.1 %collective-permute-start.16 = (bf16[2816,128]{1,0:T(8,128)(2,1)}, bf16[2816,128]{1,0:T(8,128)(2,1)S(1)}, u32[]{:S(2)}, u32[]{:S(2)}) collective-permute-start(bf16[2816,128]{1,0:T(8,128)(2,1)} %collective-permute-done.8.refs_1_), channel_id=1, source_target_pairs={{0,1},{1,0},{2,3},{3,2},{4,5},{5,4},{6,7},{7,6},{8,9},{9,8},{10,11... | collective-permute-start | bytes 2162696 | tf_op jit(solution)/shard_map/ppermute | solution.py:659
  255.1 6.1 %collective-permute-start.17 = (bf16[2816,128]{1,0:T(8,128)(2,1)}, bf16[2816,128]{1,0:T(8,128)(2,1)S(1)}, u32[]{:S(2)}, u32[]{:S(2)}) collective-permute-start(bf16[2816,128]{1,0:T(8,128)(2,1)} %copy-done.13), channel_id=1, source_target_pairs={{0,1},{1,0},{2,3},{3,2},{4,5},{5,4},{6,7},{7,6},{8,9},{9,8},{10,11... | collective-permute-start | bytes 2162696 | tf_op jit(solution)/shard_map/ppermute | solution.py:659
  255.2 6.0 %collective-permute-start.18 = (bf16[2816,128]{1,0:T(8,128)(2,1)S(1)}, bf16[2816,128]{1,0:T(8,128)(2,1)S(1)}, u32[]{:S(2)}, u32[]{:S(2)}) collective-permute-start(bf16[2816,128]{1,0:T(8,128)(2,1)S(1)} %copy-done.12), channel_id=1, source_target_pairs={{0,1},{1,0},{2,3},{3,2},{4,5},{5,4},{6,7},{7,6},{8,9},{9,8},{10,11... | collective-permute-start | bytes 2162696 | tf_op jit(solution)/shard_map/ppermute | solution.py:659
  259.0 14.0 %collective-permute-start.3 = (bf16[2,576,128]{2,1,0:T(8,128)(2,1)S(1)}, bf16[2,576,128]{2,1,0:T(8,128)(2,1)S(1)}, u32[]{:S(2)}, u32[]{:S(2)}) collective-permute-start(bf16[2,576,128]{2,1,0:T(8,128)(2,1)S(1)} %copy-done.16), channel_id=1, source_target_pairs={{0,120},{8,112},{16,104},{24,96},{32,88},{40,80},{48,72},{56,64},{... | collective-permute-start | bytes 884744 | tf_op jit(solution)/shard_map/ppermute | solution.py:664
  (13 other events, 57.8 us)
Sparse Core Ops, SparseCore 0:
  11.4 50.9 all-gather.4
  65.2 63.3 all-gather.6
  138.0 83.7 reduce-scatter.1
where the time goes:
time: 284 us; the launch traced here: 283 us
  waiting for transfers between devices  91 us (32%)
  Pallas kernels  89.9 us (32%)
  blocking collectives  39.3 us (14%)
  starting transfers between devices  37.3 us (13%)
  between operations  14 us (5%)
  local copies, waits for them, and re-layouts  8.14 us (3%)
  other arithmetic  3.65 us (1%)
    all_gather x1, waiting for transfers between devices, per_device(): kv = lax.all_gather(kv, SEQ, axis=0)  48.7 us
    ppermute x16, waiting for transfers between devices, shift(): lax.ppermute(value, axis, [(i, (i + distance) % size) for i in range(size)])  35.7 us
    all_to_all x2, blocking collectives, gather_all(): return lax.all_to_all(spread, axis, 0, 0).reshape(places * rows, lanes)  28.1 us
    pallas_call x2, Pallas kernels, feed_forward(): pl.pallas_call(functools.partial(ffn_kernel, last), grid_spec=pltpu.Prefe...  20.7 us
    pallas_call x1, Pallas kernels, attend_backward(): pl.pallas_call(backward_kernel, grid=(micro,), in_specs=[one_of(kv.shape,...  18.6 us
    pallas_call x4, Pallas kernels, simple(): pl.pallas_call(kernel, in_specs=in_specs, out_specs=[VMEM] * len(outs), o...  16.7 us
    pallas_call x2, Pallas kernels, attend_forward(): pl.pallas_call(functools.partial(forward_kernel, far), grid=(micro,), in_...  16.1 us
    all_to_all x3, starting transfers between devices, scatter_parts(): lax.all_to_all(held.reshape(places, rows // places, lanes), axis, 0, 0)  15.6 us
  transfers between devices with their start and end apart: 25, of which 11 were waited for; matrix products, arithmetic and copies ran while one was open for 2% of the time, Pallas kernels for 30%

commit v1 on v0

--- a/solution.py
+++ b/solution.py
@@ -21,7 +21,7 @@
 LANES = 128
 SIDE = 4
 KEYS = 256
-CHUNK = 384
+CHUNK = 256
 SEQ = ("z", "x")
 SIMPLE = {"kv_weights": 2.0, "input_back": 1.0, "prepare": 1.0, "query": 1.0}
 f32 = jnp.float32
@@ -67,6 +67,20 @@
 
 def side_by_side(ref):
     return jnp.concatenate([ref[m] for m in range(ref.shape[0])], axis=1)
+
+
+def interleave(keys, values):
+    parts = []
+    for g in range(KVH):
+        span = slice(g * HD, (g + 1) * HD)
+        parts += [keys[span], values[span]]
+    return jnp.concatenate(parts, axis=0)
+
+
+def part_of(flat, index):
+    return jnp.concatenate(
+        [flat[(2 * g + index) * HD : (2 * g + index + 1) * HD] for g in range(KVH)], axis=0
+    )
 
 
 def own_block():
@@ -135,8 +149,8 @@
             normed_out[m, base : base + HALF] = high
             normed_out[m, base + HALF : base + 2 * HALF] = (table[:, span] - high.astype(f32)).astype(bf16)
             base += 2 * HALF
-    parts = turn(mul(wk[...], normed), cosine, sine, KVH)
-    flat = jnp.concatenate(parts + [mul(wv[...], normed)], axis=0).astype(bf16)
+    keys = turn(mul(wk[...], normed), cosine, sine, KVH)
+    flat = interleave(jnp.concatenate(keys, axis=0), mul(wv[...], normed)).astype(bf16)
     for m in range(micro):
         kv_out[m] = flip(flat[:, m * rows : (m + 1) * rows])
 
@@ -155,11 +169,6 @@
     return jnp.concatenate(
         [ref[(group * GROUP + h) * HD : (group * GROUP + h + 1) * HD, :] for h in range(GROUP)], axis=1
     )
-
-
-def padded(block, place):
-    zero = jnp.zeros_like(block)
-    return jnp.concatenate([block, zero] if place % 2 == 0 else [zero, block], axis=0)
 
 
 def visible_bias(start, block, first_key, rows):
@@ -192,15 +201,14 @@
         block = held[pl.ds(step * per, per), 0].reshape(KEYS, held.shape[3])
         bias = visible_bias(start, block_place, step * KEYS, rows)
         tiles = [block[:, i * LANES : (i + 1) * LANES] for i in range(3)]
-        turned = [None, jnp.transpose(tiles[1]), jnp.transpose(tiles[2])]
         for g in range(KVH):
-            scores = mul(tiles[g // 2], padded(lane_heads(query, g), g)) + bias
+            heads = lane_heads(query, g)
+            scores = mul(tiles[g], jnp.concatenate([heads, jnp.zeros_like(heads)], axis=0)) + bias
             old = peak[g]
             top = jnp.maximum(old, jnp.max(scores, axis=0, keepdims=True))
             weights = jnp.exp(scores - top)
             decay = jnp.exp(old - top)
-            place = KVH + g
-            values = turned[place // 2][(place % 2) * HD : (place % 2 + 1) * HD]
+            values = jnp.transpose(tiles[g])[HD:]
             mass[g] = mass[g] * decay + jnp.sum(weights, axis=0, keepdims=True)
             acc[g] = acc[g] * decay + mul(values, weights.astype(bf16))
             peak[g] = top
@@ -245,7 +253,7 @@
 
 def backward_kernel(
     held, q1_ref, q2_ref, d1_ref, d2_ref, o1, o2, lse1, lse2, starts, far_starts, cos_ref, sin_ref,
-    kv_out, first_grad, second_grad, sums, delta, dq, query2,
+    kv_out, first_grad, second_grad, sums, delta, dq, query2, both,
 ):
     rows = q1_ref.shape[2]
     per = KEYS // rows
@@ -255,8 +263,12 @@
 
     def attention(a, q_ref, d_ref, o_ref, lse_ref, start, block_place):
         for g in range(KVH):
-            product = lane_heads(d_ref, g).astype(f32) * lane_heads(o_ref, g)
-            delta[a, g] = jnp.sum(product, axis=0, keepdims=True)
+            query, grad = lane_heads(q_ref, g), lane_heads(d_ref, g)
+            delta[a, g] = jnp.sum(grad.astype(f32) * lane_heads(o_ref, g), axis=0, keepdims=True)
+            zero = jnp.zeros_like(query)
+            both[g] = jnp.concatenate(
+                [jnp.concatenate([query, zero], axis=1), jnp.concatenate([zero, grad], axis=1)], axis=0
+            )
         first_step, last_step = key_steps(start, block_place, rows)
 
         @pl.loop(first_step, last_step)
@@ -264,24 +276,15 @@
             block = held[pl.ds(step * per, per), 0].reshape(KEYS, held.shape[3])
             bias = visible_bias(start, block_place, step * KEYS, rows)
             tiles = [block[:, i * LANES : (i + 1) * LANES] for i in range(3)]
-            turned = [jnp.transpose(tiles[0]), jnp.transpose(tiles[1])]
-            total = [None] * 3
-
-            def add(place, value):
-                total[place] = value if total[place] is None else total[place] + value
-
+            total = []
             for g in range(KVH):
-                place = KVH + g
-                keys = turned[g // 2][(g % 2) * HD : (g % 2 + 1) * HD]
-                query = padded(lane_heads(q_ref, g), g)
-                grad = padded(lane_heads(d_ref, g), place)
-                scores = mul(tiles[g // 2], query) + bias
-                weights = jnp.exp(scores - lse_ref[0, g])
-                weight_grad = mul(tiles[place // 2], grad)
-                score_grad = (weights * (weight_grad - delta[a, g])).astype(bf16)
-                dq[a, g] += mul(keys, score_grad)
-                add(g // 2, mul_nt(score_grad, query))
-                add(place // 2, mul_nt(weights.astype(bf16), grad))
+                pair = both[g]
+                lanes = pair.shape[1] // 2
+                products = mul(tiles[g], pair)
+                weights = jnp.exp(products[:, :lanes] + bias - lse_ref[0, g])
+                score_grad = (weights * (products[:, lanes:] - delta[a, g])).astype(bf16)
+                dq[a, g] += mul(jnp.transpose(tiles[g])[:HD], score_grad)
+                total.append(mul_nt(jnp.concatenate([score_grad, weights.astype(bf16)], axis=1), pair))
             joined = jnp.concatenate(total, axis=1)
             sums[pl.ds(step * per, per)] += joined.reshape(per, rows, joined.shape[1])
 
@@ -316,6 +319,7 @@
             pltpu.VMEM((2, KVH, 1, lanes), f32),
             pltpu.VMEM((2, KVH, HD, lanes), f32),
             pltpu.VMEM((width, rows), bf16),
+            pltpu.VMEM((KVH, 2 * HD, 2 * lanes), bf16),
         ],
         compiler_params=params(),
         cost_estimate=cost(7),
@@ -323,36 +327,82 @@
     )(kv, *arrays)
 
 
-def kv_weights_kernel(sums, normed, starts, far_starts, k_out, v_out):
+def weights_kernel(
+    sums, normed, starts, far_starts, own_normed, grad_ref, weight, wo_grad, gain_two_grad,
+    normed_grad, kept, away, kv_out, packed,
+):
+    rows = starts.shape[2]
+    width = weight.shape[0]
+    per = KEYS // rows
+
+    @pl.when(pl.program_id(0) == 0)
+    def _():
+        kv_out[...] = jnp.zeros_like(kv_out)
+
+    def add(step):
+        block = sums[pl.ds(step * per, per), 0].reshape(KEYS, sums.shape[3])
+        inner = [normed[step * per + i, 0] for i in range(per)]
+        values = jnp.concatenate([v[:width] for v in inner], axis=1)
+        tables = jnp.concatenate([v[width:] for v in inner], axis=1).astype(f32)
+        cosine = tables[:HALF] + tables[HALF : 2 * HALF]
+        sine = tables[2 * HALF : 3 * HALF] + tables[3 * HALF :]
+        flat = jnp.concatenate([jnp.transpose(block[:, g * LANES : (g + 1) * LANES]) for g in range(KVH)], axis=0)
+        keys = turn(part_of(flat, 0).astype(f32), cosine, -sine, KVH)
+        both = jnp.concatenate([jnp.concatenate(keys, axis=0).astype(bf16), part_of(flat, 1)], axis=0)
+        kv_out[...] += mul_nt(both, values)
+
+    near = key_steps(starts[0], own_block(), rows)
+    far = key_steps(far_starts[0], far_block(), rows)
+    pl.loop(*near)(add)
+
+    @pl.loop(*far)
+    def _(step):
+        pl.when((step < near[0]) | (step >= near[1]))(lambda: add(step))
+
+
+    @pl.when(pl.program_id(0) == pl.num_programs(0) - 1)
+    def _():
+        grad = side_by_side(grad_ref)
+        values = jnp.concatenate([own_normed[m, :width] for m in range(own_normed.shape[0])], axis=1)
+        normed_grad[...] = mul(weight[...], grad)
+        lane = lax.broadcasted_iota(jnp.int32, (width, LANES), 1)
+        gains = flip(jnp.where(lane == 0, gain_two_grad[...], 0.0))[:16]
+        base = 0
+        for array in (mul_nt(values, grad), kv_out[...], wo_grad[...], gains):
+            base = pack_rows(packed, base, array.astype(bf16))
+        packed[base:] = jnp.zeros((packed.shape[0] - base, LANES), bf16)
+        unit = kept.shape[1]
+        for dy in range(SIDE):
+            for target, dc in ((kept, 0), (away, 1)):
+                target[dy] = packed[pl.ds(pl.multiple_of(place_of(dc, dy, 1) * unit, 16), unit)]
+
+
+def weights_back(sums, normed, starts, far_starts, *others):
     micro, _, rows = starts.shape
-    width = v_out.shape[0]
-    cut = KVH * HD
-    per = KEYS // rows
-    k_out[...] = jnp.zeros_like(k_out)
-    v_out[...] = jnp.zeros_like(v_out)
-    for m in range(micro):
-
-        def add(step):
-            block = sums[pl.ds(step * per, per), m].reshape(KEYS, sums.shape[3])
-            inner = [normed[step * per + i, m] for i in range(per)]
-            values = jnp.concatenate([v[:width] for v in inner], axis=1)
-            tables = jnp.concatenate([v[width:] for v in inner], axis=1).astype(f32)
-            cosine = tables[:HALF] + tables[HALF : 2 * HALF]
-            sine = tables[2 * HALF : 3 * HALF] + tables[3 * HALF :]
-            flat = jnp.concatenate(
-                [jnp.transpose(block[:, :LANES]), jnp.transpose(block[:, LANES : 2 * LANES])[: cut - LANES]], axis=0
-            )
-            keys = jnp.concatenate(turn(flat.astype(f32), cosine, -sine, KVH), axis=0).astype(bf16)
-            k_out[...] += mul_nt(keys, values)
-            v_out[...] += mul(values, block[:, LANES:])
-
-        near = key_steps(starts[m], own_block(), rows)
-        far = key_steps(far_starts[m], far_block(), rows)
-        pl.loop(*near)(add)
-
-        @pl.loop(*far)
-        def _(step):
-            pl.when((step < near[0]) | (step >= near[1]))(lambda: add(step))
+    width = others[2].shape[0]
+    kv_width = sums.shape[3]
+    unit = tail_rows(width)
+    tail = shape_of((SIDE, unit, LANES), bf16)
+    outs = [shape_of((width, micro * rows), f32), tail, tail]
+
+    def whole(v):
+        return pl.BlockSpec(v.shape, lambda m: (0,) * len(v.shape))
+
+    return pl.pallas_call(
+        weights_kernel,
+        grid=(micro,),
+        in_specs=[one_of(sums.shape, 1), one_of(normed.shape, 1), one_of(starts.shape), one_of(starts.shape)]
+        + [whole(v) for v in others],
+        out_specs=[whole(v) for v in outs],
+        out_shape=outs,
+        scratch_shapes=[
+            pltpu.VMEM((kv_width, width), f32),
+            pltpu.VMEM((2 * SIDE * unit, LANES), bf16),
+        ],
+        compiler_params=params(),
+        cost_estimate=cost(3),
+        name="weights_back",
+    )(sums, normed, starts, far_starts, *others)
 
 
 def norm_back(vector, scale, gain, gradient):
@@ -369,8 +419,8 @@
     micro, width, rows = tokens.shape
     if last:
         before, result_before, grad_before, received = refs[:4]
-        result, main0, main1, middle_grad, d1, gain_grad, wo_grad = refs[4:11]
-        normed, normed_t, grad, grad_t, result_sum, normed_grad = refs[11:]
+        result, main, middle_grad, d1, gain_grad, wo_grad = refs[4:10]
+        normed, normed_t, grad, grad_t, result_sum, normed_grad = refs[10:]
         middle = before
     else:
         main, middle, result_sum, normed_grad = refs[:4]
@@ -413,10 +463,7 @@
             value = part[:, span].astype(bf16)
             if last:
                 value = (value.astype(f32) + received[rows_at].astype(f32)).astype(bf16)
-                for index, target in enumerate((main0, main1)):
-                    pl.when(step == index)(functools.partial(target.__setitem__, rows_at, value))
-            else:
-                main[rows_at] = value
+            main[rows_at] = value
     normed_grad[...] += mul_nt(gate_grad, wg[...]) + mul_nt(up_grad, wu[...])
     if not last:
         return
@@ -450,8 +497,8 @@
     return base
 
 
-def main_rows(width):
-    used = CHUNK // LANES * 3 * width
+def main_rows(width, hidden):
+    used = hidden // 2 // LANES * 3 * width
     unit = SIDE * SIDE * SIDE * 8
     return -(-used // unit) * unit
 
@@ -462,7 +509,6 @@
     hidden = wg.shape[1]
     steps = hidden // 2 // CHUNK
     block = pl.BlockSpec((CHUNK // LANES * 3 * width, LANES), lambda i, c: (i, 0))
-    first_block = pl.BlockSpec((CHUNK // LANES * 3 * width, LANES), lambda i, c: (0, 0))
     last = len(before) > 0
 
     def whole(*dims):
@@ -479,8 +525,7 @@
     if last:
         outs = [
             (token_shape, token_spec),
-            (shape_of((main_rows(width), LANES), bf16), first_block),
-            (shape_of((main_rows(width), LANES), bf16), first_block),
+            (shape_of((main_rows(width, hidden), LANES), bf16), block),
             (flat, spec),
             (token_shape, token_spec),
             (shape_of((width, 1), f32), whole(width, 1)),
@@ -523,30 +568,11 @@
     )(core, first, tokens, out_weight, gain, out_grad, wg, wu, wd, *before)
 
 
-def query_back_kernel(
-    normed, grad_ref, weight, wk_grad, wv_grad, wo_grad, gain_two_grad, normed_grad, kept, away, packed
-):
-    grad = side_by_side(grad_ref)
-    width = weight.shape[0]
-    values = jnp.concatenate([normed[m, :width] for m in range(normed.shape[0])], axis=1)
-    normed_grad[...] = mul(weight[...], grad)
-    lane = lax.broadcasted_iota(jnp.int32, (width, LANES), 1)
-    gains = flip(jnp.where(lane == 0, gain_two_grad[...], 0.0))[:16]
-    base = 0
-    for array in (mul_nt(values, grad), wk_grad[...], wv_grad[...], wo_grad[...], gains):
-        base = pack_rows(packed, base, array.astype(bf16))
-    packed[base:] = jnp.zeros((packed.shape[0] - base, LANES), bf16)
-    unit = kept.shape[1]
-    for dy in range(SIDE):
-        for target, dc in ((kept, 0), (away, 1)):
-            target[dy] = packed[pl.ds(pl.multiple_of(place_of(dc, dy, 1) * unit, 16), unit)]
-
-
 def tail_rows(width):
     tiles = -(-width // LANES)
-    used = tiles * (2 * width + KVH * HD + 16) + (2 * KVH * HD // LANES - 1) * width
+    used = tiles * (2 * width + 2 * KVH * HD + 16)
     unit = 2 * SIDE * SIDE * SIDE * 8
-    return -(-used // unit) * (unit // 2)
+    return -(-used // unit) * (unit // 2 // SIDE)
 
 
 def place_of(dc, dy, sign):
@@ -563,9 +589,8 @@
     flat = jnp.concatenate(
         [flip(kv_grad[m * rows : (m + 1) * rows].astype(f32)) for m in range(micro)], axis=1
     )
-    cut = KVH * HD
-    parts = turn(flat[:cut], cos_ref[...], -sin_ref[...], KVH)
-    low = jnp.concatenate(parts + [flat[cut:]], axis=0).astype(bf16)
+    parts = turn(part_of(flat, 0), cos_ref[...], -sin_ref[...], KVH)
+    low = jnp.concatenate(parts + [part_of(flat, 1)], axis=0).astype(bf16)
     weights = flip(jnp.concatenate([wk[...], wv[...]], axis=0))
     normed_grad = partial[...] + mul(weights, low)
     inputs = side_by_side(tokens).astype(f32)
@@ -577,10 +602,12 @@
 
 
 def unpack_tail_kernel(kept, away, wq, wk, wv, gain, q_out, k_out, v_out, o_out, gain_one, gain_two, held):
-    unit = kept.shape[1]
+    places, _, rows, _ = kept.shape
     for dy in range(SIDE):
         for source, dc in ((kept, 0), (away, 1)):
-            held[pl.ds(pl.multiple_of(place_of(dc, dy, -1) * unit, 16), unit)] = source[dy]
+            base = place_of(dc, dy, -1) * places * rows
+            for i in range(places):
+                held[pl.ds(pl.multiple_of(base + i * rows, 16), rows)] = source[i, dy]
     width = q_out.shape[0]
     cut = k_out.shape[0]
     base = 0
@@ -593,8 +620,8 @@
         return jnp.concatenate(parts, axis=1)[:, :cols].astype(f32)
 
     query = section(width, width)
-    key = section(cut, width)
-    value = flip(section(width, 2 * cut - LANES))[cut - LANES :]
+    both = section(2 * cut, width)
+    key, value = both[:cut], both[cut:]
     q_out[...] = query
     k_out[...] = key
     v_out[...] = value
@@ -609,24 +636,21 @@
 
 
 def unpack_main_kernel(other, *refs):
-    pieces = refs[:SIDE]
+    pieces = refs[: SIDE + 1]
     gate, up, down, held, wide, sems = refs[-6:]
     unit = pieces[0].shape[0]
-    part = unit // 2
-    for k in range(SIDE):
+    half = unit // 2
+    for k, offset, piece in zip((0, 1, 2, 2, 3), (0, 0, 0, half, 0), pieces):
         place = lax.rem(lax.axis_index("y") - k + SIDE, SIDE)
-        for index in range(2):
-            span = pl.ds(pl.multiple_of(place * part, 16), part)
-            held[index, span] = pieces[k][index * part : (index + 1) * part]
+        held[pl.ds(pl.multiple_of(place * unit + offset, 16), piece.shape[0])] = piece[...]
     core = lax.axis_index("core")
     core = 1 - core if other else core
     width, cols = wide.shape[1:]
     copies = []
     for k, target in enumerate((gate, up, down)):
         for t in range(cols // LANES):
-            per = CHUNK // LANES
-            base = (t % per * 3 + k) * width
-            wide[k, :, t * LANES : (t + 1) * LANES] = held[t // per, base : base + width].astype(f32)
+            base = (t * 3 + k) * width
+            wide[k, :, t * LANES : (t + 1) * LANES] = held[base : base + width].astype(f32)
         span = pl.ds(pl.multiple_of(core * cols, LANES), cols)
         copies.append(pltpu.make_async_copy(wide.at[k], target.at[:, span], sems.at[k]))
         copies[-1].start()
@@ -639,15 +663,15 @@
     outs = [shape_of((width, hidden), f32)] * 3
     return pl.pallas_call(
         functools.partial(unpack_main_kernel, filled is not None),
-        in_specs=[VMEM] * SIDE + ([ANY] * 3 if filled else []),
+        in_specs=[VMEM] * len(pieces) + ([ANY] * 3 if filled else []),
         out_specs=[ANY] * 3,
         out_shape=outs,
         scratch_shapes=[
-            pltpu.VMEM((2, SIDE * unit // 2, LANES), bf16),
+            pltpu.VMEM((SIDE * unit, LANES), bf16),
             pltpu.VMEM((3, width, hidden // 2), f32),
             pltpu.SemaphoreType.DMA((3,)),
         ],
-        input_output_aliases={SIDE + i: i for i in range(3)} if filled else {},
+        input_output_aliases={len(pieces) + i: i for i in range(3)} if filled else {},
         compiler_params=params(),
         cost_estimate=cost(1.5),
         name="unpack_main",
@@ -751,20 +775,17 @@
         (normed, query_weight, cosine, sine),
         "query",
     )
-    kv, q1, second_query, second_grad, gathered = lax.optimization_barrier(
-        (kv, q1, second_query, second_grad, normed)
-    )
+    far_query, far_grad = mirror(second_query), mirror(second_grad)
+    kv, q1, far_query, far_grad, gathered = lax.optimization_barrier((kv, q1, far_query, far_grad, normed))
     gathered = lax.all_gather(gathered, SEQ, axis=0)
-    far_query, far_grad = mirror(second_query), mirror(second_grad)
     first_low, first_flat, first_lse = attend_forward(False, kv, q1, starts)
-    first_low, far_query = lax.optimization_barrier((first_low, far_query))
     ffn_args = (first_low, tokens, output_weight, gain_two, out_grad, gate_weight, up_weight, wd)
     away, *before = feed_forward(core, *ffn_args, ())
     far_query = after(far_query, away)
     _, second_flat, second_lse = attend_forward(True, kv, far_query, far_starts)
     received, second_lse = lax.optimization_barrier((shift(away, "core", 1), second_lse))
-    result, main0, main1, middle_grad, d1, gain_two_grad, wo_grad = feed_forward(core, *ffn_args, (*before, received))
-    main0 = scatter_parts(main0, "y")
+    result, main, middle_grad, d1, gain_two_grad, wo_grad = feed_forward(core, *ffn_args, (*before, received))
+    main = scatter_parts(main, "y")
     kv_grad, query_grad, second_query_grad = attend_backward(
         kv,
         q1,
@@ -780,46 +801,20 @@
         cosine,
         sine,
     )
-    kv_grad, gathered = lax.optimization_barrier((kv_grad, gathered))
-    wk_grad, wv_grad = simple(
-        kv_weights_kernel,
-        [VMEM] * 4,
-        [shape_of((kwidth, width), f32), shape_of((width, 2 * kwidth - LANES), f32)],
-        (after(kv_grad, main0), gathered, starts, far_starts),
-        "kv_weights",
-    )
-    main1 = scatter_parts(after(main1, main0), "y")
+    second_query_grad = mirror(second_query_grad)
+    kv_grad, gathered, main, second_query_grad = lax.optimization_barrier((kv_grad, gathered, main, second_query_grad))
+    main = scatter_parts(sum_parts(main), SEQ)
+    normed_part, tail, tail_away = weights_back(
+        kv_grad, gathered, starts, far_starts, normed, query_grad, query_weight, wo_grad, gain_two_grad
+    )
     kv_grad = lax.psum_scatter(kv_grad.reshape(-1, 2 * kwidth), SEQ, scatter_dimension=0, tiled=True)
-    half = tail_rows(width)
-    tail_half = shape_of((SIDE, half // SIDE, LANES), bf16)
-    normed_part, tail, tail_away = pl.pallas_call(
-        query_back_kernel,
-        in_specs=[VMEM] * 7,
-        out_specs=[VMEM] * 3,
-        out_shape=[shape_of((width, total), f32), tail_half, tail_half],
-        scratch_shapes=[pltpu.VMEM((2 * half, LANES), bf16)],
-        compiler_params=params(),
-        cost_estimate=cost(1),
-        name="query_back",
-    )(normed, query_grad, query_weight, wk_grad, wv_grad, wo_grad, gain_two_grad)
-    second_query_grad = mirror(second_query_grad)
-    main1 = after(main1, normed_part)
-    main = jnp.concatenate([sum_parts(main0), sum_parts(main1)], axis=0)
-    main = scatter_parts(main, SEQ)
+    tail_away, main = lax.optimization_barrier((tail_away, main))
     tail = (tail.astype(f32) + shift(tail_away, "core", 1).astype(f32)).astype(bf16)
+    main = gather_all(sum_parts(main), SEQ)
     tail = exchange([tail[k] for k in range(SIDE)], "y").astype(bf16)
     tail, main = lax.optimization_barrier((tail, main))
-    main = gather_all(sum_parts(main), SEQ)
-    main = collect(main, "y")
-    tail = gather_all(scatter_sum(tail, SEQ), SEQ)
-    tail, main = lax.optimization_barrier((tail, main))
-    hidden = gate_weight.shape[1]
-    main_away = [shift(v, "core", 1) for v in main]
-    filled = unpack_main(main, width, hidden, None)
-    tail, filled = lax.optimization_barrier((collect(tail, "y"), filled))
-    tail = jnp.stack(tail)
-    tail_away = shift(tail, "core", 1)
-    gate, up, down = unpack_main(main_away, width, hidden, filled)
+    middle = main.shape[0] // 2
+    ahead, behind = shift(main, "y", 1), shift(main, "y", -1)
     tokens_like = shape_of((micro, width, rows), bf16)
     input_grad, second_query_grad = simple(
         input_back_kernel,
@@ -828,6 +823,22 @@
         (kv_grad, wk, wv, cosine, sine, normed_part, tokens, gain_one, middle_grad, second_query_grad),
         "input_back",
     )
+    tail = scatter_sum(tail, SEQ)
+    tail, ahead, behind = lax.optimization_barrier((tail, ahead, behind))
+    tail = jnp.stack(collect(tail, "y"))
+    places = SIDE * SIDE
+    upper, lower = shift(ahead[:middle], "y", 1), shift(behind[middle:], "y", -1)
+    tail, upper, lower = lax.optimization_barrier((tail, upper, lower))
+    tail = lax.all_to_all(jnp.broadcast_to(tail[None], (places,) + tail.shape), SEQ, 0, 0)
+    main = [main, ahead, upper, lower, behind]
+    hidden = gate_weight.shape[1]
+    main_away = [shift(v, "core", 1) for v in main]
+    filled = unpack_main(main, width, hidden, None)
+    gate, up, down = unpack_main(main_away, width, hidden, filled)
+    tail, gate, up, down, input_grad, second_query_grad = lax.optimization_barrier(
+        (tail, gate, up, down, input_grad, second_query_grad)
+    )
+    tail_away = shift(tail, "core", 1)
     square = shape_of((width, width), f32)
     narrow = shape_of((kwidth, width), f32)
     line = shape_of((width,), f32)
@@ -836,7 +847,7 @@
         in_specs=[VMEM] * 6,
         out_specs=[VMEM] * 6,
         out_shape=[square, narrow, narrow, square, line, line],
-        scratch_shapes=[pltpu.VMEM((2 * half, LANES), bf16)],
+        scratch_shapes=[pltpu.VMEM((2 * math.prod(tail.shape[:3]), LANES), bf16)],
         compiler_params=params(),
         cost_estimate=cost(1),
         name="unpack_tail",

time: 284 us -> 253 us (0.89)
  blocking collectives: 39.3 us -> 13.6 us
  starting transfers between devices: 37.3 us -> 51 us
  waiting for transfers between devices: 91 us -> 77.5 us
  Pallas kernels: 89.9 us -> 85.8 us
    all_to_all x2 -> x0, blocking collectives: 28.1 us -> none  [gather_all(): return lax.all_to_all(spread, axis, 0, 0).reshape(places * rows, lanes)]
    ppermute x3, waiting for transfers between devices: 3.01 us -> 20.1 us  [mirror(): return lax.ppermute(value, SEQ, [(i, size - 1 - i) for i in range(size)])]
    ppermute x16 -> x18, waiting for transfers between devices: 35.7 us -> 19.5 us  [shift(): lax.ppermute(value, axis, [(i, (i + distance) % size) for i in range(size)])]
    all_gather x1, waiting for transfers between devices: 48.7 us -> 32.7 us  [per_device(): kv = lax.all_gather(kv, SEQ, axis=0)]
    all_to_all x0 -> x2, starting transfers between devices: none -> 9.96 us  [the longest x1 6.36 us: per_device(): lax.all_to_all(jnp.broadcast_to(tail[None], (places,) + tail.shape), SEQ,...]
    pallas_call x4 -> x3, Pallas kernels: 16.7 us -> 8.06 us  [simple(): pl.pallas_call(kernel, in_specs=in_specs, out_specs=[VMEM] * len(outs), o...]
    ppermute x16 -> x18, starting transfers between devices: 12.8 us -> 21.2 us  [shift(): lax.ppermute(value, axis, [(i, (i + distance) % size) for i in range(size)])]
    all_to_all x3 -> x2, starting transfers between devices: 15.6 us -> 9.94 us  [scatter_parts(): lax.all_to_all(held.reshape(places, rows // places, lanes), axis, 0, 0)]
  transfers between devices with their start and end apart: 25 -> 28, of which waited for: 11 -> 12; matrix products, arithmetic and copies ran while one was open for 2% -> 2% of each run, Pallas kernels for 30% -> 31%
where the time goes in v1:
time: 253 us
  Pallas kernels  85.8 us (34%)
  waiting for transfers between devices  77.5 us (31%)
  starting transfers between devices  51 us (20%)
  between operations  14.1 us (6%)
  blocking collectives  13.6 us (5%)
  local copies, waits for them, and re-layouts  8.57 us (3%)
    all_gather x1, waiting for transfers between devices, per_device(): kv = lax.all_gather(kv, SEQ, axis=0)  32.7 us
    ppermute x18, starting transfers between devices, shift(): lax.ppermute(value, axis, [(i, (i + distance) % size) for i in range(size)])  21.2 us
    ppermute x3, waiting for transfers between devices, mirror(): return lax.ppermute(value, SEQ, [(i, size - 1 - i) for i in range(size)])  20.1 us
    pallas_call x1, Pallas kernels, attend_backward(): pl.pallas_call(backward_kernel, grid=(micro,), in_specs=[one_of(kv.shape,...  19.8 us
    ppermute x18, waiting for transfers between devices, shift(): lax.ppermute(value, axis, [(i, (i + distance) % size) for i in range(size)])  19.5 us
    pallas_call x2, Pallas kernels, feed_forward(): pl.pallas_call(functools.partial(ffn_kernel, last), grid_spec=pltpu.Prefe...  18.6 us
    pallas_call x2, Pallas kernels, attend_forward(): pl.pallas_call(functools.partial(forward_kernel, far), grid=(micro,), in_...  16.1 us
    all_to_all x1, blocking collectives, scatter_parts(): lax.all_to_all(held.reshape(places, rows // places, lanes), axis, 0, 0)  13.6 us
  transfers between devices with their start and end apart: 28, of which 12 were waited for; matrix products, arithmetic and copies ran while one was open for 2% of the time, Pallas kernels for 31%

profile of v1, /device:TPU:1, one launch (start us, length us, event | category | flops | bytes accessed | tf_op | source)
XLA Modules:
  0.0 252.5 jit_solution(16678217785167412548)
XLA Ops:
  8.8 2.6 %prepare.1 = (bf16[2,704,128]{2,1,0:T(8,128)(2,1)}, bf16[2,128,384]{2,1,0:T(8,128)(2,1)}, f32[32,256]{1,0:T(8,128)}, f32[32,256]{1,0:T(8,128)}, s32[2,1,128]{2,1,0:T(1,128)}, /*index=5*/s32[2,1,128]{2,1,0:T(1,128)}) custom-call(s32[2,16]{1,0:T(2,128)} %lengths.1, bf16[2,576,128]{2,1,0:T(8,128)(2,1)} %bitcast.49, bf16[576,1]{1,0:T(8,128)(2,1)} %reshape.63.gain, ...), custom_call_target="tpu_custom_call" | custom-call | flops 1000000000 | bytes 1000 | tf_op jit(solution)/shard_map/prepare/pallas_call | solution.py:104
  11.4 6.9 %collective-permute-start = (bf16[2,576,128]{2,1,0:T(8,128)(2,1)S(1)}, bf16[2,576,128]{2,1,0:T(8,128)(2,1)S(1)}, u32[]{:S(2)}, u32[]{:S(2)}) collective-permute-start(bf16[2,576,128]{2,1,0:T(8,128)(2,1)S(1)} %bitcast.60), channel_id=1, source_target_pairs={{0,120},{8,112},{16,104},{24,96},{32,88},{40,80},{48,72},{56,64},{... | collective-permute-start | bytes 884744 | tf_op jit(solution)/shard_map/ppermute | solution.py:688
  18.4 2.4 query.1.query_ref.q1_ref
  20.8 4.2 %collective-permute-done.query_ref.q2_ref = bf16[2,576,128]{2,1,0:T(8,128)(2,1)S(1)} collective-permute-done((bf16[2,576,128]{2,1,0:T(8,128)(2,1)S(1)}, bf16[2,576,128]{2,1,0:T(8,128)(2,1)S(1)}, u32[]{:S(2)}, u32[]{:S(2)}) %collective-permute-start) | collective-permute-done | bytes 294944 | tf_op jit(solution)/shard_map/ppermute | solution.py:688
  25.0 6.6 %collective-permute-done.1.d2_ref = bf16[2,576,128]{2,1,0:T(8,128)(2,1)S(1)} collective-permute-done((bf16[2,576,128]{2,1,0:T(8,128)(2,1)S(1)}, bf16[2,576,128]{2,1,0:T(8,128)(2,1)S(1)}, u32[]{:S(2)}, u32[]{:S(2)}) %collective-permute-start.1) | collective-permute-done | bytes 294944 | tf_op jit(solution)/shard_map/ppermute | solution.py:688
  31.6 32.7 %all-gather.5.cloned.1.call-done = bf16[32,128,384]{2,1,0:T(8,128)(2,1)} async-done(((bf16[2,128,384]{2,1,0:T(8,128)(2,1)}), bf16[32,128,384]{2,1,0:T(8,128)(2,1)}) %all-gather.5.cloned.1.call-update) | async-done | bytes 3145744 | tf_op jit(solution)/shard_map/all_gather | solution.py:770
  65.2 4.7 %attention_forward.2 = (bf16[2,576,128]{2,1,0:T(8,128)(2,1)}, f32[2,576,128]{2,1,0:T(8,128)}, f32[2,3,1,384]{3,2,1,0:T(1,128)}) custom-call(bf16[16,2,128,384]{3,2,1,0:T(8,128)(2,1)} %bitcast.57, bf16[2,576,128]{2,1,0:T(8,128)(2,1)} %query.1.query_ref.q1_ref, s32[2,1,128]{2,1,0:T(1,128)} %get-tuple-element.87.starts), custom_call_target="tpu_custom_call" | custom-call | flops 2500000000 | bytes 1000 | tf_op jit(solution)/shard_map/attention_forward/pallas_call | solution.py:236
  69.9 8.2 %feed_forward.2 = (bf16[10368,128]{1,0:T(8,128)(2,1)}, f32[576,256]{1,0:T(8,128)}, f32[256,576]{1,0:T(8,128)}, f32[256,576]{1,0:T(8,128)}) custom-call(s32[1]{0:T(128)} %bitcast.core, bf16[2,576,128]{2,1,0:T(8,128)(2,1)} %get-tuple-element.88.first, bf16[2,576,128]{2,1,0:T(8,128)(2,1)} %bitcast.50, bf16[576,576]{1,0:T(8,128)(2,1)} %out_weight.3, ...), custom_call_target="tpu_custom_call" | custom-call | flops 3000000000 | bytes 1000 | tf_op jit(solution)/shard_map/feed_forward/pallas_call | solution.py:545
  79.1 11.5 %attention_forward.3 = (bf16[2,576,128]{2,1,0:T(8,128)(2,1)}, f32[2,576,128]{2,1,0:T(8,128)}, f32[2,3,1,384]{3,2,1,0:T(1,128)}) custom-call(bf16[16,2,128,384]{3,2,1,0:T(8,128)(2,1)} %bitcast.58, bf16[2,576,128]{2,1,0:T(8,128)(2,1)} %copy-done.16, s32[2,1,128]{2,1,0:T(1,128)} %get-tuple-element.95.starts.far_starts), custom_call_target="tpu_custom_call" | custom-call | flops 2500000000 | bytes 1000 | tf_op jit(solution)/shard_map/attention_forward/pallas_call | solution.py:236
  92.1 10.4 %feed_forward.3 = (bf16[2,576,128]{2,1,0:T(8,128)(2,1)}, bf16[10752,128]{1,0:T(8,128)(2,1)}, f32[576,256]{1,0:T(8,128)}, bf16[2,576,128]{2,1,0:T(8,128)(2,1)}, f...) custom-call(s32[1]{0:T(128)} %bitcast.core, bf16[2,576,128]{2,1,0:T(8,128)(2,1)} %get-tuple-element.88.first, ...), custom_call_target="tpu_custom_call" | custom-call | flops 3000000000 | bytes 1000 | tf_op jit(solution)/shard_map/feed_forward/pallas_call | solution.py:545
  102.5 4.0 %all-to-all-start = ((bf16[4,2688,128]{2,1,0:T(8,128)(2,1)}), bf16[4,2688,128]{2,1,0:T(8,128)(2,1)S(1)}, u32[]{:S(2)}, u32[]{:S(2)}) async-start(bf16[4,2688,128]{2,1,0:T(8,128)(2,1)} %bitcast.39), calls=%async_computation | async-start | bytes 5505024 | tf_op jit(solution)/shard_map/all_to_all | solution.py:705
  106.5 19.8 %attention_backward.1 = (bf16[16,2,128,384]{3,2,1,0:T(8,128)(2,1)}, bf16[2,576,128]{2,1,0:T(8,128)(2,1)}, bf16[2,576,128]{2,1,0:T(8,128)(2,1)}) custom-call(bf16[16,2,128,384]{3,2,1,0:T(8,128)(2,1)} %bitcast.59, bf16[2,576,128]{2,1,0:T(8,128)(2,1)} %query.1.query_ref.q1_ref, bf16[2,576,128]{2,1,0:T(8,128)(2,1)} %copy-done.16, ...), custom_call_target="tpu_custom_call" | custom-call | flops 7000000000 | bytes 1000 | tf_op jit(solution)/shard_map/attention_backward/pallas_call | solution.py:311
  126.3 2.9 %collective-permute-start.3 = (bf16[2,576,128]{2,1,0:T(8,128)(2,1)}, bf16[2,576,128]{2,1,0:T(8,128)(2,1)}, u32[]{:S(2)}, u32[]{:S(2)}) collective-permute-start(bf16[2,576,128]{2,1,0:T(8,128)(2,1)} %get-tuple-element.108), channel_id=1, source_target_pairs={{0,120},{8,112},{16,104},{24,96},{32,88},{40,80},{48,72},{56,64},{... | collective-permute-start | bytes 884744 | tf_op jit(solution)/shard_map/ppermute | solution.py:688
  129.2 9.2 %collective-permute-done.3.second = bf16[2,576,128]{2,1,0:T(8,128)(2,1)} collective-permute-done((bf16[2,576,128]{2,1,0:T(8,128)(2,1)}, bf16[2,576,128]{2,1,0:T(8,128)(2,1)}, u32[]{:S(2)}, u32[]{:S(2)}) %collective-permute-start.3) | collective-permute-done | bytes 294944 | tf_op jit(solution)/shard_map/ppermute | solution.py:688
  141.2 5.9 %all-to-all-start.1 = ((bf16[16,168,128]{2,1,0:T(8,128)(2,1)}), bf16[16,168,128]{2,1,0:T(8,128)(2,1)S(1)}, u32[]{:S(2)}, u32[]{:S(2)}) async-start(bf16[16,168,128]{2,1,0:T(8,128)(2,1)} %bitcast.12), calls=%async_computation.1 | async-start | bytes 1376256 | tf_op jit(solution)/shard_map/all_to_all | solution.py:705
  147.1 9.7 %weights_back.1 = (f32[576,256]{1,0:T(8,128)}, bf16[4,1024,128]{2,1,0:T(8,128)(2,1)}, bf16[4,1024,128]{2,1,0:T(8,128)(2,1)}) custom-call(bf16[16,2,128,384]{3,2,1,0:T(8,128)(2,1)} %get-tuple-element.109.sums, bf16[16,2,704,128]{3,2,1,0:T(8,128)(2,1)} %bitcast.37, s32[2,1,128]{2,1,0:T(1,128)} %get-tuple-element.87.starts, ...), custom_call_target="tpu_custom_call" | custom-call | flops 3000000000 | bytes 1000 | tf_op jit(solution)/shard_map/weights_back/pallas_call | solution.py:391
  156.8 3.9 %all-to-all-done.1 = bf16[16,168,128]{2,1,0:T(8,128)(2,1)S(1)} async-done(((bf16[16,168,128]{2,1,0:T(8,128)(2,1)}), bf16[16,168,128]{2,1,0:T(8,128)(2,1)S(1)}, u32[]{:S(2)}, u32[]{:S(2)}) %all-to-all-start.1) | async-done | bytes 688160 | tf_op jit(solution)/shard_map/all_to_all | solution.py:705
  160.7 2.5 %collective-permute-start.4 = (bf16[4,1024,128]{2,1,0:T(8,128)(2,1)}, bf16[4,1024,128]{2,1,0:T(8,128)(2,1)S(1)}, u32[]{:S(2)}, u32[]{:S(2)}) collective-permute-start(bf16[4,1024,128]{2,1,0:T(8,128)(2,1)} %get-tuple-element.117), channel_id=1, source_target_pairs={{0,1},{1,0},{2,3},{3,2},{4,5},{5,4},{6,7},{7,6},{8,9},{9,8},{10,11... | collective-permute-start | bytes 3145736 | tf_op jit(solution)/shard_map/ppermute | solution.py:683
  164.2 3.6 %all-to-all-start.2 = ((bf16[16,168,128]{2,1,0:T(8,128)(2,1)}), bf16[16,168,128]{2,1,0:T(8,128)(2,1)S(1)}, u32[]{:S(2)}, u32[]{:S(2)}) async-start(bf16[16,168,128]{2,1,0:T(8,128)(2,1)} %broadcast_in_dim.4), calls=%async_computation.2 | async-start | bytes 1376256 | tf_op jit(solution)/shard_map/all_to_all | solution.py:720
  169.6 2.4 collective-permute-start.6
  172.1 5.4 %collective-permute-done.5 = bf16[1024,128]{1,0:T(8,128)(2,1)S(1)} collective-permute-done((bf16[1024,128]{1,0:T(8,128)(2,1)S(1)}, bf16[1024,128]{1,0:T(8,128)(2,1)S(1)}, u32[]{:S(2)}, u32[]{:S(2)}) %collective-permute-start.5) | collective-permute-done | bytes 262176 | tf_op jit(solution)/shard_map/ppermute | solution.py:683
  177.5 6.5 %collective-permute-done.6 = bf16[1024,128]{1,0:T(8,128)(2,1)S(1)} collective-permute-done((bf16[1024,128]{1,0:T(8,128)(2,1)S(1)}, bf16[1024,128]{1,0:T(8,128)(2,1)S(1)}, u32[]{:S(2)}, u32[]{:S(2)}) %collective-permute-start.6) | collective-permute-done | bytes 262176 | tf_op jit(solution)/shard_map/ppermute | solution.py:683
  187.0 13.6 %all_to_all.25 = bf16[16,64,128]{2,1,0:T(8,128)(2,1)S(1)} all-to-all(bf16[16,64,128]{2,1,0:T(8,128)(2,1)S(1)} %bitcast.42), channel_id=1, replica_groups=mesh['z'=4,'x'=4,'y'=4,'core'=2] {'z','x'}, dimensions={0} | all-to-all | bytes 524288 | tf_op jit(solution)/shard_map/all_to_all | solution.py:705
  204.6 2.3 collective-permute-start.11
  207.7 2.9 %collective-permute-done.10 = bf16[64,128]{1,0:T(8,128)(2,1)S(1)} collective-permute-done((bf16[64,128]{1,0:T(8,128)(2,1)S(1)}, bf16[64,128]{1,0:T(8,128)(2,1)S(1)}, u32[]{:S(2)}, u32[]{:S(2)}) %collective-permute-start.10) | collective-permute-done | bytes 16416 | tf_op jit(solution)/shard_map/ppermute | solution.py:683
  213.1 6.4 %all-to-all-start.4 = ((bf16[16,4,64,128]{3,2,1,0:T(8,128)(2,1)}), bf16[16,4,64,128]{3,2,1,0:T(8,128)(2,1)S(1)}, u32[]{:S(2)}, u32[]{:S(2)}) async-start(bf16[16,4,64,128]{3,2,1,0:T(8,128)(2,1)} %broadcast_in_dim.5), calls=%async_computation.4 | async-start | bytes 2097152 | tf_op jit(solution)/shard_map/all_to_all | solution.py:832
  219.5 3.2 %collective-permute-start.15 = (bf16[2688,128]{1,0:T(8,128)(2,1)S(1)}, bf16[2688,128]{1,0:T(8,128)(2,1)S(1)}, u32[]{:S(2)}, u32[]{:S(2)}) collective-permute-start(bf16[2688,128]{1,0:T(8,128)(2,1)S(1)} %bitcast.45), channel_id=1, source_target_pairs={{0,1},{1,0},{2,3},{3,2},{4,5},{5,4},{6,7},{7,6},{8,9},{9,8},{10,11... | collective-permute-start | bytes 2064392 | tf_op jit(solution)/shard_map/ppermute | solution.py:683
  223.7 4.4 %unpack_main.2 = (f32[576,1536]{1,0:T(8,128)}, f32[576,1536]{1,0:T(8,128)}, f32[576,1536]{1,0:T(8,128)}) custom-call(bf16[2688,128]{1,0:T(8,128)(2,1)} %bitcast.46, bf16[2688,128]{1,0:T(8,128)(2,1)} %copy-done.9, bf16[1344,128]{1,0:T(8,128)(2,1)} %copy-done.13, bf16[1344,128]{1,0:T(8,128)(2,1)} %collective-permute-done.14.refs_3_, bf16[2688,128]{1,0:T(8,128)(2,1)} %copy-done.10), custom_call_target="tpu_custom_call" | custom-call | flops 1500000000 | bytes 1000 | tf_op jit(solution)/shard_map/unpack_main/pallas_call | solution.py:664
  229.7 4.4 %unpack_main.3 = (f32[576,1536]{1,0:T(8,128)}, f32[576,1536]{1,0:T(8,128)}, f32[576,1536]{1,0:T(8,128)}) custom-call(bf16[2688,128]{1,0:T(8,128)(2,1)} %copy-done.4, bf16[2688,128]{1,0:T(8,128)(2,1)} %copy-done.5, bf16[1344,128]{1,0:T(8,128)(2,1)} %copy-done.7, ...), custom_call_target="tpu_custom_call", output_to_operand_aliasing={{0}: (5, {}), {1}: (6, {}), {2}: (7, {})} | custom-call | flops 1500000000 | bytes 1000 | tf_op jit(solution)/shard_map/unpack_main/pallas_call | solution.py:664
  234.1 3.1 %input_back.1 = (bf16[2,576,128]{2,1,0:T(8,128)(2,1)}, bf16[2,576,128]{2,1,0:T(8,128)(2,1)}) custom-call(bf16[256,384]{1,0:T(8,128)(2,1)} %reduce-scatter.2.cloned.1.call-done.kv_grad, bf16[192,576]{1,0:T(8,128)(2,1)} %bitcast.64, bf16[192,576]{1,0:T(8,128)(2,1)} %bitcast.67, f32[32,256]{1,0:T(8,128)} %get-tuple-element.83.cos_ref, ...), custom_call_target="tpu_custom_call" | custom-call | flops 1000000000 | bytes 1000 | tf_op jit(solution)/shard_map/input_back/pallas_call | solution.py:104
  238.1 2.3 collective-permute-done.20.away
  241.4 4.6 %unpack_tail.1 = (f32[576,576]{1,0:T(8,128)}, f32[192,576]{1,0:T(8,128)}, f32[192,576]{1,0:T(8,128)}, f32[576,576]{1,0:T(8,128)}, f32[576]{0:T(1024)}, /*index=5*/f32[576]{0:T(1024)}) custom-call(bf16[16,4,64,128]{3,2,1,0:T(8,128)(2,1)} %copy-done.2, bf16[16,4,64,128]{3,2,1,0:T(8,128)(2,1)} %copy-done.12, bf16[576,576]{1,0:T(8,128)(2,1)} %wq.1, ...), custom_call_target="tpu_custom_call" | custom-call | flops 1000000000 | bytes 1000 | tf_op jit(solution)/shard_map/unpack_tail/pallas_call | solution.py:845
  (89 shorter events, 25.2 us)
Async XLA Ops:
  7.2 57.2 %all-gather.5.cloned.1.call-start = ((), (), s32[]{:S(2)}) async-start(), calls=%async_computation.7 | async-start | bytes 3342336 | tf_op jit(solution)/shard_map/all_gather | solution.py:770
  11.4 53.0 %copy-start.11 = (bf16[576]{0:T(1024)(128)(2,1)S(1)}, bf16[576]{0:T(1024)(128)(2,1)}, u32[]{:S(2)}) copy-start(bf16[576]{0:T(1024)(128)(2,1)} %param.24) | copy-start | bytes 3460
  11.4 128.3 %all-gather.7.cloned.1.call-start = ((), (), s32[]{:S(2)}) async-start(), calls=%async_computation.8 | async-start | bytes 6127616 | tf_op jit(solution)/shard_map/all_gather | solution.py:780
  11.4 13.6 %collective-permute-start = (bf16[2,576,128]{2,1,0:T(8,128)(2,1)S(1)}, bf16[2,576,128]{2,1,0:T(8,128)(2,1)S(1)}, u32[]{:S(2)}, u32[]{:S(2)}) collective-permute-start(bf16[2,576,128]{2,1,0:T(8,128)(2,1)S(1)} %bitcast.60), channel_id=1, source_target_pairs={{0,120},{8,112},{16,104},{24,96},{32,88},{40,80},{48,72},{56,64},{... | collective-permute-start | bytes 884744 | tf_op jit(solution)/shard_map/ppermute | solution.py:688
  18.3 13.3 %collective-permute-start.1 = (bf16[2,576,128]{2,1,0:T(8,128)(2,1)S(1)}, bf16[2,576,128]{2,1,0:T(8,128)(2,1)S(1)}, u32[]{:S(2)}, u32[]{:S(2)}) collective-permute-start(bf16[2,576,128]{2,1,0:T(8,128)(2,1)S(1)} %bitcast.61), channel_id=1, source_target_pairs={{0,120},{8,112},{16,104},{24,96},{32,88},{40,80},{48,72},{56,64},{... | collective-permute-start | bytes 884744 | tf_op jit(solution)/shard_map/ppermute | solution.py:688
  25.0 44.8 %copy-start.16 = (bf16[2,576,128]{2,1,0:T(8,128)(2,1)}, bf16[2,576,128]{2,1,0:T(8,128)(2,1)S(1)}, u32[]{:S(2)}) copy-start(bf16[2,576,128]{2,1,0:T(8,128)(2,1)S(1)} %collective-permute-done.query_ref.q2_ref) | copy-start | bytes 884740
  31.6 38.2 %copy-start.17 = (bf16[2,576,128]{2,1,0:T(8,128)(2,1)}, bf16[2,576,128]{2,1,0:T(8,128)(2,1)S(1)}, u32[]{:S(2)}) copy-start(bf16[2,576,128]{2,1,0:T(8,128)(2,1)S(1)} %collective-permute-done.1.d2_ref) | copy-start | bytes 884740
  78.1 12.5 %collective-permute-start.2 = (bf16[10368,128]{1,0:T(8,128)(2,1)}, bf16[10368,128]{1,0:T(8,128)(2,1)S(1)}, u32[]{:S(2)}, u32[]{:S(2)}) collective-permute-start(bf16[10368,128]{1,0:T(8,128)(2,1)} %get-tuple-element.92), channel_id=1, source_target_pairs={{0,1},{1,0},{2,3},{3,2},{4,5},{5,4},{6,7},{7,6},{8,9},{9,8},{10,11... | collective-permute-start | bytes 7962632 | tf_op jit(solution)/shard_map/ppermute | solution.py:683
  102.5 37.2 %all-to-all-start = ((bf16[4,2688,128]{2,1,0:T(8,128)(2,1)}), bf16[4,2688,128]{2,1,0:T(8,128)(2,1)S(1)}, u32[]{:S(2)}, u32[]{:S(2)}) async-start(bf16[4,2688,128]{2,1,0:T(8,128)(2,1)} %bitcast.39), calls=%async_computation | async-start | bytes 5505024 | tf_op jit(solution)/shard_map/all_to_all | solution.py:705
  106.5 127.6 %reduce-scatter.2.cloned.1.call-start = ((), (), s32[]{:S(2)}) async-start(), calls=%async_computation.6 | async-start | bytes 3342336 | tf_op jit(solution)/shard_map/reduce_scatter | solution.py:810
  126.3 12.1 %collective-permute-start.3 = (bf16[2,576,128]{2,1,0:T(8,128)(2,1)}, bf16[2,576,128]{2,1,0:T(8,128)(2,1)}, u32[]{:S(2)}, u32[]{:S(2)}) collective-permute-start(bf16[2,576,128]{2,1,0:T(8,128)(2,1)} %get-tuple-element.108), channel_id=1, source_target_pairs={{0,120},{8,112},{16,104},{24,96},{32,88},{40,80},{48,72},{56,64},{... | collective-permute-start | bytes 884744 | tf_op jit(solution)/shard_map/ppermute | solution.py:688
  141.2 19.5 %all-to-all-start.1 = ((bf16[16,168,128]{2,1,0:T(8,128)(2,1)}), bf16[16,168,128]{2,1,0:T(8,128)(2,1)S(1)}, u32[]{:S(2)}, u32[]{:S(2)}) async-start(bf16[16,168,128]{2,1,0:T(8,128)(2,1)} %bitcast.12), calls=%async_computation.1 | async-start | bytes 1376256 | tf_op jit(solution)/shard_map/all_to_all | solution.py:705
  160.7 7.2 %collective-permute-start.4 = (bf16[4,1024,128]{2,1,0:T(8,128)(2,1)}, bf16[4,1024,128]{2,1,0:T(8,128)(2,1)S(1)}, u32[]{:S(2)}, u32[]{:S(2)}) collective-permute-start(bf16[4,1024,128]{2,1,0:T(8,128)(2,1)} %get-tuple-element.117), channel_id=1, source_target_pairs={{0,1},{1,0},{2,3},{3,2},{4,5},{5,4},{6,7},{7,6},{8,9},{9,8},{10,11... | collective-permute-start | bytes 3145736 | tf_op jit(solution)/shard_map/ppermute | solution.py:683
  164.2 20.0 %all-to-all-start.2 = ((bf16[16,168,128]{2,1,0:T(8,128)(2,1)}), bf16[16,168,128]{2,1,0:T(8,128)(2,1)S(1)}, u32[]{:S(2)}, u32[]{:S(2)}) async-start(bf16[16,168,128]{2,1,0:T(8,128)(2,1)} %broadcast_in_dim.4), calls=%async_computation.2 | async-start | bytes 1376256 | tf_op jit(solution)/shard_map/all_to_all | solution.py:720
  168.2 9.3 %collective-permute-start.5 = (bf16[1024,128]{1,0:T(8,128)(2,1)S(1)}, bf16[1024,128]{1,0:T(8,128)(2,1)S(1)}, u32[]{:S(2)}, u32[]{:S(2)}) collective-permute-start(bf16[1024,128]{1,0:T(8,128)(2,1)S(1)} %get-tuple-element.150), channel_id=1, source_target_pairs={{0,2},{2,4},{4,6},{6,0},{1,3},{3,5},{5,7},{7,1},{8,10},{10,12},{12... | collective-permute-start | bytes 786440 | tf_op jit(solution)/shard_map/ppermute | solution.py:683
  169.6 14.5 %collective-permute-start.6 = (bf16[1024,128]{1,0:T(8,128)(2,1)S(1)}, bf16[1024,128]{1,0:T(8,128)(2,1)S(1)}, u32[]{:S(2)}, u32[]{:S(2)}) collective-permute-start(bf16[1024,128]{1,0:T(8,128)(2,1)S(1)} %get-tuple-element.152), channel_id=1, source_target_pairs={{0,4},{2,6},{4,0},{6,2},{1,5},{3,7},{5,1},{7,3},{8,12},{10,14},{12... | collective-permute-start | bytes 786440 | tf_op jit(solution)/shard_map/ppermute | solution.py:683
  172.0 12.1 %collective-permute-start.7 = (bf16[1024,128]{1,0:T(8,128)(2,1)S(1)}, bf16[1024,128]{1,0:T(8,128)(2,1)S(1)}, u32[]{:S(2)}, u32[]{:S(2)}) collective-permute-start(bf16[1024,128]{1,0:T(8,128)(2,1)S(1)} %get-tuple-element.151), channel_id=1, source_target_pairs={{0,6},{2,0},{4,2},{6,4},{1,7},{3,1},{5,3},{7,5},{8,14},{10,8},{12,... | collective-permute-start | bytes 786440 | tf_op jit(solution)/shard_map/ppermute | solution.py:683
  184.2 35.3 %copy-start.3 = (bf16[16,168,128]{2,1,0:T(8,128)(2,1)}, bf16[16,168,128]{2,1,0:T(8,128)(2,1)S(1)}, u32[]{:S(2)}) copy-start(bf16[16,168,128]{2,1,0:T(8,128)(2,1)S(1)} %all-to-all-done.2) | copy-start | bytes 2064388
  184.2 17.5 %collective-permute-start.8 = (bf16[2688,128]{1,0:T(8,128)(2,1)S(1)}, bf16[2688,128]{1,0:T(8,128)(2,1)S(1)}, u32[]{:S(2)}, u32[]{:S(2)}) collective-permute-start(bf16[2688,128]{1,0:T(8,128)(2,1)S(1)} %bitcast.43), channel_id=1, source_target_pairs={{0,2},{2,4},{4,6},{6,0},{1,3},{3,5},{5,7},{7,1},{8,10},{10,12},{12... | collective-permute-start | bytes 2064392 | tf_op jit(solution)/shard_map/ppermute | solution.py:683
  185.3 16.4 %collective-permute-start.9 = (bf16[2688,128]{1,0:T(8,128)(2,1)S(1)}, bf16[2688,128]{1,0:T(8,128)(2,1)S(1)}, u32[]{:S(2)}, u32[]{:S(2)}) collective-permute-start(bf16[2688,128]{1,0:T(8,128)(2,1)S(1)} %bitcast.44), channel_id=1, source_target_pairs={{0,6},{2,0},{4,2},{6,4},{1,7},{3,1},{5,3},{7,5},{8,14},{10,8},{12,... | collective-permute-start | bytes 2064392 | tf_op jit(solution)/shard_map/ppermute | solution.py:683
  201.7 10.1 %collective-permute-start.13 = (bf16[1344,128]{1,0:T(8,128)(2,1)S(1)}, bf16[1344,128]{1,0:T(8,128)(2,1)S(1)}, u32[]{:S(2)}, u32[]{:S(2)}) collective-permute-start(bf16[1344,128]{1,0:T(8,128)(2,1)S(1)} %slice.22), channel_id=1, source_target_pairs={{0,2},{2,4},{4,6},{6,0},{1,3},{3,5},{5,7},{7,1},{8,10},{10,12},{12... | collective-permute-start | bytes 1032200 | tf_op jit(solution)/shard_map/ppermute | solution.py:683
  202.7 9.2 %collective-permute-start.14 = (bf16[1344,128]{1,0:T(8,128)(2,1)S(1)}, bf16[1344,128]{1,0:T(8,128)(2,1)}, u32[]{:S(2)}, u32[]{:S(2)}) collective-permute-start(bf16[1344,128]{1,0:T(8,128)(2,1)S(1)} %slice.23), channel_id=1, source_target_pairs={{0,6},{2,0},{4,2},{6,4},{1,7},{3,1},{5,3},{7,5},{8,14},{10,8},{12,... | collective-permute-start | bytes 1032200 | tf_op jit(solution)/shard_map/ppermute | solution.py:683
  204.6 6.0 %collective-permute-start.10 = (bf16[64,128]{1,0:T(8,128)(2,1)S(1)}, bf16[64,128]{1,0:T(8,128)(2,1)S(1)}, u32[]{:S(2)}, u32[]{:S(2)}) collective-permute-start(bf16[64,128]{1,0:T(8,128)(2,1)S(1)} %reduce_sum.38), channel_id=1, source_target_pairs={{0,2},{2,4},{4,6},{6,0},{1,3},{3,5},{5,7},{7,1},{8,10},{10,12},{12... | collective-permute-start | bytes 49160 | tf_op jit(solution)/shard_map/ppermute | solution.py:683
  204.6 7.3 %collective-permute-start.11 = (bf16[64,128]{1,0:T(8,128)(2,1)S(1)}, bf16[64,128]{1,0:T(8,128)(2,1)S(1)}, u32[]{:S(2)}, u32[]{:S(2)}) collective-permute-start(bf16[64,128]{1,0:T(8,128)(2,1)S(1)} %reduce_sum.38), channel_id=1, source_target_pairs={{0,4},{2,6},{4,0},{6,2},{1,5},{3,7},{5,1},{7,3},{8,12},{10,14},{12... | collective-permute-start | bytes 49160 | tf_op jit(solution)/shard_map/ppermute | solution.py:683
  206.9 5.0 %collective-permute-start.12 = (bf16[64,128]{1,0:T(8,128)(2,1)S(1)}, bf16[64,128]{1,0:T(8,128)(2,1)S(1)}, u32[]{:S(2)}, u32[]{:S(2)}) collective-permute-start(bf16[64,128]{1,0:T(8,128)(2,1)S(1)} %reduce_sum.38), channel_id=1, source_target_pairs={{0,6},{2,0},{4,2},{6,4},{1,7},{3,1},{5,3},{7,5},{8,14},{10,8},{12,... | collective-permute-start | bytes 49160 | tf_op jit(solution)/shard_map/ppermute | solution.py:683
  213.1 24.1 %all-to-all-start.4 = ((bf16[16,4,64,128]{3,2,1,0:T(8,128)(2,1)}), bf16[16,4,64,128]{3,2,1,0:T(8,128)(2,1)S(1)}, u32[]{:S(2)}, u32[]{:S(2)}) async-start(bf16[16,4,64,128]{3,2,1,0:T(8,128)(2,1)} %broadcast_in_dim.5), calls=%async_computation.4 | async-start | bytes 2097152 | tf_op jit(solution)/shard_map/all_to_all | solution.py:832
  219.5 8.6 %collective-permute-start.15 = (bf16[2688,128]{1,0:T(8,128)(2,1)S(1)}, bf16[2688,128]{1,0:T(8,128)(2,1)S(1)}, u32[]{:S(2)}, u32[]{:S(2)}) collective-permute-start(bf16[2688,128]{1,0:T(8,128)(2,1)S(1)} %bitcast.45), channel_id=1, source_target_pairs={{0,1},{1,0},{2,3},{3,2},{4,5},{5,4},{6,7},{7,6},{8,9},{9,8},{10,11... | collective-permute-start | bytes 2064392 | tf_op jit(solution)/shard_map/ppermute | solution.py:683
  222.6 5.5 %collective-permute-start.16 = (bf16[2688,128]{1,0:T(8,128)(2,1)S(1)}, bf16[2688,128]{1,0:T(8,128)(2,1)S(1)}, u32[]{:S(2)}, u32[]{:S(2)}) collective-permute-start(bf16[2688,128]{1,0:T(8,128)(2,1)S(1)} %collective-permute-done.8.refs_1_), channel_id=1, source_target_pairs={{0,1},{1,0},{2,3},{3,2},{4,5},{5,4},{6,7},{7,6},{8,9},{9,8},{10,11... | collective-permute-start | bytes 2064392 | tf_op jit(solution)/shard_map/ppermute | solution.py:683
  222.7 5.5 %collective-permute-start.19 = (bf16[2688,128]{1,0:T(8,128)(2,1)S(1)}, bf16[2688,128]{1,0:T(8,128)(2,1)S(1)}, u32[]{:S(2)}, u32[]{:S(2)}) collective-permute-start(bf16[2688,128]{1,0:T(8,128)(2,1)S(1)} %collective-permute-done.9.refs_4_), channel_id=1, source_target_pairs={{0,1},{1,0},{2,3},{3,2},{4,5},{5,4},{6,7},{7,6},{8,9},{9,8},{10,11... | collective-permute-start | bytes 2064392 | tf_op jit(solution)/shard_map/ppermute | solution.py:683
  223.2 5.0 %collective-permute-start.17 = (bf16[1344,128]{1,0:T(8,128)(2,1)S(1)}, bf16[1344,128]{1,0:T(8,128)(2,1)S(1)}, u32[]{:S(2)}, u32[]{:S(2)}) collective-permute-start(bf16[1344,128]{1,0:T(8,128)(2,1)S(1)} %collective-permute-done.13.refs_2_), channel_id=1, source_target_pairs={{0,1},{1,0},{2,3},{3,2},{4,5},{5,4},{6,7},{7,6},{8,9},{9,8},{10,11... | collective-permute-start | bytes 1032200 | tf_op jit(solution)/shard_map/ppermute | solution.py:683
  223.2 4.9 %collective-permute-start.18 = (bf16[1344,128]{1,0:T(8,128)(2,1)}, bf16[1344,128]{1,0:T(8,128)(2,1)S(1)}, u32[]{:S(2)}, u32[]{:S(2)}) collective-permute-start(bf16[1344,128]{1,0:T(8,128)(2,1)} %collective-permute-done.14.refs_3_), channel_id=1, source_target_pairs={{0,1},{1,0},{2,3},{3,2},{4,5},{5,4},{6,7},{7,6},{8,9},{9,8},{10,11... | collective-permute-start | bytes 1032200 | tf_op jit(solution)/shard_map/ppermute | solution.py:683
  237.2 3.2 %collective-permute-start.20 = (bf16[16,4,64,128]{3,2,1,0:T(8,128)(2,1)S(1)}, bf16[16,4,64,128]{3,2,1,0:T(8,128)(2,1)S(1)}, u32[]{:S(2)}, u32[]{:S(2)}) collective-permute-start(bf16[16,4,64,128]{3,2,1,0:T(8,128)(2,1)S(1)} %all-to-all-done.4.kept), channel_id=1, source_target_pairs={{0,1},{1,0},{2,3},{3,2},{4,5},{5,4},{6,7},{7,6},{8,9},{9,8},{10,11... | collective-permute-start | bytes 3145736 | tf_op jit(solution)/shard_map/ppermute | solution.py:683
  (14 other events, 93.4 us)
Sparse Core Ops, SparseCore 0:
  11.5 52.8 all-gather.4
  67.1 58.1 all-gather.6
  139.8 83.1 reduce-scatter.1

commit v2 on v1

--- a/solution.py
+++ b/solution.py
@@ -20,7 +20,7 @@
 FACTOR = 1.0 / math.sqrt(HD)
 LANES = 128
 SIDE = 4
-KEYS = 256
+KEYS = 512
 CHUNK = 256
 SEQ = ("z", "x")
 SIMPLE = {"kv_weights": 2.0, "input_back": 1.0, "prepare": 1.0, "query": 1.0}
@@ -138,7 +138,9 @@
     sin_out[...] = sine
     inputs = side_by_side(tokens).astype(f32)
     scale = lax.rsqrt(jnp.mean(inputs * inputs, axis=0, keepdims=True) + EPSILON)
-    normed = (inputs * scale * gain[...].astype(f32)).astype(bf16)
+    line = gain[...].astype(f32).reshape(1, gain.shape[0])
+    column = flip(jnp.broadcast_to(line, (LANES, gain.shape[0])))[:, :1]
+    normed = (inputs * scale * column).astype(bf16)
     width = tokens.shape[1]
     for m in range(micro):
         span = slice(m * rows, (m + 1) * rows)
@@ -184,16 +186,12 @@
     return jnp.min(start) // KEYS, block // per + 1
 
 
-def forward_kernel(far, held, query_ref, starts, low_out, flat_out, lse_out, acc, peak, mass, query):
-    block_place = far_block() if far else own_block()
-    scale = FACTOR if far else 1.0
-    query[...] = (query_ref[0] * scale).astype(bf16)
+def run_forward(held, query, start, block_place, acc, peak, mass):
     rows = query.shape[1]
     per = KEYS // rows
     acc[...] = jnp.zeros_like(acc)
     peak[...] = jnp.full_like(peak, NEGATIVE)
     mass[...] = jnp.zeros_like(mass)
-    start = starts[0]
     first_step, last_step = key_steps(start, block_place, rows)
 
     @pl.loop(first_step, last_step)
@@ -214,11 +212,19 @@
             peak[g] = top
 
     for g in range(KVH):
-        lse_out[0, g] = peak[g] + jnp.log(mass[g])
-        result = acc[g] * (1.0 / mass[g])
+        acc[g] = acc[g] * (1.0 / mass[g])
+        peak[g] = peak[g] + jnp.log(mass[g])
+
+
+def forward_kernel(held, query_ref, starts, low_out, flat_out, lse_out, acc, peak, mass):
+    query = query_ref.at[0]
+    rows = query.shape[1]
+    run_forward(held, query, starts[0], own_block(), acc, peak, mass)
+    for g in range(KVH):
+        lse_out[0, g] = peak[g]
         for h in range(GROUP):
             head = g * GROUP + h
-            flat_out[0, head * HD : (head + 1) * HD, :] = result[:, h * rows : (h + 1) * rows]
+            flat_out[0, head * HD : (head + 1) * HD, :] = acc[g, :, h * rows : (h + 1) * rows]
     low_out[...] = flat_out[...].astype(bf16)
 
 
@@ -227,14 +233,14 @@
     return pl.BlockSpec(block, lambda m: tuple(m if i == axis else 0 for i in range(len(dims))))
 
 
-def attend_forward(far, kv, query, starts):
+def attend_forward(kv, query, starts):
     micro, width, rows = query.shape
     lanes = GROUP * rows
     low = shape_of(query.shape, bf16)
     flat = shape_of(query.shape, f32)
     lse = shape_of((micro, KVH, 1, lanes), f32)
     return pl.pallas_call(
-        functools.partial(forward_kernel, far),
+        forward_kernel,
         grid=(micro,),
         in_specs=[one_of(kv.shape, 1), one_of(query.shape), one_of(starts.shape)],
         out_specs=[one_of(v.shape) for v in (low, flat, lse)],
@@ -243,7 +249,6 @@
             pltpu.VMEM((KVH, HD, lanes), f32),
             pltpu.VMEM((KVH, 1, lanes), f32),
             pltpu.VMEM((KVH, 1, lanes), f32),
-            pltpu.VMEM((width, rows), bf16),
         ],
         compiler_params=params(),
         cost_estimate=cost(2.5),
@@ -252,8 +257,8 @@
 
 
 def backward_kernel(
-    held, q1_ref, q2_ref, d1_ref, d2_ref, o1, o2, lse1, lse2, starts, far_starts, cos_ref, sin_ref,
-    kv_out, first_grad, second_grad, sums, delta, dq, query2, both,
+    held, q1_ref, q2_ref, d1_ref, d2_ref, o1, lse1, starts, far_starts, cos_ref, sin_ref,
+    kv_out, first_grad, second_grad, sums, delta, dq, query2, both, acc, peak, mass,
 ):
     rows = q1_ref.shape[2]
     per = KEYS // rows
@@ -261,10 +266,10 @@
     sums[...] = jnp.zeros_like(sums)
     dq[...] = jnp.zeros_like(dq)
 
-    def attention(a, q_ref, d_ref, o_ref, lse_ref, start, block_place):
+    def attention(a, q_ref, d_ref, outs, lse, start, block_place):
         for g in range(KVH):
             query, grad = lane_heads(q_ref, g), lane_heads(d_ref, g)
-            delta[a, g] = jnp.sum(grad.astype(f32) * lane_heads(o_ref, g), axis=0, keepdims=True)
+            delta[a, g] = jnp.sum(grad.astype(f32) * outs(g), axis=0, keepdims=True)
             zero = jnp.zeros_like(query)
             both[g] = jnp.concatenate(
                 [jnp.concatenate([query, zero], axis=1), jnp.concatenate([zero, grad], axis=1)], axis=0
@@ -281,15 +286,16 @@
                 pair = both[g]
                 lanes = pair.shape[1] // 2
                 products = mul(tiles[g], pair)
-                weights = jnp.exp(products[:, :lanes] + bias - lse_ref[0, g])
+                weights = jnp.exp(products[:, :lanes] + bias - lse[g])
                 score_grad = (weights * (products[:, lanes:] - delta[a, g])).astype(bf16)
                 dq[a, g] += mul(jnp.transpose(tiles[g])[:HD], score_grad)
                 total.append(mul_nt(jnp.concatenate([score_grad, weights.astype(bf16)], axis=1), pair))
             joined = jnp.concatenate(total, axis=1)
             sums[pl.ds(step * per, per)] += joined.reshape(per, rows, joined.shape[1])
 
-    attention(0, q1_ref.at[0], d1_ref.at[0], o1.at[0], lse1, starts[0], own_block())
-    attention(1, query2, d2_ref.at[0], o2.at[0], lse2, far_starts[0], far_block())
+    run_forward(held, query2, far_starts[0], far_block(), acc, peak, mass)
+    attention(0, q1_ref.at[0], d1_ref.at[0], lambda g: lane_heads(o1.at[0], g), lse1.at[0], starts[0], own_block())
+    attention(1, query2, d2_ref.at[0], lambda g: acc[g], peak, far_starts[0], far_block())
     kv_out[:, 0] = sums[...].astype(bf16)
     cosine, sine = cos_ref[...], -sin_ref[...]
     for g in range(KVH):
@@ -320,6 +326,9 @@
             pltpu.VMEM((2, KVH, HD, lanes), f32),
             pltpu.VMEM((width, rows), bf16),
             pltpu.VMEM((KVH, 2 * HD, 2 * lanes), bf16),
+            pltpu.VMEM((KVH, HD, lanes), f32),
+            pltpu.VMEM((KVH, 1, lanes), f32),
+            pltpu.VMEM((KVH, 1, lanes), f32),
         ],
         compiler_params=params(),
         cost_estimate=cost(7),
@@ -418,9 +427,9 @@
     step = pl.program_id(0)
     micro, width, rows = tokens.shape
     if last:
-        before, result_before, grad_before, received = refs[:4]
-        result, main, middle_grad, d1, gain_grad, wo_grad = refs[4:10]
-        normed, normed_t, grad, grad_t, result_sum, normed_grad = refs[10:]
+        before, result_before, grad_before = refs[:3]
+        result, main, middle_grad, d1, gain_grad, wo_grad = refs[3:9]
+        normed, normed_t, grad, grad_t, result_sum, normed_grad = refs[9:]
         middle = before
     else:
         main, middle, result_sum, normed_grad = refs[:4]
@@ -460,10 +469,7 @@
         span = slice(i * LANES, (i + 1) * LANES)
         for k, part in enumerate(parts):
             rows_at = slice((i * 3 + k) * width, (i * 3 + k + 1) * width)
-            value = part[:, span].astype(bf16)
-            if last:
-                value = (value.astype(f32) + received[rows_at].astype(f32)).astype(bf16)
-            main[rows_at] = value
+            main[rows_at] = part[:, span].astype(bf16)
     normed_grad[...] += mul_nt(gate_grad, wg[...]) + mul_nt(up_grad, wu[...])
     if not last:
         return
@@ -531,11 +537,11 @@
             (shape_of((width, 1), f32), whole(width, 1)),
             (shape_of((width, width), bf16), whole(width, width)),
         ]
-        more = [spec, tall, tall, block]
+        more = [spec, tall, tall]
         scratch = [pltpu.VMEM((total, width), f32)] * 2
     else:
         outs = [
-            (shape_of((hidden // 2 // LANES * 3 * width, LANES), bf16), block),
+            (shape_of((main_rows(width, hidden), LANES), bf16), block),
             (flat, spec),
             (natural, tall),
             (natural, tall),
@@ -764,7 +770,7 @@
             start,
             start,
         ],
-        (doc_lengths, tokens, gain_one, wk, wv),
+        (doc_lengths, tokens, first_gain, wk, wv),
         "prepare",
     )
     kv = lax.all_gather(kv, SEQ, axis=0)
@@ -778,13 +784,11 @@
     far_query, far_grad = mirror(second_query), mirror(second_grad)
     kv, q1, far_query, far_grad, gathered = lax.optimization_barrier((kv, q1, far_query, far_grad, normed))
     gathered = lax.all_gather(gathered, SEQ, axis=0)
-    first_low, first_flat, first_lse = attend_forward(False, kv, q1, starts)
+    first_low, first_flat, first_lse = attend_forward(kv, q1, starts)
     ffn_args = (first_low, tokens, output_weight, gain_two, out_grad, gate_weight, up_weight, wd)
     away, *before = feed_forward(core, *ffn_args, ())
-    far_query = after(far_query, away)
-    _, second_flat, second_lse = attend_forward(True, kv, far_query, far_starts)
-    received, second_lse = lax.optimization_barrier((shift(away, "core", 1), second_lse))
-    result, main, middle_grad, d1, gain_two_grad, wo_grad = feed_forward(core, *ffn_args, (*before, received))
+    result, main, middle_grad, d1, gain_two_grad, wo_grad = feed_forward(core, *ffn_args, before)
+    main = (main.astype(f32) + shift(away, "core", 1).astype(f32)).astype(bf16)
     main = scatter_parts(main, "y")
     kv_grad, query_grad, second_query_grad = attend_backward(
         kv,
@@ -793,16 +797,14 @@
         d1,
         far_grad,
         first_flat,
-        second_flat,
         first_lse,
-        second_lse,
         starts,
         far_starts,
         cosine,
         sine,
     )
     second_query_grad = mirror(second_query_grad)
-    kv_grad, gathered, main, second_query_grad = lax.optimization_barrier((kv_grad, gathered, main, second_query_grad))
+    kv_grad, gathered, main = lax.optimization_barrier((kv_grad, gathered, main))
     main = scatter_parts(sum_parts(main), SEQ)
     normed_part, tail, tail_away = weights_back(
         kv_grad, gathered, starts, far_starts, normed, query_grad, query_weight, wo_grad, gain_two_grad
@@ -812,7 +814,7 @@
     tail = (tail.astype(f32) + shift(tail_away, "core", 1).astype(f32)).astype(bf16)
     main = gather_all(sum_parts(main), SEQ)
     tail = exchange([tail[k] for k in range(SIDE)], "y").astype(bf16)
-    tail, main = lax.optimization_barrier((tail, main))
+    tail, main, second_query_grad = lax.optimization_barrier((tail, main, second_query_grad))
     middle = main.shape[0] // 2
     ahead, behind = shift(main, "y", 1), shift(main, "y", -1)
     tokens_like = shape_of((micro, width, rows), bf16)

time: 253 us -> 251 us (level)
  Pallas kernels: 85.8 us -> 82.1 us
  other arithmetic: 1.99 us -> 5.23 us
    pallas_call x2 -> x1, Pallas kernels: 16.1 us -> 5.67 us  [attend_forward(): pl.pallas_call(forward_kernel, grid=(micro,), in_specs=[one_of(kv.shape,...]
    pallas_call x1, Pallas kernels: 19.8 us -> 27 us  [attend_backward(): pl.pallas_call(backward_kernel, grid=(micro,), in_specs=[one_of(kv.shape,...]
    all_to_all x2, waiting for transfers between devices: 5.14 us -> 11.5 us  [scatter_parts(): lax.all_to_all(held.reshape(places, rows // places, lanes), axis, 0, 0)]
    convert_element_type x0 -> x1, other arithmetic: none -> 3.24 us  [per_device(): main = (main.astype(f32) + shift(away, 'core', 1).astype(f32)).astype(bf16)]
    ppermute x3, waiting for transfers between devices: 20.1 us -> 16.9 us  [mirror(): return lax.ppermute(value, SEQ, [(i, size - 1 - i) for i in range(size)])]
    all_to_all x2, starting transfers between devices: 9.94 us -> 12.8 us  [scatter_parts(): lax.all_to_all(held.reshape(places, rows // places, lanes), axis, 0, 0)]
  transfers between devices with their start and end apart: 28 -> 28, of which waited for: 12 -> 12; matrix products, arithmetic and copies ran while one was open for 2% -> 4% of each run, Pallas kernels for 31% -> 30%
where the time goes in v2:
time: 251 us; the launch traced here: 250 us
  Pallas kernels  82.1 us (33%)
  waiting for transfers between devices  79.6 us (32%)
  starting transfers between devices  51 us (20%)
  between operations  14.1 us (6%)
  blocking collectives  11.5 us (5%)
  local copies, waits for them, and re-layouts  6.36 us (3%)
  other arithmetic  5.23 us (2%)
    all_gather x1, waiting for transfers between devices, per_device(): kv = lax.all_gather(kv, SEQ, axis=0)  32.8 us
    pallas_call x1, Pallas kernels, attend_backward(): pl.pallas_call(backward_kernel, grid=(micro,), in_specs=[one_of(kv.shape,...  27 us
    ppermute x18, starting transfers between devices, shift(): lax.ppermute(value, axis, [(i, (i + distance) % size) for i in range(size)])  18.7 us
    pallas_call x2, Pallas kernels, feed_forward(): pl.pallas_call(functools.partial(ffn_kernel, last), grid_spec=pltpu.Prefe...  18.6 us
    ppermute x18, waiting for transfers between devices, shift(): lax.ppermute(value, axis, [(i, (i + distance) % size) for i in range(size)])  18.3 us
    ppermute x3, waiting for transfers between devices, mirror(): return lax.ppermute(value, SEQ, [(i, size - 1 - i) for i in range(size)])  16.9 us
    all_to_all x2, starting transfers between devices, scatter_parts(): lax.all_to_all(held.reshape(places, rows // places, lanes), axis, 0, 0)  12.8 us
    ppermute x3, starting transfers between devices, mirror(): return lax.ppermute(value, SEQ, [(i, size - 1 - i) for i in range(size)])  11.6 us
  transfers between devices with their start and end apart: 28, of which 12 were waited for; matrix products, arithmetic and copies ran while one was open for 4% of the time, Pallas kernels for 30%

profile of v2, /device:TPU:1, one launch (start us, length us, event | category | flops | bytes accessed | tf_op | source)
XLA Modules:
  0.0 249.9 jit_solution(2271629738633776652)
XLA Ops:
  7.2 2.7 %prepare.1 = (bf16[2,704,128]{2,1,0:T(8,128)(2,1)}, bf16[2,128,384]{2,1,0:T(8,128)(2,1)}, f32[32,256]{1,0:T(8,128)}, f32[32,256]{1,0:T(8,128)}, s32[2,1,128]{2,1,0:T(1,128)}, /*index=5*/s32[2,1,128]{2,1,0:T(1,128)}) custom-call(s32[2,16]{1,0:T(2,128)} %lengths.1, bf16[2,576,128]{2,1,0:T(8,128)(2,1)} %bitcast.57, bf16[576]{0:T(1024)(128)(2,1)} %gain.1, ...), custom_call_target="tpu_custom_call" | custom-call | flops 1000000000 | bytes 1000 | tf_op jit(solution)/shard_map/prepare/pallas_call | solution.py:104
  10.0 6.9 %collective-permute-start = (bf16[2,576,128]{2,1,0:T(8,128)(2,1)S(1)}, bf16[2,576,128]{2,1,0:T(8,128)(2,1)S(1)}, u32[]{:S(2)}, u32[]{:S(2)}) collective-permute-start(bf16[2,576,128]{2,1,0:T(8,128)(2,1)S(1)} %bitcast.53), channel_id=1, source_target_pairs={{0,120},{8,112},{16,104},{24,96},{32,88},{40,80},{48,72},{56,64},{... | collective-permute-start | bytes 884744 | tf_op jit(solution)/shard_map/ppermute | solution.py:694
  19.4 4.2 %collective-permute-done.q2_ref = bf16[2,576,128]{2,1,0:T(8,128)(2,1)S(1)} collective-permute-done((bf16[2,576,128]{2,1,0:T(8,128)(2,1)S(1)}, bf16[2,576,128]{2,1,0:T(8,128)(2,1)S(1)}, u32[]{:S(2)}, u32[]{:S(2)}) %collective-permute-start) | collective-permute-done | bytes 294944 | tf_op jit(solution)/shard_map/ppermute | solution.py:694
  23.6 6.4 %collective-permute-done.1.d2_ref = bf16[2,576,128]{2,1,0:T(8,128)(2,1)S(1)} collective-permute-done((bf16[2,576,128]{2,1,0:T(8,128)(2,1)S(1)}, bf16[2,576,128]{2,1,0:T(8,128)(2,1)S(1)}, u32[]{:S(2)}, u32[]{:S(2)}) %collective-permute-start.1) | collective-permute-done | bytes 294944 | tf_op jit(solution)/shard_map/ppermute | solution.py:694
  30.1 32.8 %all-gather.5.cloned.1.call-done = bf16[32,128,384]{2,1,0:T(8,128)(2,1)} async-done(((bf16[2,128,384]{2,1,0:T(8,128)(2,1)}), bf16[32,128,384]{2,1,0:T(8,128)(2,1)}) %all-gather.5.cloned.1.call-update) | async-done | bytes 3145744 | tf_op jit(solution)/shard_map/all_gather | solution.py:776
  63.7 5.7 %attention_forward.1 = (bf16[2,576,128]{2,1,0:T(8,128)(2,1)}, f32[2,576,128]{2,1,0:T(8,128)}, f32[2,3,1,384]{3,2,1,0:T(1,128)}) custom-call(bf16[16,2,128,384]{3,2,1,0:T(8,128)(2,1)} %bitcast.49, bf16[2,576,128]{2,1,0:T(8,128)(2,1)} %query.1.query_ref.q1_ref, s32[2,1,128]{2,1,0:T(1,128)} %get-tuple-element.82.starts), custom_call_target="tpu_custom_call" | custom-call | flops 2500000000 | bytes 1000 | tf_op jit(solution)/shard_map/attention_forward/pallas_call | solution.py:242
  69.4 8.6 %feed_forward.2 = (bf16[10752,128]{1,0:T(8,128)(2,1)}, f32[576,256]{1,0:T(8,128)}, f32[256,576]{1,0:T(8,128)}, f32[256,576]{1,0:T(8,128)}) custom-call(s32[1]{0:T(128)} %bitcast.core, bf16[2,576,128]{2,1,0:T(8,128)(2,1)} %get-tuple-element.83.first, bf16[2,576,128]{2,1,0:T(8,128)(2,1)} %bitcast.58, bf16[576,576]{1,0:T(8,128)(2,1)} %out_weight.3, ...), custom_call_target="tpu_custom_call" | custom-call | flops 3000000000 | bytes 1000 | tf_op jit(solution)/shard_map/feed_forward/pallas_call | solution.py:551
  79.0 10.0 %feed_forward.3 = (bf16[2,576,128]{2,1,0:T(8,128)(2,1)}, bf16[10752,128]{1,0:T(8,128)(2,1)}, f32[576,256]{1,0:T(8,128)}, bf16[2,576,128]{2,1,0:T(8,128)(2,1)}, f...) custom-call(s32[1]{0:T(128)} %bitcast.core, bf16[2,576,128]{2,1,0:T(8,128)(2,1)} %get-tuple-element.83.first, ...), custom_call_target="tpu_custom_call" | custom-call | flops 3000000000 | bytes 1000 | tf_op jit(solution)/shard_map/feed_forward/pallas_call | solution.py:551
  89.1 3.2 %add_convert_fusion = bf16[10752,128]{1,0:T(8,128)(2,1)} fusion(bf16[10752,128]{1,0:T(8,128)(2,1)S(1)} %collective-permute-done.2, bf16[10752,128]{1,0:T(8,128)(2,1)} %get-tuple-element.96), kind=kLoop, calls=%fused_computation | loop fusion | flops 5505024 | bytes 8257536 | tf_op jit(solution)/shard_map/convert_element_type | solution.py:791
  92.3 4.0 %all-to-all-start = ((bf16[4,2688,128]{2,1,0:T(8,128)(2,1)}), bf16[4,2688,128]{2,1,0:T(8,128)(2,1)S(1)}, u32[]{:S(2)}, u32[]{:S(2)}) async-start(bf16[4,2688,128]{2,1,0:T(8,128)(2,1)} %bitcast.37), calls=%async_computation | async-start | bytes 5505024 | tf_op jit(solution)/shard_map/all_to_all | solution.py:711
  96.3 27.0 %attention_backward.1 = (bf16[16,2,128,384]{3,2,1,0:T(8,128)(2,1)}, bf16[2,576,128]{2,1,0:T(8,128)(2,1)}, bf16[2,576,128]{2,1,0:T(8,128)(2,1)}) custom-call(bf16[16,2,128,384]{3,2,1,0:T(8,128)(2,1)} %bitcast.50, bf16[2,576,128]{2,1,0:T(8,128)(2,1)} %query.1.query_ref.q1_ref, bf16[2,576,128]{2,1,0:T(8,128)(2,1)} %copy-done.17, ...), custom_call_target="tpu_custom_call" | custom-call | flops 7000000000 | bytes 1000 | tf_op jit(solution)/shard_map/attention_backward/pallas_call | solution.py:317
  123.4 6.2 %all-to-all-done = bf16[4,2688,128]{2,1,0:T(8,128)(2,1)S(1)} async-done(((bf16[4,2688,128]{2,1,0:T(8,128)(2,1)}), bf16[4,2688,128]{2,1,0:T(8,128)(2,1)S(1)}, u32[]{:S(2)}, u32[]{:S(2)}) %all-to-all-start) | async-done | bytes 2752544 | tf_op jit(solution)/shard_map/all_to_all | solution.py:711
  131.0 8.8 %all-to-all-start.1 = ((bf16[16,168,128]{2,1,0:T(8,128)(2,1)}), bf16[16,168,128]{2,1,0:T(8,128)(2,1)S(1)}, u32[]{:S(2)}, u32[]{:S(2)}) async-start(bf16[16,168,128]{2,1,0:T(8,128)(2,1)} %bitcast.12), calls=%async_computation.1 | async-start | bytes 1376256 | tf_op jit(solution)/shard_map/all_to_all | solution.py:711
  139.8 9.2 %weights_back.1 = (f32[576,256]{1,0:T(8,128)}, bf16[4,1024,128]{2,1,0:T(8,128)(2,1)}, bf16[4,1024,128]{2,1,0:T(8,128)(2,1)}) custom-call(bf16[16,2,128,384]{3,2,1,0:T(8,128)(2,1)} %get-tuple-element.98.sums, bf16[16,2,704,128]{3,2,1,0:T(8,128)(2,1)} %bitcast.38, s32[2,1,128]{2,1,0:T(1,128)} %get-tuple-element.82.starts, ...), custom_call_target="tpu_custom_call" | custom-call | flops 3000000000 | bytes 1000 | tf_op jit(solution)/shard_map/weights_back/pallas_call | solution.py:400
  149.0 5.3 %all-to-all-done.1 = bf16[16,168,128]{2,1,0:T(8,128)(2,1)S(1)} async-done(((bf16[16,168,128]{2,1,0:T(8,128)(2,1)}), bf16[16,168,128]{2,1,0:T(8,128)(2,1)S(1)}, u32[]{:S(2)}, u32[]{:S(2)}) %all-to-all-start.1) | async-done | bytes 688160 | tf_op jit(solution)/shard_map/all_to_all | solution.py:711
  157.2 3.7 %all-to-all-start.2 = ((bf16[16,168,128]{2,1,0:T(8,128)(2,1)}), bf16[16,168,128]{2,1,0:T(8,128)(2,1)S(1)}, u32[]{:S(2)}, u32[]{:S(2)}) async-start(bf16[16,168,128]{2,1,0:T(8,128)(2,1)} %broadcast_in_dim.4), calls=%async_computation.2 | async-start | bytes 1376256 | tf_op jit(solution)/shard_map/all_to_all | solution.py:726
  164.2 4.7 %collective-permute-start.7 = (bf16[2,576,128]{2,1,0:T(8,128)(2,1)S(1)}, bf16[2,576,128]{2,1,0:T(8,128)(2,1)}, u32[]{:S(2)}, u32[]{:S(2)}) collective-permute-start(bf16[2,576,128]{2,1,0:T(8,128)(2,1)S(1)} %copy-done.16), channel_id=1, source_target_pairs={{0,120},{8,112},{16,104},{24,96},{32,88},{40,80},{48,72},{56,64},{... | collective-permute-start | bytes 884744 | tf_op jit(solution)/shard_map/ppermute | solution.py:694
  168.9 7.4 %collective-permute-done.4 = bf16[1024,128]{1,0:T(8,128)(2,1)S(1)} collective-permute-done((bf16[1024,128]{1,0:T(8,128)(2,1)S(1)}, bf16[1024,128]{1,0:T(8,128)(2,1)S(1)}, u32[]{:S(2)}, u32[]{:S(2)}) %collective-permute-start.4) | collective-permute-done | bytes 262176 | tf_op jit(solution)/shard_map/ppermute | solution.py:689
  176.7 6.3 %collective-permute-done.7.second = bf16[2,576,128]{2,1,0:T(8,128)(2,1)} collective-permute-done((bf16[2,576,128]{2,1,0:T(8,128)(2,1)S(1)}, bf16[2,576,128]{2,1,0:T(8,128)(2,1)}, u32[]{:S(2)}, u32[]{:S(2)}) %collective-permute-start.7) | collective-permute-done | bytes 294944 | tf_op jit(solution)/shard_map/ppermute | solution.py:694
  183.0 2.6 %collective-permute-start.9 = (bf16[2688,128]{1,0:T(8,128)(2,1)S(1)}, bf16[2688,128]{1,0:T(8,128)(2,1)S(1)}, u32[]{:S(2)}, u32[]{:S(2)}) collective-permute-start(bf16[2688,128]{1,0:T(8,128)(2,1)S(1)} %bitcast.42), channel_id=1, source_target_pairs={{0,6},{2,0},{4,2},{6,4},{1,7},{3,1},{5,3},{7,5},{8,14},{10,8},{12,... | collective-permute-start | bytes 2064392 | tf_op jit(solution)/shard_map/ppermute | solution.py:689
  185.6 11.5 %all_to_all.25 = bf16[16,64,128]{2,1,0:T(8,128)(2,1)S(1)} all-to-all(bf16[16,64,128]{2,1,0:T(8,128)(2,1)S(1)} %bitcast.40), channel_id=1, replica_groups=mesh['z'=4,'x'=4,'y'=4,'core'=2] {'z','x'}, dimensions={0} | all-to-all | bytes 524288 | tf_op jit(solution)/shard_map/all_to_all | solution.py:711
  197.1 3.4 %collective-permute-done.8.refs_1_ = bf16[2688,128]{1,0:T(8,128)(2,1)S(1)} collective-permute-done((bf16[2688,128]{1,0:T(8,128)(2,1)S(1)}, bf16[2688,128]{1,0:T(8,128)(2,1)S(1)}, u32[]{:S(2)}, u32[]{:S(2)}) %collective-permute-start.8) | collective-permute-done | bytes 688160 | tf_op jit(solution)/shard_map/ppermute | solution.py:689
  200.7 2.7 %collective-permute-start.14 = (bf16[1344,128]{1,0:T(8,128)(2,1)S(1)}, bf16[1344,128]{1,0:T(8,128)(2,1)}, u32[]{:S(2)}, u32[]{:S(2)}) collective-permute-start(bf16[1344,128]{1,0:T(8,128)(2,1)S(1)} %slice.23), channel_id=1, source_target_pairs={{0,6},{2,0},{4,2},{6,4},{1,7},{3,1},{5,3},{7,5},{8,14},{10,8},{12,... | collective-permute-start | bytes 1032200 | tf_op jit(solution)/shard_map/ppermute | solution.py:689
  203.4 2.4 collective-permute-start.11
  206.6 3.8 %collective-permute-done.10 = bf16[64,128]{1,0:T(8,128)(2,1)S(1)} collective-permute-done((bf16[64,128]{1,0:T(8,128)(2,1)S(1)}, bf16[64,128]{1,0:T(8,128)(2,1)S(1)}, u32[]{:S(2)}, u32[]{:S(2)}) %collective-permute-start.10) | collective-permute-done | bytes 16416 | tf_op jit(solution)/shard_map/ppermute | solution.py:689
  212.4 4.0 %all-to-all-start.4 = ((bf16[16,4,64,128]{3,2,1,0:T(8,128)(2,1)}), bf16[16,4,64,128]{3,2,1,0:T(8,128)(2,1)S(1)}, u32[]{:S(2)}, u32[]{:S(2)}) async-start(bf16[16,4,64,128]{3,2,1,0:T(8,128)(2,1)} %broadcast_in_dim.5), calls=%async_computation.4 | async-start | bytes 2097152 | tf_op jit(solution)/shard_map/all_to_all | solution.py:834
  216.5 3.1 %collective-permute-start.15 = (bf16[2688,128]{1,0:T(8,128)(2,1)S(1)}, bf16[2688,128]{1,0:T(8,128)(2,1)S(1)}, u32[]{:S(2)}, u32[]{:S(2)}) collective-permute-start(bf16[2688,128]{1,0:T(8,128)(2,1)S(1)} %bitcast.43), channel_id=1, source_target_pairs={{0,1},{1,0},{2,3},{3,2},{4,5},{5,4},{6,7},{7,6},{8,9},{9,8},{10,11... | collective-permute-start | bytes 2064392 | tf_op jit(solution)/shard_map/ppermute | solution.py:689
  221.4 4.4 %unpack_main.2 = (f32[576,1536]{1,0:T(8,128)}, f32[576,1536]{1,0:T(8,128)}, f32[576,1536]{1,0:T(8,128)}) custom-call(bf16[2688,128]{1,0:T(8,128)(2,1)} %bitcast.44, bf16[2688,128]{1,0:T(8,128)(2,1)} %copy-done.8, bf16[1344,128]{1,0:T(8,128)(2,1)} %copy-done.13, bf16[1344,128]{1,0:T(8,128)(2,1)} %collective-permute-done.14.refs_3_, bf16[2688,128]{1,0:T(8,128)(2,1)} %copy-done.9), custom_call_target="tpu_custom_call" | custom-call | flops 1500000000 | bytes 1000 | tf_op jit(solution)/shard_map/unpack_main/pallas_call | solution.py:670
  227.4 4.4 %unpack_main.3 = (f32[576,1536]{1,0:T(8,128)}, f32[576,1536]{1,0:T(8,128)}, f32[576,1536]{1,0:T(8,128)}) custom-call(bf16[2688,128]{1,0:T(8,128)(2,1)} %copy-done.3, bf16[2688,128]{1,0:T(8,128)(2,1)} %copy-done.4, bf16[1344,128]{1,0:T(8,128)(2,1)} %copy-done.6, ...), custom_call_target="tpu_custom_call", output_to_operand_aliasing={{0}: (5, {}), {1}: (6, {}), {2}: (7, {})} | custom-call | flops 1500000000 | bytes 1000 | tf_op jit(solution)/shard_map/unpack_main/pallas_call | solution.py:670
  231.9 3.1 %input_back.1 = (bf16[2,576,128]{2,1,0:T(8,128)(2,1)}, bf16[2,576,128]{2,1,0:T(8,128)(2,1)}) custom-call(bf16[256,384]{1,0:T(8,128)(2,1)} %reduce-scatter.2.cloned.1.call-done.kv_grad, bf16[192,576]{1,0:T(8,128)(2,1)} %bitcast.62, bf16[192,576]{1,0:T(8,128)(2,1)} %bitcast.65, f32[32,256]{1,0:T(8,128)} %get-tuple-element.78.cos_ref, ...), custom_call_target="tpu_custom_call" | custom-call | flops 1000000000 | bytes 1000 | tf_op jit(solution)/shard_map/input_back/pallas_call | solution.py:104
  235.2 2.5 %collective-permute-done.20.away = bf16[16,4,64,128]{3,2,1,0:T(8,128)(2,1)S(1)} collective-permute-done((bf16[16,4,64,128]{3,2,1,0:T(8,128)(2,1)S(1)}, bf16[16,4,64,128]{3,2,1,0:T(8,128)(2,1)S(1)}, u32[]{:S(2)}, u32[]{:S(2)}) %collective-permute-start.20) | collective-permute-done | bytes 1048608 | tf_op jit(solution)/shard_map/ppermute | solution.py:689
  238.7 4.6 %unpack_tail.1 = (f32[576,576]{1,0:T(8,128)}, f32[192,576]{1,0:T(8,128)}, f32[192,576]{1,0:T(8,128)}, f32[576,576]{1,0:T(8,128)}, f32[576]{0:T(1024)}, /*index=5*/f32[576]{0:T(1024)}) custom-call(bf16[16,4,64,128]{3,2,1,0:T(8,128)(2,1)} %copy-done.1, bf16[16,4,64,128]{3,2,1,0:T(8,128)(2,1)} %copy-done.12, bf16[576,576]{1,0:T(8,128)(2,1)} %wq.1, ...), custom_call_target="tpu_custom_call" | custom-call | flops 1000000000 | bytes 1000 | tf_op jit(solution)/shard_map/unpack_tail/pallas_call | solution.py:847
  (91 shorter events, 20.0 us)
Async XLA Ops:
  7.2 55.7 %all-gather.5.cloned.1.call-start = ((), (), s32[]{:S(2)}) async-start(), calls=%async_computation.7 | async-start | bytes 3342336 | tf_op jit(solution)/shard_map/all_gather | solution.py:776
  9.9 53.0 %copy-start.10 = (bf16[576]{0:T(1024)(128)(2,1)S(1)}, bf16[576]{0:T(1024)(128)(2,1)}, u32[]{:S(2)}) copy-start(bf16[576]{0:T(1024)(128)(2,1)} %param.24) | copy-start | bytes 3460
  10.0 119.6 %all-gather.7.cloned.1.call-start = ((), (), s32[]{:S(2)}) async-start(), calls=%async_computation.8 | async-start | bytes 6127616 | tf_op jit(solution)/shard_map/all_gather | solution.py:786
  10.0 13.6 %collective-permute-start = (bf16[2,576,128]{2,1,0:T(8,128)(2,1)S(1)}, bf16[2,576,128]{2,1,0:T(8,128)(2,1)S(1)}, u32[]{:S(2)}, u32[]{:S(2)}) collective-permute-start(bf16[2,576,128]{2,1,0:T(8,128)(2,1)S(1)} %bitcast.53), channel_id=1, source_target_pairs={{0,120},{8,112},{16,104},{24,96},{32,88},{40,80},{48,72},{56,64},{... | collective-permute-start | bytes 884744 | tf_op jit(solution)/shard_map/ppermute | solution.py:694
  16.9 13.2 %collective-permute-start.1 = (bf16[2,576,128]{2,1,0:T(8,128)(2,1)S(1)}, bf16[2,576,128]{2,1,0:T(8,128)(2,1)S(1)}, u32[]{:S(2)}, u32[]{:S(2)}) collective-permute-start(bf16[2,576,128]{2,1,0:T(8,128)(2,1)S(1)} %bitcast.54), channel_id=1, source_target_pairs={{0,120},{8,112},{16,104},{24,96},{32,88},{40,80},{48,72},{56,64},{... | collective-permute-start | bytes 884744 | tf_op jit(solution)/shard_map/ppermute | solution.py:694
  23.6 45.8 %copy-start.17 = (bf16[2,576,128]{2,1,0:T(8,128)(2,1)}, bf16[2,576,128]{2,1,0:T(8,128)(2,1)S(1)}, u32[]{:S(2)}) copy-start(bf16[2,576,128]{2,1,0:T(8,128)(2,1)S(1)} %collective-permute-done.q2_ref) | copy-start | bytes 884740
  30.1 39.3 %copy-start.18 = (bf16[2,576,128]{2,1,0:T(8,128)(2,1)}, bf16[2,576,128]{2,1,0:T(8,128)(2,1)S(1)}, u32[]{:S(2)}) copy-start(bf16[2,576,128]{2,1,0:T(8,128)(2,1)S(1)} %collective-permute-done.1.d2_ref) | copy-start | bytes 884740
  78.0 11.0 %collective-permute-start.2 = (bf16[10752,128]{1,0:T(8,128)(2,1)}, bf16[10752,128]{1,0:T(8,128)(2,1)S(1)}, u32[]{:S(2)}, u32[]{:S(2)}) collective-permute-start(bf16[10752,128]{1,0:T(8,128)(2,1)} %get-tuple-element.97), channel_id=1, source_target_pairs={{0,1},{1,0},{2,3},{3,2},{4,5},{5,4},{6,7},{7,6},{8,9},{9,8},{10,11... | collective-permute-start | bytes 8257544 | tf_op jit(solution)/shard_map/ppermute | solution.py:689
  92.3 37.2 %all-to-all-start = ((bf16[4,2688,128]{2,1,0:T(8,128)(2,1)}), bf16[4,2688,128]{2,1,0:T(8,128)(2,1)S(1)}, u32[]{:S(2)}, u32[]{:S(2)}) async-start(bf16[4,2688,128]{2,1,0:T(8,128)(2,1)} %bitcast.37), calls=%async_computation | async-start | bytes 5505024 | tf_op jit(solution)/shard_map/all_to_all | solution.py:711
  96.3 135.6 %reduce-scatter.2.cloned.1.call-start = ((), (), s32[]{:S(2)}) async-start(), calls=%async_computation.6 | async-start | bytes 3342336 | tf_op jit(solution)/shard_map/reduce_scatter | solution.py:812
  131.0 23.3 %all-to-all-start.1 = ((bf16[16,168,128]{2,1,0:T(8,128)(2,1)}), bf16[16,168,128]{2,1,0:T(8,128)(2,1)S(1)}, u32[]{:S(2)}, u32[]{:S(2)}) async-start(bf16[16,168,128]{2,1,0:T(8,128)(2,1)} %bitcast.12), calls=%async_computation.1 | async-start | bytes 1376256 | tf_op jit(solution)/shard_map/all_to_all | solution.py:711
  154.3 6.7 %collective-permute-start.3 = (bf16[4,1024,128]{2,1,0:T(8,128)(2,1)}, bf16[4,1024,128]{2,1,0:T(8,128)(2,1)S(1)}, u32[]{:S(2)}, u32[]{:S(2)}) collective-permute-start(bf16[4,1024,128]{2,1,0:T(8,128)(2,1)} %get-tuple-element.106), channel_id=1, source_target_pairs={{0,1},{1,0},{2,3},{3,2},{4,5},{5,4},{6,7},{7,6},{8,9},{9,8},{10,11... | collective-permute-start | bytes 3145736 | tf_op jit(solution)/shard_map/ppermute | solution.py:689
  157.2 25.7 %all-to-all-start.2 = ((bf16[16,168,128]{2,1,0:T(8,128)(2,1)}), bf16[16,168,128]{2,1,0:T(8,128)(2,1)S(1)}, u32[]{:S(2)}, u32[]{:S(2)}) async-start(bf16[16,168,128]{2,1,0:T(8,128)(2,1)} %broadcast_in_dim.4), calls=%async_computation.2 | async-start | bytes 1376256 | tf_op jit(solution)/shard_map/all_to_all | solution.py:726
  161.3 14.9 %collective-permute-start.4 = (bf16[1024,128]{1,0:T(8,128)(2,1)S(1)}, bf16[1024,128]{1,0:T(8,128)(2,1)S(1)}, u32[]{:S(2)}, u32[]{:S(2)}) collective-permute-start(bf16[1024,128]{1,0:T(8,128)(2,1)S(1)} %get-tuple-element.140), channel_id=1, source_target_pairs={{0,2},{2,4},{4,6},{6,0},{1,3},{3,5},{5,7},{7,1},{8,10},{10,12},{12... | collective-permute-start | bytes 786440 | tf_op jit(solution)/shard_map/ppermute | solution.py:689
  161.7 14.5 %collective-permute-start.5 = (bf16[1024,128]{1,0:T(8,128)(2,1)S(1)}, bf16[1024,128]{1,0:T(8,128)(2,1)S(1)}, u32[]{:S(2)}, u32[]{:S(2)}) collective-permute-start(bf16[1024,128]{1,0:T(8,128)(2,1)S(1)} %get-tuple-element.142), channel_id=1, source_target_pairs={{0,4},{2,6},{4,0},{6,2},{1,5},{3,7},{5,1},{7,3},{8,12},{10,14},{12... | collective-permute-start | bytes 786440 | tf_op jit(solution)/shard_map/ppermute | solution.py:689
  163.4 13.1 %collective-permute-start.6 = (bf16[1024,128]{1,0:T(8,128)(2,1)S(1)}, bf16[1024,128]{1,0:T(8,128)(2,1)S(1)}, u32[]{:S(2)}, u32[]{:S(2)}) collective-permute-start(bf16[1024,128]{1,0:T(8,128)(2,1)S(1)} %get-tuple-element.141), channel_id=1, source_target_pairs={{0,6},{2,0},{4,2},{6,4},{1,7},{3,1},{5,3},{7,5},{8,14},{10,8},{12,... | collective-permute-start | bytes 786440 | tf_op jit(solution)/shard_map/ppermute | solution.py:689
  164.2 18.7 %collective-permute-start.7 = (bf16[2,576,128]{2,1,0:T(8,128)(2,1)S(1)}, bf16[2,576,128]{2,1,0:T(8,128)(2,1)}, u32[]{:S(2)}, u32[]{:S(2)}) collective-permute-start(bf16[2,576,128]{2,1,0:T(8,128)(2,1)S(1)} %copy-done.16), channel_id=1, source_target_pairs={{0,120},{8,112},{16,104},{24,96},{32,88},{40,80},{48,72},{56,64},{... | collective-permute-start | bytes 884744 | tf_op jit(solution)/shard_map/ppermute | solution.py:694
  183.0 17.6 %collective-permute-start.8 = (bf16[2688,128]{1,0:T(8,128)(2,1)S(1)}, bf16[2688,128]{1,0:T(8,128)(2,1)S(1)}, u32[]{:S(2)}, u32[]{:S(2)}) collective-permute-start(bf16[2688,128]{1,0:T(8,128)(2,1)S(1)} %bitcast.41), channel_id=1, source_target_pairs={{0,2},{2,4},{4,6},{6,0},{1,3},{3,5},{5,7},{7,1},{8,10},{10,12},{12... | collective-permute-start | bytes 2064392 | tf_op jit(solution)/shard_map/ppermute | solution.py:689
  183.0 17.6 %collective-permute-start.9 = (bf16[2688,128]{1,0:T(8,128)(2,1)S(1)}, bf16[2688,128]{1,0:T(8,128)(2,1)S(1)}, u32[]{:S(2)}, u32[]{:S(2)}) collective-permute-start(bf16[2688,128]{1,0:T(8,128)(2,1)S(1)} %bitcast.42), channel_id=1, source_target_pairs={{0,6},{2,0},{4,2},{6,4},{1,7},{3,1},{5,3},{7,5},{8,14},{10,8},{12,... | collective-permute-start | bytes 2064392 | tf_op jit(solution)/shard_map/ppermute | solution.py:689
  185.6 35.0 %copy-start.11 = (bf16[576]{0:T(1024)(128)(2,1)S(1)}, bf16[576]{0:T(1024)(128)(2,1)}, u32[]{:S(2)}) copy-start(bf16[576]{0:T(1024)(128)(2,1)} %gain.1) | copy-start | bytes 3460
  200.6 10.6 %collective-permute-start.13 = (bf16[1344,128]{1,0:T(8,128)(2,1)S(1)}, bf16[1344,128]{1,0:T(8,128)(2,1)S(1)}, u32[]{:S(2)}, u32[]{:S(2)}) collective-permute-start(bf16[1344,128]{1,0:T(8,128)(2,1)S(1)} %slice.22), channel_id=1, source_target_pairs={{0,2},{2,4},{4,6},{6,0},{1,3},{3,5},{5,7},{7,1},{8,10},{10,12},{12... | collective-permute-start | bytes 1032200 | tf_op jit(solution)/shard_map/ppermute | solution.py:689
  200.7 10.5 %collective-permute-start.14 = (bf16[1344,128]{1,0:T(8,128)(2,1)S(1)}, bf16[1344,128]{1,0:T(8,128)(2,1)}, u32[]{:S(2)}, u32[]{:S(2)}) collective-permute-start(bf16[1344,128]{1,0:T(8,128)(2,1)S(1)} %slice.23), channel_id=1, source_target_pairs={{0,6},{2,0},{4,2},{6,4},{1,7},{3,1},{5,3},{7,5},{8,14},{10,8},{12,... | collective-permute-start | bytes 1032200 | tf_op jit(solution)/shard_map/ppermute | solution.py:689
  203.4 6.9 %collective-permute-start.10 = (bf16[64,128]{1,0:T(8,128)(2,1)S(1)}, bf16[64,128]{1,0:T(8,128)(2,1)S(1)}, u32[]{:S(2)}, u32[]{:S(2)}) collective-permute-start(bf16[64,128]{1,0:T(8,128)(2,1)S(1)} %reduce_sum.38), channel_id=1, source_target_pairs={{0,2},{2,4},{4,6},{6,0},{1,3},{3,5},{5,7},{7,1},{8,10},{10,12},{12... | collective-permute-start | bytes 49160 | tf_op jit(solution)/shard_map/ppermute | solution.py:689
  203.4 7.7 %collective-permute-start.11 = (bf16[64,128]{1,0:T(8,128)(2,1)S(1)}, bf16[64,128]{1,0:T(8,128)(2,1)S(1)}, u32[]{:S(2)}, u32[]{:S(2)}) collective-permute-start(bf16[64,128]{1,0:T(8,128)(2,1)S(1)} %reduce_sum.38), channel_id=1, source_target_pairs={{0,4},{2,6},{4,0},{6,2},{1,5},{3,7},{5,1},{7,3},{8,12},{10,14},{12... | collective-permute-start | bytes 49160 | tf_op jit(solution)/shard_map/ppermute | solution.py:689
  205.9 5.3 %collective-permute-start.12 = (bf16[64,128]{1,0:T(8,128)(2,1)S(1)}, bf16[64,128]{1,0:T(8,128)(2,1)S(1)}, u32[]{:S(2)}, u32[]{:S(2)}) collective-permute-start(bf16[64,128]{1,0:T(8,128)(2,1)S(1)} %reduce_sum.38), channel_id=1, source_target_pairs={{0,6},{2,0},{4,2},{6,4},{1,7},{3,1},{5,3},{7,5},{8,14},{10,8},{12,... | collective-permute-start | bytes 49160 | tf_op jit(solution)/shard_map/ppermute | solution.py:689
  212.4 22.6 %all-to-all-start.4 = ((bf16[16,4,64,128]{3,2,1,0:T(8,128)(2,1)}), bf16[16,4,64,128]{3,2,1,0:T(8,128)(2,1)S(1)}, u32[]{:S(2)}, u32[]{:S(2)}) async-start(bf16[16,4,64,128]{3,2,1,0:T(8,128)(2,1)} %broadcast_in_dim.5), calls=%async_computation.4 | async-start | bytes 2097152 | tf_op jit(solution)/shard_map/all_to_all | solution.py:834
  216.5 9.4 %collective-permute-start.15 = (bf16[2688,128]{1,0:T(8,128)(2,1)S(1)}, bf16[2688,128]{1,0:T(8,128)(2,1)S(1)}, u32[]{:S(2)}, u32[]{:S(2)}) collective-permute-start(bf16[2688,128]{1,0:T(8,128)(2,1)S(1)} %bitcast.43), channel_id=1, source_target_pairs={{0,1},{1,0},{2,3},{3,2},{4,5},{5,4},{6,7},{7,6},{8,9},{9,8},{10,11... | collective-permute-start | bytes 2064392 | tf_op jit(solution)/shard_map/ppermute | solution.py:689
  219.6 6.4 %collective-permute-start.16 = (bf16[2688,128]{1,0:T(8,128)(2,1)S(1)}, bf16[2688,128]{1,0:T(8,128)(2,1)S(1)}, u32[]{:S(2)}, u32[]{:S(2)}) collective-permute-start(bf16[2688,128]{1,0:T(8,128)(2,1)S(1)} %collective-permute-done.8.refs_1_), channel_id=1, source_target_pairs={{0,1},{1,0},{2,3},{3,2},{4,5},{5,4},{6,7},{7,6},{8,9},{9,8},{10,11... | collective-permute-start | bytes 2064392 | tf_op jit(solution)/shard_map/ppermute | solution.py:689
  219.7 6.3 %collective-permute-start.19 = (bf16[2688,128]{1,0:T(8,128)(2,1)S(1)}, bf16[2688,128]{1,0:T(8,128)(2,1)S(1)}, u32[]{:S(2)}, u32[]{:S(2)}) collective-permute-start(bf16[2688,128]{1,0:T(8,128)(2,1)S(1)} %collective-permute-done.9.refs_4_), channel_id=1, source_target_pairs={{0,1},{1,0},{2,3},{3,2},{4,5},{5,4},{6,7},{7,6},{8,9},{9,8},{10,11... | collective-permute-start | bytes 2064392 | tf_op jit(solution)/shard_map/ppermute | solution.py:689
  220.1 5.8 %collective-permute-start.17 = (bf16[1344,128]{1,0:T(8,128)(2,1)S(1)}, bf16[1344,128]{1,0:T(8,128)(2,1)S(1)}, u32[]{:S(2)}, u32[]{:S(2)}) collective-permute-start(bf16[1344,128]{1,0:T(8,128)(2,1)S(1)} %collective-permute-done.13.refs_2_), channel_id=1, source_target_pairs={{0,1},{1,0},{2,3},{3,2},{4,5},{5,4},{6,7},{7,6},{8,9},{9,8},{10,11... | collective-permute-start | bytes 1032200 | tf_op jit(solution)/shard_map/ppermute | solution.py:689
  220.2 5.7 %collective-permute-start.18 = (bf16[1344,128]{1,0:T(8,128)(2,1)}, bf16[1344,128]{1,0:T(8,128)(2,1)S(1)}, u32[]{:S(2)}, u32[]{:S(2)}) collective-permute-start(bf16[1344,128]{1,0:T(8,128)(2,1)} %collective-permute-done.14.refs_3_), channel_id=1, source_target_pairs={{0,1},{1,0},{2,3},{3,2},{4,5},{5,4},{6,7},{7,6},{8,9},{9,8},{10,11... | collective-permute-start | bytes 1032200 | tf_op jit(solution)/shard_map/ppermute | solution.py:689
  235.0 2.7 %collective-permute-start.20 = (bf16[16,4,64,128]{3,2,1,0:T(8,128)(2,1)S(1)}, bf16[16,4,64,128]{3,2,1,0:T(8,128)(2,1)S(1)}, u32[]{:S(2)}, u32[]{:S(2)}) collective-permute-start(bf16[16,4,64,128]{3,2,1,0:T(8,128)(2,1)S(1)} %all-to-all-done.4.kept), channel_id=1, source_target_pairs={{0,1},{1,0},{2,3},{3,2},{4,5},{5,4},{6,7},{7,6},{8,9},{9,8},{10,11... | collective-permute-start | bytes 3145736 | tf_op jit(solution)/shard_map/ppermute | solution.py:689
  (15 other events, 126.3 us)
Sparse Core Ops, SparseCore 0:
  10.7 52.0 all-gather.4
  65.6 58.1 all-gather.6
  129.7 90.1 reduce-scatter.1

commit v3 on v2

--- a/solution.py
+++ b/solution.py
@@ -173,10 +173,10 @@
     )
 
 
-def visible_bias(start, block, first_key, rows):
+def visible_bias(start, block, first_key, limit, rows):
     keys = first_key + lax.broadcasted_iota(jnp.int32, (KEYS, rows), 0)
     queries = block * rows + lax.broadcasted_iota(jnp.int32, (KEYS, rows), 1)
-    seen = (keys >= start) & (keys <= queries)
+    seen = (keys >= start) & (keys <= queries) & (keys < limit)
     bias = jnp.where(seen, 0.0, NEGATIVE)
     return jnp.concatenate([bias] * GROUP, axis=1)
 
@@ -186,18 +186,28 @@
     return jnp.min(start) // KEYS, block // per + 1
 
 
+def key_windows(start, block, rows):
+    per = KEYS // rows
+    return (block - jnp.min(start) // rows + per) // per
+
+
+def window(held, step, start, block, rows):
+    per = KEYS // rows
+    end = block + 1 - step * per
+    first = jnp.maximum(end - per, 0)
+    keys = held[pl.ds(first, per), 0].reshape(KEYS, held.shape[3])
+    return first, keys, visible_bias(start, block, first * rows, end * rows, rows)
+
+
 def run_forward(held, query, start, block_place, acc, peak, mass):
     rows = query.shape[1]
-    per = KEYS // rows
     acc[...] = jnp.zeros_like(acc)
     peak[...] = jnp.full_like(peak, NEGATIVE)
     mass[...] = jnp.zeros_like(mass)
-    first_step, last_step = key_steps(start, block_place, rows)
-
-    @pl.loop(first_step, last_step)
+
+    @pl.loop(0, key_windows(start, block_place, rows))
     def _(step):
-        block = held[pl.ds(step * per, per), 0].reshape(KEYS, held.shape[3])
-        bias = visible_bias(start, block_place, step * KEYS, rows)
+        _, block, bias = window(held, step, start, block_place, rows)
         tiles = [block[:, i * LANES : (i + 1) * LANES] for i in range(3)]
         for g in range(KVH):
             heads = lane_heads(query, g)
@@ -274,12 +284,10 @@
             both[g] = jnp.concatenate(
                 [jnp.concatenate([query, zero], axis=1), jnp.concatenate([zero, grad], axis=1)], axis=0
             )
-        first_step, last_step = key_steps(start, block_place, rows)
-
-        @pl.loop(first_step, last_step)
+
+        @pl.loop(0, key_windows(start, block_place, rows))
         def _(step):
-            block = held[pl.ds(step * per, per), 0].reshape(KEYS, held.shape[3])
-            bias = visible_bias(start, block_place, step * KEYS, rows)
+            first, block, bias = window(held, step, start, block_place, rows)
             tiles = [block[:, i * LANES : (i + 1) * LANES] for i in range(3)]
             total = []
             for g in range(KVH):
@@ -291,7 +299,7 @@
                 dq[a, g] += mul(jnp.transpose(tiles[g])[:HD], score_grad)
                 total.append(mul_nt(jnp.concatenate([score_grad, weights.astype(bf16)], axis=1), pair))
             joined = jnp.concatenate(total, axis=1)
-            sums[pl.ds(step * per, per)] += joined.reshape(per, rows, joined.shape[1])
+            sums[pl.ds(first, per)] += joined.reshape(per, rows, joined.shape[1])
 
     run_forward(held, query2, far_starts[0], far_block(), acc, peak, mass)
     attention(0, q1_ref.at[0], d1_ref.at[0], lambda g: lane_heads(o1.at[0], g), lse1.at[0], starts[0], own_block())

time: 251 us -> 250 us (level)
  transfers between devices with their start and end apart: 28 -> 28, of which waited for: 12 -> 13; matrix products, arithmetic and copies ran while one was open for 4% -> 4% of each run, Pallas kernels for 30% -> 30%
where the time goes in v3:
time: 250 us
  Pallas kernels  82.2 us (33%)
  waiting for transfers between devices  79 us (32%)
  starting transfers between devices  50.9 us (20%)
  between operations  14.1 us (6%)
  blocking collectives  11.9 us (5%)
  local copies, waits for them, and re-layouts  6.36 us (3%)
  other arithmetic  5.23 us (2%)
    all_gather x1, waiting for transfers between devices, per_device(): kv = lax.all_gather(kv, SEQ, axis=0)  32.8 us
    pallas_call x1, Pallas kernels, attend_backward(): pl.pallas_call(backward_kernel, grid=(micro,), in_specs=[one_of(kv.shape,...  27.1 us
    pallas_call x2, Pallas kernels, feed_forward(): pl.pallas_call(functools.partial(ffn_kernel, last), grid_spec=pltpu.Prefe...  18.7 us
    ppermute x18, starting transfers between devices, shift(): lax.ppermute(value, axis, [(i, (i + distance) % size) for i in range(size)])  18.3 us
    ppermute x18, waiting for transfers between devices, shift(): lax.ppermute(value, axis, [(i, (i + distance) % size) for i in range(size)])  17.7 us
    ppermute x3, waiting for transfers between devices, mirror(): return lax.ppermute(value, SEQ, [(i, size - 1 - i) for i in range(size)])  16.9 us
    all_to_all x2, starting transfers between devices, scatter_parts(): lax.all_to_all(held.reshape(places, rows // places, lanes), axis, 0, 0)  12.4 us
    all_to_all x1, blocking collectives, scatter_parts(): lax.all_to_all(held.reshape(places, rows // places, lanes), axis, 0, 0)  11.9 us
  transfers between devices with their start and end apart: 28, of which 13 were waited for; matrix products, arithmetic and copies ran while one was open for 4% of the time, Pallas kernels for 30%

profile of v3, /device:TPU:1, one launch (start us, length us, event | category | flops | bytes accessed | tf_op | source)
XLA Modules:
  0.0 249.7 jit_solution(9695988299290362092)
XLA Ops:
  7.2 2.7 %prepare.1 = (bf16[2,704,128]{2,1,0:T(8,128)(2,1)}, bf16[2,128,384]{2,1,0:T(8,128)(2,1)}, f32[32,256]{1,0:T(8,128)}, f32[32,256]{1,0:T(8,128)}, s32[2,1,128]{2,1,0:T(1,128)}, /*index=5*/s32[2,1,128]{2,1,0:T(1,128)}) custom-call(s32[2,16]{1,0:T(2,128)} %lengths.1, bf16[2,576,128]{2,1,0:T(8,128)(2,1)} %bitcast.57, bf16[576]{0:T(1024)(128)(2,1)} %gain.1, ...), custom_call_target="tpu_custom_call" | custom-call | flops 1000000000 | bytes 1000 | tf_op jit(solution)/shard_map/prepare/pallas_call | solution.py:104
  10.0 6.9 %collective-permute-start = (bf16[2,576,128]{2,1,0:T(8,128)(2,1)S(1)}, bf16[2,576,128]{2,1,0:T(8,128)(2,1)S(1)}, u32[]{:S(2)}, u32[]{:S(2)}) collective-permute-start(bf16[2,576,128]{2,1,0:T(8,128)(2,1)S(1)} %bitcast.53), channel_id=1, source_target_pairs={{0,120},{8,112},{16,104},{24,96},{32,88},{40,80},{48,72},{56,64},{... | collective-permute-start | bytes 884744 | tf_op jit(solution)/shard_map/ppermute | solution.py:702
  17.0 2.4 query.1.query_ref.q1_ref
  19.4 4.2 %collective-permute-done.q2_ref = bf16[2,576,128]{2,1,0:T(8,128)(2,1)S(1)} collective-permute-done((bf16[2,576,128]{2,1,0:T(8,128)(2,1)S(1)}, bf16[2,576,128]{2,1,0:T(8,128)(2,1)S(1)}, u32[]{:S(2)}, u32[]{:S(2)}) %collective-permute-start) | collective-permute-done | bytes 294944 | tf_op jit(solution)/shard_map/ppermute | solution.py:702
  23.6 6.4 %collective-permute-done.1.d2_ref = bf16[2,576,128]{2,1,0:T(8,128)(2,1)S(1)} collective-permute-done((bf16[2,576,128]{2,1,0:T(8,128)(2,1)S(1)}, bf16[2,576,128]{2,1,0:T(8,128)(2,1)S(1)}, u32[]{:S(2)}, u32[]{:S(2)}) %collective-permute-start.1) | collective-permute-done | bytes 294944 | tf_op jit(solution)/shard_map/ppermute | solution.py:702
  30.1 32.8 %all-gather.5.cloned.1.call-done = bf16[32,128,384]{2,1,0:T(8,128)(2,1)} async-done(((bf16[2,128,384]{2,1,0:T(8,128)(2,1)}), bf16[32,128,384]{2,1,0:T(8,128)(2,1)}) %all-gather.5.cloned.1.call-update) | async-done | bytes 3145744 | tf_op jit(solution)/shard_map/all_gather | solution.py:784
  63.7 5.7 %attention_forward.1 = (bf16[2,576,128]{2,1,0:T(8,128)(2,1)}, f32[2,576,128]{2,1,0:T(8,128)}, f32[2,3,1,384]{3,2,1,0:T(1,128)}) custom-call(bf16[16,2,128,384]{3,2,1,0:T(8,128)(2,1)} %bitcast.49, bf16[2,576,128]{2,1,0:T(8,128)(2,1)} %query.1.query_ref.q1_ref, s32[2,1,128]{2,1,0:T(1,128)} %get-tuple-element.82.starts), custom_call_target="tpu_custom_call" | custom-call | flops 2500000000 | bytes 1000 | tf_op jit(solution)/shard_map/attention_forward/pallas_call | solution.py:252
  69.4 8.6 %feed_forward.2 = (bf16[10752,128]{1,0:T(8,128)(2,1)}, f32[576,256]{1,0:T(8,128)}, f32[256,576]{1,0:T(8,128)}, f32[256,576]{1,0:T(8,128)}) custom-call(s32[1]{0:T(128)} %bitcast.core, bf16[2,576,128]{2,1,0:T(8,128)(2,1)} %get-tuple-element.83.first, bf16[2,576,128]{2,1,0:T(8,128)(2,1)} %bitcast.58, bf16[576,576]{1,0:T(8,128)(2,1)} %out_weight.3, ...), custom_call_target="tpu_custom_call" | custom-call | flops 3000000000 | bytes 1000 | tf_op jit(solution)/shard_map/feed_forward/pallas_call | solution.py:559
  79.1 10.0 %feed_forward.3 = (bf16[2,576,128]{2,1,0:T(8,128)(2,1)}, bf16[10752,128]{1,0:T(8,128)(2,1)}, f32[576,256]{1,0:T(8,128)}, bf16[2,576,128]{2,1,0:T(8,128)(2,1)}, f...) custom-call(s32[1]{0:T(128)} %bitcast.core, bf16[2,576,128]{2,1,0:T(8,128)(2,1)} %get-tuple-element.83.first, ...), custom_call_target="tpu_custom_call" | custom-call | flops 3000000000 | bytes 1000 | tf_op jit(solution)/shard_map/feed_forward/pallas_call | solution.py:559
  89.1 3.2 %add_convert_fusion = bf16[10752,128]{1,0:T(8,128)(2,1)} fusion(bf16[10752,128]{1,0:T(8,128)(2,1)S(1)} %collective-permute-done.2, bf16[10752,128]{1,0:T(8,128)(2,1)} %get-tuple-element.96), kind=kLoop, calls=%fused_computation | loop fusion | flops 5505024 | bytes 8257536 | tf_op jit(solution)/shard_map/convert_element_type | solution.py:799
  92.3 4.0 %all-to-all-start = ((bf16[4,2688,128]{2,1,0:T(8,128)(2,1)}), bf16[4,2688,128]{2,1,0:T(8,128)(2,1)S(1)}, u32[]{:S(2)}, u32[]{:S(2)}) async-start(bf16[4,2688,128]{2,1,0:T(8,128)(2,1)} %bitcast.37), calls=%async_computation | async-start | bytes 5505024 | tf_op jit(solution)/shard_map/all_to_all | solution.py:719
  96.3 27.1 %attention_backward.1 = (bf16[16,2,128,384]{3,2,1,0:T(8,128)(2,1)}, bf16[2,576,128]{2,1,0:T(8,128)(2,1)}, bf16[2,576,128]{2,1,0:T(8,128)(2,1)}) custom-call(bf16[16,2,128,384]{3,2,1,0:T(8,128)(2,1)} %bitcast.50, bf16[2,576,128]{2,1,0:T(8,128)(2,1)} %query.1.query_ref.q1_ref, bf16[2,576,128]{2,1,0:T(8,128)(2,1)} %copy-done.17, ...), custom_call_target="tpu_custom_call" | custom-call | flops 7000000000 | bytes 1000 | tf_op jit(solution)/shard_map/attention_backward/pallas_call | solution.py:325
  123.4 6.1 %all-to-all-done = bf16[4,2688,128]{2,1,0:T(8,128)(2,1)S(1)} async-done(((bf16[4,2688,128]{2,1,0:T(8,128)(2,1)}), bf16[4,2688,128]{2,1,0:T(8,128)(2,1)S(1)}, u32[]{:S(2)}, u32[]{:S(2)}) %all-to-all-start) | async-done | bytes 2752544 | tf_op jit(solution)/shard_map/all_to_all | solution.py:719
  131.0 8.4 %all-to-all-start.1 = ((bf16[16,168,128]{2,1,0:T(8,128)(2,1)}), bf16[16,168,128]{2,1,0:T(8,128)(2,1)S(1)}, u32[]{:S(2)}, u32[]{:S(2)}) async-start(bf16[16,168,128]{2,1,0:T(8,128)(2,1)} %bitcast.12), calls=%async_computation.1 | async-start | bytes 1376256 | tf_op jit(solution)/shard_map/all_to_all | solution.py:719
  139.4 9.2 %weights_back.1 = (f32[576,256]{1,0:T(8,128)}, bf16[4,1024,128]{2,1,0:T(8,128)(2,1)}, bf16[4,1024,128]{2,1,0:T(8,128)(2,1)}) custom-call(bf16[16,2,128,384]{3,2,1,0:T(8,128)(2,1)} %get-tuple-element.98.sums, bf16[16,2,704,128]{3,2,1,0:T(8,128)(2,1)} %bitcast.38, s32[2,1,128]{2,1,0:T(1,128)} %get-tuple-element.82.starts, ...), custom_call_target="tpu_custom_call" | custom-call | flops 3000000000 | bytes 1000 | tf_op jit(solution)/shard_map/weights_back/pallas_call | solution.py:408
  148.6 5.5 %all-to-all-done.1 = bf16[16,168,128]{2,1,0:T(8,128)(2,1)S(1)} async-done(((bf16[16,168,128]{2,1,0:T(8,128)(2,1)}), bf16[16,168,128]{2,1,0:T(8,128)(2,1)S(1)}, u32[]{:S(2)}, u32[]{:S(2)}) %all-to-all-start.1) | async-done | bytes 688160 | tf_op jit(solution)/shard_map/all_to_all | solution.py:719
  156.8 3.7 %all-to-all-start.2 = ((bf16[16,168,128]{2,1,0:T(8,128)(2,1)}), bf16[16,168,128]{2,1,0:T(8,128)(2,1)S(1)}, u32[]{:S(2)}, u32[]{:S(2)}) async-start(bf16[16,168,128]{2,1,0:T(8,128)(2,1)} %broadcast_in_dim.4), calls=%async_computation.2 | async-start | bytes 1376256 | tf_op jit(solution)/shard_map/all_to_all | solution.py:734
  163.7 4.7 %collective-permute-start.7 = (bf16[2,576,128]{2,1,0:T(8,128)(2,1)S(1)}, bf16[2,576,128]{2,1,0:T(8,128)(2,1)}, u32[]{:S(2)}, u32[]{:S(2)}) collective-permute-start(bf16[2,576,128]{2,1,0:T(8,128)(2,1)S(1)} %copy-done.16), channel_id=1, source_target_pairs={{0,120},{8,112},{16,104},{24,96},{32,88},{40,80},{48,72},{56,64},{... | collective-permute-start | bytes 884744 | tf_op jit(solution)/shard_map/ppermute | solution.py:702
  170.6 4.8 %collective-permute-done.5 = bf16[1024,128]{1,0:T(8,128)(2,1)S(1)} collective-permute-done((bf16[1024,128]{1,0:T(8,128)(2,1)S(1)}, bf16[1024,128]{1,0:T(8,128)(2,1)S(1)}, u32[]{:S(2)}, u32[]{:S(2)}) %collective-permute-start.5) | collective-permute-done | bytes 262176 | tf_op jit(solution)/shard_map/ppermute | solution.py:697
  176.2 6.2 %collective-permute-done.7.second = bf16[2,576,128]{2,1,0:T(8,128)(2,1)} collective-permute-done((bf16[2,576,128]{2,1,0:T(8,128)(2,1)S(1)}, bf16[2,576,128]{2,1,0:T(8,128)(2,1)}, u32[]{:S(2)}, u32[]{:S(2)}) %collective-permute-start.7) | collective-permute-done | bytes 294944 | tf_op jit(solution)/shard_map/ppermute | solution.py:702
  182.5 2.6 %collective-permute-start.9 = (bf16[2688,128]{1,0:T(8,128)(2,1)S(1)}, bf16[2688,128]{1,0:T(8,128)(2,1)S(1)}, u32[]{:S(2)}, u32[]{:S(2)}) collective-permute-start(bf16[2688,128]{1,0:T(8,128)(2,1)S(1)} %bitcast.42), channel_id=1, source_target_pairs={{0,6},{2,0},{4,2},{6,4},{1,7},{3,1},{5,3},{7,5},{8,14},{10,8},{12,... | collective-permute-start | bytes 2064392 | tf_op jit(solution)/shard_map/ppermute | solution.py:697
  185.1 11.9 %all_to_all.25 = bf16[16,64,128]{2,1,0:T(8,128)(2,1)S(1)} all-to-all(bf16[16,64,128]{2,1,0:T(8,128)(2,1)S(1)} %bitcast.40), channel_id=1, replica_groups=mesh['z'=4,'x'=4,'y'=4,'core'=2] {'z','x'}, dimensions={0} | all-to-all | bytes 524288 | tf_op jit(solution)/shard_map/all_to_all | solution.py:719
  197.0 2.9 %collective-permute-done.8.refs_1_ = bf16[2688,128]{1,0:T(8,128)(2,1)S(1)} collective-permute-done((bf16[2688,128]{1,0:T(8,128)(2,1)S(1)}, bf16[2688,128]{1,0:T(8,128)(2,1)S(1)}, u32[]{:S(2)}, u32[]{:S(2)}) %collective-permute-start.8) | collective-permute-done | bytes 688160 | tf_op jit(solution)/shard_map/ppermute | solution.py:697
  200.1 2.7 %collective-permute-start.14 = (bf16[1344,128]{1,0:T(8,128)(2,1)S(1)}, bf16[1344,128]{1,0:T(8,128)(2,1)}, u32[]{:S(2)}, u32[]{:S(2)}) collective-permute-start(bf16[1344,128]{1,0:T(8,128)(2,1)S(1)} %slice.23), channel_id=1, source_target_pairs={{0,6},{2,0},{4,2},{6,4},{1,7},{3,1},{5,3},{7,5},{8,14},{10,8},{12,... | collective-permute-start | bytes 1032200 | tf_op jit(solution)/shard_map/ppermute | solution.py:697
  205.9 3.8 %collective-permute-done.10 = bf16[64,128]{1,0:T(8,128)(2,1)S(1)} collective-permute-done((bf16[64,128]{1,0:T(8,128)(2,1)S(1)}, bf16[64,128]{1,0:T(8,128)(2,1)S(1)}, u32[]{:S(2)}, u32[]{:S(2)}) %collective-permute-start.10) | collective-permute-done | bytes 16416 | tf_op jit(solution)/shard_map/ppermute | solution.py:697
  211.5 4.8 %all-to-all-start.4 = ((bf16[16,4,64,128]{3,2,1,0:T(8,128)(2,1)}), bf16[16,4,64,128]{3,2,1,0:T(8,128)(2,1)S(1)}, u32[]{:S(2)}, u32[]{:S(2)}) async-start(bf16[16,4,64,128]{3,2,1,0:T(8,128)(2,1)} %broadcast_in_dim.5), calls=%async_computation.4 | async-start | bytes 2097152 | tf_op jit(solution)/shard_map/all_to_all | solution.py:842
  216.4 3.1 %collective-permute-start.15 = (bf16[2688,128]{1,0:T(8,128)(2,1)S(1)}, bf16[2688,128]{1,0:T(8,128)(2,1)S(1)}, u32[]{:S(2)}, u32[]{:S(2)}) collective-permute-start(bf16[2688,128]{1,0:T(8,128)(2,1)S(1)} %bitcast.43), channel_id=1, source_target_pairs={{0,1},{1,0},{2,3},{3,2},{4,5},{5,4},{6,7},{7,6},{8,9},{9,8},{10,11... | collective-permute-start | bytes 2064392 | tf_op jit(solution)/shard_map/ppermute | solution.py:697
  221.3 4.4 %unpack_main.2 = (f32[576,1536]{1,0:T(8,128)}, f32[576,1536]{1,0:T(8,128)}, f32[576,1536]{1,0:T(8,128)}) custom-call(bf16[2688,128]{1,0:T(8,128)(2,1)} %bitcast.44, bf16[2688,128]{1,0:T(8,128)(2,1)} %copy-done.8, bf16[1344,128]{1,0:T(8,128)(2,1)} %copy-done.13, bf16[1344,128]{1,0:T(8,128)(2,1)} %collective-permute-done.14.refs_3_, bf16[2688,128]{1,0:T(8,128)(2,1)} %copy-done.9), custom_call_target="tpu_custom_call" | custom-call | flops 1500000000 | bytes 1000 | tf_op jit(solution)/shard_map/unpack_main/pallas_call | solution.py:678
  227.3 4.4 %unpack_main.3 = (f32[576,1536]{1,0:T(8,128)}, f32[576,1536]{1,0:T(8,128)}, f32[576,1536]{1,0:T(8,128)}) custom-call(bf16[2688,128]{1,0:T(8,128)(2,1)} %copy-done.3, bf16[2688,128]{1,0:T(8,128)(2,1)} %copy-done.4, bf16[1344,128]{1,0:T(8,128)(2,1)} %copy-done.6, ...), custom_call_target="tpu_custom_call", output_to_operand_aliasing={{0}: (5, {}), {1}: (6, {}), {2}: (7, {})} | custom-call | flops 1500000000 | bytes 1000 | tf_op jit(solution)/shard_map/unpack_main/pallas_call | solution.py:678
  231.8 3.1 %input_back.1 = (bf16[2,576,128]{2,1,0:T(8,128)(2,1)}, bf16[2,576,128]{2,1,0:T(8,128)(2,1)}) custom-call(bf16[256,384]{1,0:T(8,128)(2,1)} %reduce-scatter.2.cloned.1.call-done.kv_grad, bf16[192,576]{1,0:T(8,128)(2,1)} %bitcast.62, bf16[192,576]{1,0:T(8,128)(2,1)} %bitcast.65, f32[32,256]{1,0:T(8,128)} %get-tuple-element.78.cos_ref, ...), custom_call_target="tpu_custom_call" | custom-call | flops 1000000000 | bytes 1000 | tf_op jit(solution)/shard_map/input_back/pallas_call | solution.py:104
  235.1 2.6 %collective-permute-done.20.away = bf16[16,4,64,128]{3,2,1,0:T(8,128)(2,1)S(1)} collective-permute-done((bf16[16,4,64,128]{3,2,1,0:T(8,128)(2,1)S(1)}, bf16[16,4,64,128]{3,2,1,0:T(8,128)(2,1)S(1)}, u32[]{:S(2)}, u32[]{:S(2)}) %collective-permute-start.20) | collective-permute-done | bytes 1048608 | tf_op jit(solution)/shard_map/ppermute | solution.py:697
  238.6 4.6 %unpack_tail.1 = (f32[576,576]{1,0:T(8,128)}, f32[192,576]{1,0:T(8,128)}, f32[192,576]{1,0:T(8,128)}, f32[576,576]{1,0:T(8,128)}, f32[576]{0:T(1024)}, /*index=5*/f32[576]{0:T(1024)}) custom-call(bf16[16,4,64,128]{3,2,1,0:T(8,128)(2,1)} %copy-done.1, bf16[16,4,64,128]{3,2,1,0:T(8,128)(2,1)} %copy-done.12, bf16[576,576]{1,0:T(8,128)(2,1)} %wq.1, ...), custom_call_target="tpu_custom_call" | custom-call | flops 1000000000 | bytes 1000 | tf_op jit(solution)/shard_map/unpack_tail/pallas_call | solution.py:855
  (91 shorter events, 22.1 us)
Async XLA Ops:
  7.2 55.7 %all-gather.5.cloned.1.call-start = ((), (), s32[]{:S(2)}) async-start(), calls=%async_computation.7 | async-start | bytes 3342336 | tf_op jit(solution)/shard_map/all_gather | solution.py:784
  9.9 53.0 %copy-start.10 = (bf16[576]{0:T(1024)(128)(2,1)S(1)}, bf16[576]{0:T(1024)(128)(2,1)}, u32[]{:S(2)}) copy-start(bf16[576]{0:T(1024)(128)(2,1)} %param.24) | copy-start | bytes 3460
  10.0 119.6 %all-gather.7.cloned.1.call-start = ((), (), s32[]{:S(2)}) async-start(), calls=%async_computation.8 | async-start | bytes 6127616 | tf_op jit(solution)/shard_map/all_gather | solution.py:794
  10.0 13.6 %collective-permute-start = (bf16[2,576,128]{2,1,0:T(8,128)(2,1)S(1)}, bf16[2,576,128]{2,1,0:T(8,128)(2,1)S(1)}, u32[]{:S(2)}, u32[]{:S(2)}) collective-permute-start(bf16[2,576,128]{2,1,0:T(8,128)(2,1)S(1)} %bitcast.53), channel_id=1, source_target_pairs={{0,120},{8,112},{16,104},{24,96},{32,88},{40,80},{48,72},{56,64},{... | collective-permute-start | bytes 884744 | tf_op jit(solution)/shard_map/ppermute | solution.py:702
  16.9 13.2 %collective-permute-start.1 = (bf16[2,576,128]{2,1,0:T(8,128)(2,1)S(1)}, bf16[2,576,128]{2,1,0:T(8,128)(2,1)S(1)}, u32[]{:S(2)}, u32[]{:S(2)}) collective-permute-start(bf16[2,576,128]{2,1,0:T(8,128)(2,1)S(1)} %bitcast.54), channel_id=1, source_target_pairs={{0,120},{8,112},{16,104},{24,96},{32,88},{40,80},{48,72},{56,64},{... | collective-permute-start | bytes 884744 | tf_op jit(solution)/shard_map/ppermute | solution.py:702
  23.6 45.8 %copy-start.17 = (bf16[2,576,128]{2,1,0:T(8,128)(2,1)}, bf16[2,576,128]{2,1,0:T(8,128)(2,1)S(1)}, u32[]{:S(2)}) copy-start(bf16[2,576,128]{2,1,0:T(8,128)(2,1)S(1)} %collective-permute-done.q2_ref) | copy-start | bytes 884740
  30.1 39.4 %copy-start.18 = (bf16[2,576,128]{2,1,0:T(8,128)(2,1)}, bf16[2,576,128]{2,1,0:T(8,128)(2,1)S(1)}, u32[]{:S(2)}) copy-start(bf16[2,576,128]{2,1,0:T(8,128)(2,1)S(1)} %collective-permute-done.1.d2_ref) | copy-start | bytes 884740
  78.1 11.0 %collective-permute-start.2 = (bf16[10752,128]{1,0:T(8,128)(2,1)}, bf16[10752,128]{1,0:T(8,128)(2,1)S(1)}, u32[]{:S(2)}, u32[]{:S(2)}) collective-permute-start(bf16[10752,128]{1,0:T(8,128)(2,1)} %get-tuple-element.97), channel_id=1, source_target_pairs={{0,1},{1,0},{2,3},{3,2},{4,5},{5,4},{6,7},{7,6},{8,9},{9,8},{10,11... | collective-permute-start | bytes 8257544 | tf_op jit(solution)/shard_map/ppermute | solution.py:697
  92.3 37.2 %all-to-all-start = ((bf16[4,2688,128]{2,1,0:T(8,128)(2,1)}), bf16[4,2688,128]{2,1,0:T(8,128)(2,1)S(1)}, u32[]{:S(2)}, u32[]{:S(2)}) async-start(bf16[4,2688,128]{2,1,0:T(8,128)(2,1)} %bitcast.37), calls=%async_computation | async-start | bytes 5505024 | tf_op jit(solution)/shard_map/all_to_all | solution.py:719
  96.3 135.4 %reduce-scatter.2.cloned.1.call-start = ((), (), s32[]{:S(2)}) async-start(), calls=%async_computation.6 | async-start | bytes 3342336 | tf_op jit(solution)/shard_map/reduce_scatter | solution.py:820
  131.0 23.1 %all-to-all-start.1 = ((bf16[16,168,128]{2,1,0:T(8,128)(2,1)}), bf16[16,168,128]{2,1,0:T(8,128)(2,1)S(1)}, u32[]{:S(2)}, u32[]{:S(2)}) async-start(bf16[16,168,128]{2,1,0:T(8,128)(2,1)} %bitcast.12), calls=%async_computation.1 | async-start | bytes 1376256 | tf_op jit(solution)/shard_map/all_to_all | solution.py:719
  154.0 6.5 %collective-permute-start.3 = (bf16[4,1024,128]{2,1,0:T(8,128)(2,1)}, bf16[4,1024,128]{2,1,0:T(8,128)(2,1)S(1)}, u32[]{:S(2)}, u32[]{:S(2)}) collective-permute-start(bf16[4,1024,128]{2,1,0:T(8,128)(2,1)} %get-tuple-element.106), channel_id=1, source_target_pairs={{0,1},{1,0},{2,3},{3,2},{4,5},{5,4},{6,7},{7,6},{8,9},{9,8},{10,11... | collective-permute-start | bytes 3145736 | tf_op jit(solution)/shard_map/ppermute | solution.py:697
  156.8 25.7 %all-to-all-start.2 = ((bf16[16,168,128]{2,1,0:T(8,128)(2,1)}), bf16[16,168,128]{2,1,0:T(8,128)(2,1)S(1)}, u32[]{:S(2)}, u32[]{:S(2)}) async-start(bf16[16,168,128]{2,1,0:T(8,128)(2,1)} %broadcast_in_dim.4), calls=%async_computation.2 | async-start | bytes 1376256 | tf_op jit(solution)/shard_map/all_to_all | solution.py:734
  160.9 9.7 %collective-permute-start.4 = (bf16[1024,128]{1,0:T(8,128)(2,1)S(1)}, bf16[1024,128]{1,0:T(8,128)(2,1)S(1)}, u32[]{:S(2)}, u32[]{:S(2)}) collective-permute-start(bf16[1024,128]{1,0:T(8,128)(2,1)S(1)} %get-tuple-element.140), channel_id=1, source_target_pairs={{0,2},{2,4},{4,6},{6,0},{1,3},{3,5},{5,7},{7,1},{8,10},{10,12},{12... | collective-permute-start | bytes 786440 | tf_op jit(solution)/shard_map/ppermute | solution.py:697
  161.2 14.2 %collective-permute-start.5 = (bf16[1024,128]{1,0:T(8,128)(2,1)S(1)}, bf16[1024,128]{1,0:T(8,128)(2,1)S(1)}, u32[]{:S(2)}, u32[]{:S(2)}) collective-permute-start(bf16[1024,128]{1,0:T(8,128)(2,1)S(1)} %get-tuple-element.142), channel_id=1, source_target_pairs={{0,4},{2,6},{4,0},{6,2},{1,5},{3,7},{5,1},{7,3},{8,12},{10,14},{12... | collective-permute-start | bytes 786440 | tf_op jit(solution)/shard_map/ppermute | solution.py:697
  163.1 13.0 %collective-permute-start.6 = (bf16[1024,128]{1,0:T(8,128)(2,1)S(1)}, bf16[1024,128]{1,0:T(8,128)(2,1)S(1)}, u32[]{:S(2)}, u32[]{:S(2)}) collective-permute-start(bf16[1024,128]{1,0:T(8,128)(2,1)S(1)} %get-tuple-element.141), channel_id=1, source_target_pairs={{0,6},{2,0},{4,2},{6,4},{1,7},{3,1},{5,3},{7,5},{8,14},{10,8},{12,... | collective-permute-start | bytes 786440 | tf_op jit(solution)/shard_map/ppermute | solution.py:697
  163.7 18.8 %collective-permute-start.7 = (bf16[2,576,128]{2,1,0:T(8,128)(2,1)S(1)}, bf16[2,576,128]{2,1,0:T(8,128)(2,1)}, u32[]{:S(2)}, u32[]{:S(2)}) collective-permute-start(bf16[2,576,128]{2,1,0:T(8,128)(2,1)S(1)} %copy-done.16), channel_id=1, source_target_pairs={{0,120},{8,112},{16,104},{24,96},{32,88},{40,80},{48,72},{56,64},{... | collective-permute-start | bytes 884744 | tf_op jit(solution)/shard_map/ppermute | solution.py:702
  182.4 17.5 %collective-permute-start.8 = (bf16[2688,128]{1,0:T(8,128)(2,1)S(1)}, bf16[2688,128]{1,0:T(8,128)(2,1)S(1)}, u32[]{:S(2)}, u32[]{:S(2)}) collective-permute-start(bf16[2688,128]{1,0:T(8,128)(2,1)S(1)} %bitcast.41), channel_id=1, source_target_pairs={{0,2},{2,4},{4,6},{6,0},{1,3},{3,5},{5,7},{7,1},{8,10},{10,12},{12... | collective-permute-start | bytes 2064392 | tf_op jit(solution)/shard_map/ppermute | solution.py:697
  182.5 17.5 %collective-permute-start.9 = (bf16[2688,128]{1,0:T(8,128)(2,1)S(1)}, bf16[2688,128]{1,0:T(8,128)(2,1)S(1)}, u32[]{:S(2)}, u32[]{:S(2)}) collective-permute-start(bf16[2688,128]{1,0:T(8,128)(2,1)S(1)} %bitcast.42), channel_id=1, source_target_pairs={{0,6},{2,0},{4,2},{6,4},{1,7},{3,1},{5,3},{7,5},{8,14},{10,8},{12,... | collective-permute-start | bytes 2064392 | tf_op jit(solution)/shard_map/ppermute | solution.py:697
  185.1 35.4 %copy-start.11 = (bf16[576]{0:T(1024)(128)(2,1)S(1)}, bf16[576]{0:T(1024)(128)(2,1)}, u32[]{:S(2)}) copy-start(bf16[576]{0:T(1024)(128)(2,1)} %gain.1) | copy-start | bytes 3460
  200.0 10.3 %collective-permute-start.13 = (bf16[1344,128]{1,0:T(8,128)(2,1)S(1)}, bf16[1344,128]{1,0:T(8,128)(2,1)S(1)}, u32[]{:S(2)}, u32[]{:S(2)}) collective-permute-start(bf16[1344,128]{1,0:T(8,128)(2,1)S(1)} %slice.22), channel_id=1, source_target_pairs={{0,2},{2,4},{4,6},{6,0},{1,3},{3,5},{5,7},{7,1},{8,10},{10,12},{12... | collective-permute-start | bytes 1032200 | tf_op jit(solution)/shard_map/ppermute | solution.py:697
  200.1 10.2 %collective-permute-start.14 = (bf16[1344,128]{1,0:T(8,128)(2,1)S(1)}, bf16[1344,128]{1,0:T(8,128)(2,1)}, u32[]{:S(2)}, u32[]{:S(2)}) collective-permute-start(bf16[1344,128]{1,0:T(8,128)(2,1)S(1)} %slice.23), channel_id=1, source_target_pairs={{0,6},{2,0},{4,2},{6,4},{1,7},{3,1},{5,3},{7,5},{8,14},{10,8},{12,... | collective-permute-start | bytes 1032200 | tf_op jit(solution)/shard_map/ppermute | solution.py:697
  202.8 6.8 %collective-permute-start.10 = (bf16[64,128]{1,0:T(8,128)(2,1)S(1)}, bf16[64,128]{1,0:T(8,128)(2,1)S(1)}, u32[]{:S(2)}, u32[]{:S(2)}) collective-permute-start(bf16[64,128]{1,0:T(8,128)(2,1)S(1)} %reduce_sum.38), channel_id=1, source_target_pairs={{0,2},{2,4},{4,6},{6,0},{1,3},{3,5},{5,7},{7,1},{8,10},{10,12},{12... | collective-permute-start | bytes 49160 | tf_op jit(solution)/shard_map/ppermute | solution.py:697
  202.9 7.4 %collective-permute-start.11 = (bf16[64,128]{1,0:T(8,128)(2,1)S(1)}, bf16[64,128]{1,0:T(8,128)(2,1)S(1)}, u32[]{:S(2)}, u32[]{:S(2)}) collective-permute-start(bf16[64,128]{1,0:T(8,128)(2,1)S(1)} %reduce_sum.38), channel_id=1, source_target_pairs={{0,4},{2,6},{4,0},{6,2},{1,5},{3,7},{5,1},{7,3},{8,12},{10,14},{12... | collective-permute-start | bytes 49160 | tf_op jit(solution)/shard_map/ppermute | solution.py:697
  205.2 5.1 %collective-permute-start.12 = (bf16[64,128]{1,0:T(8,128)(2,1)S(1)}, bf16[64,128]{1,0:T(8,128)(2,1)S(1)}, u32[]{:S(2)}, u32[]{:S(2)}) collective-permute-start(bf16[64,128]{1,0:T(8,128)(2,1)S(1)} %reduce_sum.38), channel_id=1, source_target_pairs={{0,6},{2,0},{4,2},{6,4},{1,7},{3,1},{5,3},{7,5},{8,14},{10,8},{12,... | collective-permute-start | bytes 49160 | tf_op jit(solution)/shard_map/ppermute | solution.py:697
  211.5 23.3 %all-to-all-start.4 = ((bf16[16,4,64,128]{3,2,1,0:T(8,128)(2,1)}), bf16[16,4,64,128]{3,2,1,0:T(8,128)(2,1)S(1)}, u32[]{:S(2)}, u32[]{:S(2)}) async-start(bf16[16,4,64,128]{3,2,1,0:T(8,128)(2,1)} %broadcast_in_dim.5), calls=%async_computation.4 | async-start | bytes 2097152 | tf_op jit(solution)/shard_map/all_to_all | solution.py:842
  216.4 9.4 %collective-permute-start.15 = (bf16[2688,128]{1,0:T(8,128)(2,1)S(1)}, bf16[2688,128]{1,0:T(8,128)(2,1)S(1)}, u32[]{:S(2)}, u32[]{:S(2)}) collective-permute-start(bf16[2688,128]{1,0:T(8,128)(2,1)S(1)} %bitcast.43), channel_id=1, source_target_pairs={{0,1},{1,0},{2,3},{3,2},{4,5},{5,4},{6,7},{7,6},{8,9},{9,8},{10,11... | collective-permute-start | bytes 2064392 | tf_op jit(solution)/shard_map/ppermute | solution.py:697
  219.5 6.4 %collective-permute-start.16 = (bf16[2688,128]{1,0:T(8,128)(2,1)S(1)}, bf16[2688,128]{1,0:T(8,128)(2,1)S(1)}, u32[]{:S(2)}, u32[]{:S(2)}) collective-permute-start(bf16[2688,128]{1,0:T(8,128)(2,1)S(1)} %collective-permute-done.8.refs_1_), channel_id=1, source_target_pairs={{0,1},{1,0},{2,3},{3,2},{4,5},{5,4},{6,7},{7,6},{8,9},{9,8},{10,11... | collective-permute-start | bytes 2064392 | tf_op jit(solution)/shard_map/ppermute | solution.py:697
  219.6 6.3 %collective-permute-start.19 = (bf16[2688,128]{1,0:T(8,128)(2,1)S(1)}, bf16[2688,128]{1,0:T(8,128)(2,1)S(1)}, u32[]{:S(2)}, u32[]{:S(2)}) collective-permute-start(bf16[2688,128]{1,0:T(8,128)(2,1)S(1)} %collective-permute-done.9.refs_4_), channel_id=1, source_target_pairs={{0,1},{1,0},{2,3},{3,2},{4,5},{5,4},{6,7},{7,6},{8,9},{9,8},{10,11... | collective-permute-start | bytes 2064392 | tf_op jit(solution)/shard_map/ppermute | solution.py:697
  220.0 5.8 %collective-permute-start.17 = (bf16[1344,128]{1,0:T(8,128)(2,1)S(1)}, bf16[1344,128]{1,0:T(8,128)(2,1)S(1)}, u32[]{:S(2)}, u32[]{:S(2)}) collective-permute-start(bf16[1344,128]{1,0:T(8,128)(2,1)S(1)} %collective-permute-done.13.refs_2_), channel_id=1, source_target_pairs={{0,1},{1,0},{2,3},{3,2},{4,5},{5,4},{6,7},{7,6},{8,9},{9,8},{10,11... | collective-permute-start | bytes 1032200 | tf_op jit(solution)/shard_map/ppermute | solution.py:697
  220.1 5.7 %collective-permute-start.18 = (bf16[1344,128]{1,0:T(8,128)(2,1)}, bf16[1344,128]{1,0:T(8,128)(2,1)S(1)}, u32[]{:S(2)}, u32[]{:S(2)}) collective-permute-start(bf16[1344,128]{1,0:T(8,128)(2,1)} %collective-permute-done.14.refs_3_), channel_id=1, source_target_pairs={{0,1},{1,0},{2,3},{3,2},{4,5},{5,4},{6,7},{7,6},{8,9},{9,8},{10,11... | collective-permute-start | bytes 1032200 | tf_op jit(solution)/shard_map/ppermute | solution.py:697
  234.9 2.7 %collective-permute-start.20 = (bf16[16,4,64,128]{3,2,1,0:T(8,128)(2,1)S(1)}, bf16[16,4,64,128]{3,2,1,0:T(8,128)(2,1)S(1)}, u32[]{:S(2)}, u32[]{:S(2)}) collective-permute-start(bf16[16,4,64,128]{3,2,1,0:T(8,128)(2,1)S(1)} %all-to-all-done.4.kept), channel_id=1, source_target_pairs={{0,1},{1,0},{2,3},{3,2},{4,5},{5,4},{6,7},{7,6},{8,9},{9,8},{10,11... | collective-permute-start | bytes 3145736 | tf_op jit(solution)/shard_map/ppermute | solution.py:697
  (15 other events, 128.3 us)
Sparse Core Ops, SparseCore 0:
  10.7 52.0 all-gather.4
  65.6 58.1 all-gather.6
  129.7 89.0 reduce-scatter.1
